TPU v7x, 128 devices: a whole 4x4x4 slice. The times are simulated.
128 devices in a mesh: slab: 16 (over y, x), view: 8 (over z, core).
Axes of the slice: x: 4, y: 4, z: 4, core: 2. Of those that a mesh axis runs over, the one named last changes fastest.
Arguments:
- object_field: float32 [2, 128, 1024, 1024], P(None, 'view', 'slab'), may hold values from -0.8 to 0.8
- probe: float32 [2, 256, 256], replicated, may hold values from -6 to 6
- amplitude: float32 [4096, 256, 256], P(('slab', 'view')), may hold values from 0.1 to 3
- offsets: int32 [4096, 2], P(('slab', 'view')), may hold values from 0 to 1023, as said below
Outputs:
- object_new: float32 [2, 128, 1024, 1024], P(None, 'view', 'slab')
- probe_step: float32 [2, 256, 256], replicated
Inputs may be any that keep to these rules, and one draw needn't show every extreme that they name: `offsets`: A position handled by the device at slab index s has its row offset in s * 64 to (s + 1) * 64 - 1 and its column offset in 0 to 768; on every device the first position lies at the slab's first row and column 0 and the second at the slab's last row and column 768.
All inputs are finite; a program needn't handle non-finite values.
Results may differ from a plain program's by a relative error of at most 0.0029.
Values may be sent and summed in bfloat16 or wider, within the bound.
No kernel may reach another device: no remote copies, remote signals or barrier semaphores. Data moves between devices by JAX's collectives and lax.ppermute only.
A program may use at most 128 MiB of HBM per device.

v0:
```python
import math

import jax
import jax.numpy as jnp
from jax import lax
from jax.sharding import PartitionSpec as P


def passed_along(value, axis, steps):
    count = lax.axis_size(axis)
    first, last = (max(0, -steps), min(count, count - steps))
    return lax.ppermute(value, axis, [(source, source + steps) for source in range(first, last)])


def dft_tables(order):
    index = jnp.arange(order, dtype=jnp.int32)
    product = index[:, None] * index[None, :] % order
    angle = product.astype(jnp.float32) * (-2.0 * math.pi / order)
    factor = 1.0 / math.sqrt(order)
    return (jnp.cos(angle) * factor, jnp.sin(angle) * factor)


def real_dot(left, right):
    return jnp.dot(left, right, precision=lax.Precision.HIGHEST, preferred_element_type=jnp.float32)


def complex_dot(left_re, left_im, right_re, right_im):
    out_re = real_dot(left_re, right_re) - real_dot(left_im, right_im)
    out_im = real_dot(left_re, right_im) + real_dot(left_im, right_re)
    return (out_re, out_im)


def exit_update(patch, probe, amplitude, cosines, sines):
    patch_re, patch_im = (patch[0], patch[1])
    probe_re, probe_im = (probe[0], probe[1])
    exit_re = probe_re * patch_re - probe_im * patch_im
    exit_im = probe_re * patch_im + probe_im * patch_re
    half_re, half_im = complex_dot(cosines, sines, exit_re, exit_im)
    far_re, far_im = complex_dot(half_re, half_im, cosines, sines)
    factor = amplitude / jnp.sqrt(far_re * far_re + far_im * far_im + 0.25)
    fixed_re, fixed_im = (far_re * factor, far_im * factor)
    back_re, back_im = complex_dot(cosines, -sines, fixed_re, fixed_im)
    new_re, new_im = complex_dot(back_re, back_im, cosines, -sines)
    diff_re, diff_im = (new_re - exit_re, new_im - exit_im)
    object_term = jnp.stack(
        [probe_re * diff_re + probe_im * diff_im, probe_re * diff_im - probe_im * diff_re]
    )
    probe_term = jnp.stack(
        [patch_re * diff_re + patch_im * diff_im, patch_re * diff_im - patch_im * diff_re]
    )
    weight = patch_re * patch_re + patch_im * patch_im
    return (object_term, probe_term, weight)


def extend(field, reach_count):
    blocks = [field]
    for step in range(1, reach_count + 1):
        blocks.append(passed_along(field, "slab", -step))
    return jnp.concatenate(blocks, axis=1)


def retract(buffer, slab_rows, reach_count):
    blocks = [
        buffer[:, block * slab_rows : (block + 1) * slab_rows] for block in range(reach_count + 1)
    ]
    total = blocks[0]
    for step in range(1, reach_count + 1):
        total = total + passed_along(blocks[step], "slab", step)
    return total


def on_device(object_field, probe, amplitude, offsets):
    depth_dev = object_field.shape[1]
    slab_rows = object_field.shape[2]
    columns = object_field.shape[3]
    frame_size = probe.shape[1]
    reach_count = frame_size // slab_rows
    pad_width = depth_dev * lax.axis_size("view")
    layer_ids = lax.axis_index("view") * depth_dev + jnp.arange(depth_dev, dtype=jnp.int32)
    padded = jnp.pad(object_field, ((0, 0), (0, 0), (0, 0), (pad_width, 0)))

    def shift_in(layer, layer_id):
        return lax.dynamic_slice_in_dim(layer, pad_width - layer_id, columns, 2)

    partial_value = jnp.sum(jax.vmap(shift_in, in_axes=(1, 0))(padded, layer_ids), axis=0)
    projected = lax.psum(partial_value, "view").astype(jnp.bfloat16)
    band = extend(projected, reach_count)
    cosines, sines = dft_tables(frame_size)
    zero_index = jnp.zeros((), jnp.int32)
    band_start = lax.axis_index("slab") * slab_rows

    def visit(carry, item):
        update, numer, denom = carry
        corner, measured = item
        starts = (zero_index, corner[0] - band_start, corner[1])
        patch = lax.dynamic_slice(band, starts, (2, frame_size, frame_size)).astype(jnp.float32)
        object_term, probe_term, weight = exit_update(patch, probe, measured, cosines, sines)
        current = lax.dynamic_slice(update, starts, (2, frame_size, frame_size))
        update = lax.dynamic_update_slice(update, current + object_term, starts)
        return ((update, numer + probe_term, denom + weight), None)

    start = (
        jnp.zeros(band.shape, jnp.float32),
        jnp.zeros((2, frame_size, frame_size), jnp.float32),
        jnp.zeros((frame_size, frame_size), jnp.float32),
    )
    (update, numer, denom), _ = lax.scan(visit, start, (offsets, amplitude))
    summed = lax.psum(retract(update, slab_rows, reach_count), "view")
    padded_back = jnp.pad(summed, ((0, 0), (0, 0), (0, pad_width)))

    def shift_out(layer_id):
        return lax.dynamic_slice_in_dim(padded_back, layer_id, columns, 2)

    back = jax.vmap(shift_out, out_axes=1)(layer_ids)
    peak = jnp.max(probe[0] * probe[0] + probe[1] * probe[1]) + 1e-06
    object_new = object_field + 0.5 * back / peak
    totals = lax.psum((numer, denom), ("slab", "view"))
    probe_step = totals[0] / totals[1][None]
    return (object_new, probe_step)


def solution(mesh):
    return jax.shard_map(
        on_device,
        mesh=mesh,
        in_specs=(
            P(None, "view", "slab", None),
            P(),
            P(("slab", "view"), None, None),
            P(("slab", "view"), None),
        ),
        out_specs=(P(None, "view", "slab", None), P()),
        check_vma=False,
    )
```

profile of v0, /device:TPU:1, one launch (start us, length us, event | category | flops | bytes accessed | tf_op | source)
XLA Modules:
  0.0 1618.9 jit_solution(2415765146345300016)
XLA Ops:
  7.2 8.1 pad_bitcast_fusion
  15.4 62.0 %while.19 = (s32[]{:T(128)}, f32[16,2,64,1152]{3,2,1,0:T(8,128)}, s32[16,4]{0,1:T(4,128)S(1)}, f32[16,2,64,1024]{3,2,1,0:T(8,128)}, s32[]{:T(128)}) while((s32[]{:T(128)}, f32[16,2,64,1152]{3,2,1,0:T(8,128)}, s32[16,4]{0,1:T(4,128)S(1)}, f32[16,2,64,1024]{3,2,1,0:T(8,128)}, s32[]{:T(128)}) %tuple.80), condition=%wide.while_cond, body=%wide.while_body.sunk | while | flops 2 | bytes 1050225 | solution.py:83
  16.0 3.2 dynamic-slice_dynamic-update-slice_fusion.2
  19.9 3.2 dynamic-slice_dynamic-update-slice_fusion.2
  23.8 3.2 dynamic-slice_dynamic-update-slice_fusion.2
  27.7 3.2 dynamic-slice_dynamic-update-slice_fusion.2
  31.5 3.2 dynamic-slice_dynamic-update-slice_fusion.2
  35.4 3.2 dynamic-slice_dynamic-update-slice_fusion.2
  39.3 3.2 dynamic-slice_dynamic-update-slice_fusion.2
  43.2 3.2 dynamic-slice_dynamic-update-slice_fusion.2
  47.0 3.2 dynamic-slice_dynamic-update-slice_fusion.2
  50.9 3.2 dynamic-slice_dynamic-update-slice_fusion.2
  54.8 3.2 dynamic-slice_dynamic-update-slice_fusion.2
  58.7 3.2 dynamic-slice_dynamic-update-slice_fusion.2
  62.5 3.2 dynamic-slice_dynamic-update-slice_fusion.2
  66.4 3.2 dynamic-slice_dynamic-update-slice_fusion.2
  70.3 3.2 dynamic-slice_dynamic-update-slice_fusion.2
  74.2 3.2 dynamic-slice_dynamic-update-slice_fusion.2
  77.4 4.3 reduce_sum.9
  81.7 30.2 %all-reduce.12 = bf16[2,64,1024]{2,1,0:T(8,128)(2,1)S(1)} all-reduce(f32[2,64,1024]{2,1,0:T(8,128)S(1)} %reduce_sum.9), channel_id=1, replica_groups=mesh['slab'=16,'view'=8] {'view'}, use_global_device_ids=true, to_apply=%region_1.2 | all-reduce | flops 131072 | bytes 786432 | tf_op jit(solution)/shard_map/psum | solution.py:86
  123.3 6.1 collective-permute-done.2
  132.6 1179.1 %while.21 = (s32[]{:T(128)}, f32[2,320,1024]{2,1,0:T(8,128)}, f32[2,256,256]{2,1,0:T(8,128)S(1)}, f32[256,256]{1,0:T(8,128)S(1)}, s32[32,2]{0,1:T(2,128)S(1)}, /...) while((s32[]{:T(128)}, f32[2,320,1024]{2,1,0:T(8,128)}, ...), condition=%wide.region_3.4_spmd.clone.clone, body=%wide.region_2.3_spmd.clone.clone.sunk | while | flops 3240624128 | bytes 20971796 | solution.py:107
  163.4 5.6 dynamic_update_slice.7
  199.7 4.4 dynamic_update_slice.7
  234.9 6.1 dynamic_update_slice.7
  271.8 6.1 dynamic_update_slice.7
  308.7 6.1 dynamic_update_slice.7
  345.5 5.9 dynamic_update_slice.7
  382.3 6.1 dynamic_update_slice.7
  419.2 6.2 dynamic_update_slice.7
  456.1 6.0 dynamic_update_slice.7
  492.9 6.1 dynamic_update_slice.7
  529.8 6.4 dynamic_update_slice.7
  567.0 6.1 dynamic_update_slice.7
  603.9 6.1 dynamic_update_slice.7
  640.8 6.2 dynamic_update_slice.7
  677.8 6.2 dynamic_update_slice.7
  714.8 6.1 dynamic_update_slice.7
  751.7 5.9 dynamic_update_slice.7
  788.4 6.2 dynamic_update_slice.7
  825.3 6.2 dynamic_update_slice.7
  862.4 6.3 dynamic_update_slice.7
  899.4 6.2 dynamic_update_slice.7
  936.4 6.2 dynamic_update_slice.7
  973.4 5.9 dynamic_update_slice.7
  1010.1 6.2 dynamic_update_slice.7
  1047.1 6.1 dynamic_update_slice.7
  1084.0 6.4 dynamic_update_slice.7
  1121.1 6.0 dynamic_update_slice.7
  1157.9 6.2 dynamic_update_slice.7
  1194.9 6.1 dynamic_update_slice.7
  1231.8 6.2 dynamic_update_slice.7
  1268.9 5.9 dynamic_update_slice.7
  1305.6 6.2 dynamic_update_slice.7
  1311.8 3.2 fusion.116
  1315.0 6.2 collective-permute-start.4
  1321.1 12.2 collective-permute-start.5
  1335.6 3.3 collective-permute-start.7
  1342.7 13.3 collective-permute-done.6
  1356.0 20.3 %collective-permute-done.7 = f32[2,64,1024]{2,1,0:T(8,128)S(1)} collective-permute-done((f32[2,64,1024]{2,1,0:T(8,128)}, f32[2,64,1024]{2,1,0:T(8,128)S(1)}, u32[]{:S(2)}, u32[]{:S(2)}) %collective-permute-start.7) | collective-permute-done | bytes 524320 | tf_op jit(solution)/shard_map/ppermute | solution.py:12
  1379.0 123.7 %all-reduce.11.cloned.1.call-done = (f32[2,256,256]{2,1,0:T(8,128)}, f32[256,256]{1,0:T(8,128)}) async-done(((f32[2,256,256]{2,1,0:T(8,128)}, f32[256,256]{1,0:T(8,128)}), (f32[2,256,256]{2,1,0:T(8,128)}, f32[256,256]{1,0:T(8,128)})) %all-reduce.11.cloned.1.call-update) | async-done | bytes 786448 | tf_op jit(solution)/shard_map/psum | solution.py:117
  1504.7 57.7 %all-reduce.9.cloned.1.call-done = f32[2,64,1024]{2,1,0:T(8,128)} async-done(((f32[2,64,1024]{2,1,0:T(8,128)}), f32[2,64,1024]{2,1,0:T(8,128)}) %all-reduce.9.cloned.1.call-update) | async-done | bytes 524304 | tf_op jit(solution)/shard_map/psum | solution.py:108
  1563.5 36.3 %while.20 = (s32[]{:T(128)}, f32[2,64,1152]{2,1,0:T(8,128)S(1)}, s32[16,3]{0,1:T(4,128)S(1)}, f32[16,2,64,1024]{3,2,0,1:T(8,128)}, s32[]{:T(128)}) while((s32[]{:T(128)}, f32[2,64,1152]{2,1,0:T(8,128)S(1)}, s32[16,3]{0,1:T(4,128)S(1)}, f32[16,2,64,1024]{3,2,0,1:T(8,128)}, s32[]{:T(128)}) %tuple.86), condition=%wide.while_cond.1, body=%wide.while_body.1.sunk | while | flops 2 | bytes 1049697 | solution.py:112
  1599.8 12.2 bitcast_add_fusion
  (793 shorter events, 971.1 us)
Async XLA Ops:
  7.2 1495.6 %all-reduce.11.cloned.1.call-start = ((), (), s32[]{:S(2)}) async-start(), calls=%async_computation.1 | async-start | bytes 1572864 | tf_op jit(solution)/shard_map/psum | solution.py:117
  77.4 55.2 %copy-start = (f32[2,256,256]{2,1,0:T(8,128)S(1)}, f32[2,256,256]{2,1,0:T(8,128)}, u32[]{:S(2)}) copy-start(f32[2,256,256]{2,1,0:T(8,128)} %param.7) | copy-start | bytes 1572868
  77.4 55.2 %copy-start.3 = (s32[32,2]{0,1:T(2,128)S(1)}, s32[32,2]{0,1:T(2,128)}, u32[]{:S(2)}) copy-start(s32[32,2]{0,1:T(2,128)} %param.9) | copy-start | bytes 772
  111.9 7.1 collective-permute-start
  113.2 9.3 collective-permute-start.1
  114.5 14.8 collective-permute-start.2
  115.8 14.3 collective-permute-start.3
  1311.8 27.2 %copy-start.1 = (f32[2,256,256]{2,1,0:T(8,128)}, f32[2,256,256]{2,1,0:T(8,128)S(1)}, u32[]{:S(2)}) copy-start(f32[2,256,256]{2,1,0:T(8,128)S(1)} %get-tuple-element.150) | copy-start | bytes 1572868
  1311.8 27.2 %copy-start.2 = (f32[256,256]{1,0:T(8,128)}, f32[256,256]{1,0:T(8,128)S(1)}, u32[]{:S(2)}) copy-start(f32[256,256]{1,0:T(8,128)S(1)} %get-tuple-element.151) | copy-start | bytes 786436
  1315.0 24.7 %collective-permute-start.4 = (f32[2,64,1024]{2,1,0:T(8,128)}, f32[2,64,1024]{2,1,0:T(8,128)S(1)}, u32[]{:S(2)}, u32[]{:S(2)}) collective-permute-start(f32[2,64,1024]{2,1,0:T(8,128)} %get-tuple-element.301), channel_id=1, source_target_pairs={{0,8},{8,16},{16,24},{24,32},{32,40},{40,48},{48,56},{56,64},{64,7... | collective-permute-start | bytes 1572872 | tf_op jit(solution)/shard_map/ppermute | solution.py:12
  1321.1 21.6 %collective-permute-start.5 = (f32[2,64,1024]{2,1,0:T(8,128)}, f32[2,64,1024]{2,1,0:T(8,128)S(1)}, u32[]{:S(2)}, u32[]{:S(2)}) collective-permute-start(f32[2,64,1024]{2,1,0:T(8,128)} %get-tuple-element.304), channel_id=1, source_target_pairs={{0,16},{8,24},{16,32},{24,40},{32,48},{40,56},{48,64},{56,72},{64,... | collective-permute-start | bytes 1572872 | tf_op jit(solution)/shard_map/ppermute | solution.py:12
  1333.4 22.6 %collective-permute-start.6 = (f32[2,64,1024]{2,1,0:T(8,128)}, f32[2,64,1024]{2,1,0:T(8,128)S(1)}, u32[]{:S(2)}, u32[]{:S(2)}) collective-permute-start(f32[2,64,1024]{2,1,0:T(8,128)} %get-tuple-element.303), channel_id=1, source_target_pairs={{0,24},{8,32},{16,40},{24,48},{32,56},{40,64},{48,72},{56,80},{64,... | collective-permute-start | bytes 1572872 | tf_op jit(solution)/shard_map/ppermute | solution.py:12
  1335.6 40.7 %collective-permute-start.7 = (f32[2,64,1024]{2,1,0:T(8,128)}, f32[2,64,1024]{2,1,0:T(8,128)S(1)}, u32[]{:S(2)}, u32[]{:S(2)}) collective-permute-start(f32[2,64,1024]{2,1,0:T(8,128)} %get-tuple-element.302), channel_id=1, source_target_pairs={{0,32},{8,40},{16,48},{24,56},{32,64},{40,72},{48,80},{56,88},{64,... | collective-permute-start | bytes 1572872 | tf_op jit(solution)/shard_map/ppermute | solution.py:12
  1339.0 223.4 %all-reduce.9.cloned.1.call-start = ((), (), s32[]{:S(2)}) async-start(), calls=%async_computation | async-start | bytes 1048576 | tf_op jit(solution)/shard_map/psum | solution.py:108
Sparse Core Ops, SparseCore 0:
  1339.1 163.5 all-reduce.10
  1505.1 57.2 all-reduce.8
where the time goes:
time: 1630 us; the launch traced here: 1620 us
  matrix products  789 us (48%)
  local copies, waits for them, and re-layouts  331 us (20%)
  waiting for transfers between devices  228 us (14%)
  other arithmetic  109 us (7%)
  loops' own time  86.6 us (5%)
  blocking collectives  30.2 us (2%)
  starting transfers between devices  29.2 us (2%)
    dot_general x512, matrix products, real_dot(): jnp.dot(left, right, precision=lax.Precision.HIGHEST, preferred_element_t...  789 us
    dynamic_update_slice x32, local copies, waits for them, and re-layouts, visit(): update = lax.dynamic_update_slice(update, current + object_term, starts)  194 us
    psum x1, waiting for transfers between devices, on_device(): totals = lax.psum((numer, denom), ('slab', 'view'))  124 us
    gather x96, local copies, waits for them, and re-layouts  98.3 us
    another operation x1, loops' own time, on_device(): (update, numer, denom), _ = lax.scan(visit, start, (offsets, amplitude))  86.5 us
    psum x1, waiting for transfers between devices, on_device(): summed = lax.psum(retract(update, slab_rows, reach_count), 'view')  57.7 us
    add x32, other arithmetic, visit(): update = lax.dynamic_update_slice(update, current + object_term, starts)  47.6 us
    ppermute x8, waiting for transfers between devices, passed_along(): lax.ppermute(value, axis, [(source, source + steps) for source in range(f...  46.7 us
  transfers between devices with their start and end apart: 10, of which 8 were waited for; matrix products, arithmetic and copies ran while one was open for 0% of the time, Pallas kernels for 0%

commit v1 on v0

v1 whole, which is shorter than its diff:
```python
import functools
import math

import jax
import jax.numpy as jnp
import ml_dtypes
import numpy as np
from jax import lax
from jax.experimental import pallas as pl
from jax.experimental.pallas import tpu as pltpu
from jax.sharding import PartitionSpec as P

F32 = jnp.float32
BF16 = jnp.bfloat16
FRAME = 256
LANES = 128
SLAB = 64
VIEWS = 8
ROWS = SLAB // VIEWS
COLUMNS = 1024
TILES = COLUMNS // LANES
BLOCKS = 5
BAND = BLOCKS * SLAB
PER_STEP = 4
VMEM = pl.BlockSpec(memory_space=pltpu.VMEM)
SMEM = pl.BlockSpec(memory_space=pltpu.SMEM)


def dft_blocks(order):
    index = np.arange(order, dtype=np.int32)
    product = index[:, None] * index[None, :] % order
    angle = product.astype(np.float32) * np.float32(-2.0 * math.pi / order)
    factor = np.float32(1.0 / math.sqrt(order))
    c, s = np.cos(angle) * factor, np.sin(angle) * factor
    fore = np.block([[c, -s], [s, c]]).astype(ml_dtypes.bfloat16)
    back = np.block([[c, s], [-s, c]]).astype(ml_dtypes.bfloat16)
    return fore, back


def shifted(value, steps, left):
    lane = lax.broadcasted_iota(jnp.int32, value.shape, 1)
    if left:
        return jnp.where(lane < COLUMNS - steps, pltpu.roll(value, (COLUMNS - steps) % COLUMNS, 1), 0.0)
    return jnp.where(lane >= steps, pltpu.roll(value, steps, 1), 0.0)


def project_kernel(first_ref, field_ref, out_ref):
    layers = field_ref.shape[1]

    def layer(k):
        return jnp.concatenate([field_ref[0, k], field_ref[1, k]], 0)

    total = layer(layers - 1)
    for k in reversed(range(layers - 1)):
        total = shifted(total, 1, False) + layer(k)
    out_ref[0] = shifted(total, first_ref[0], False)


def project(first, field):
    layers = field.shape[1]
    return pl.pallas_call(
        project_kernel,
        grid=(VIEWS,),
        in_specs=[SMEM, pl.BlockSpec((2, layers, ROWS, COLUMNS), lambda i: (0, 0, i, 0))],
        out_specs=pl.BlockSpec((1, 2 * ROWS, COLUMNS), lambda i: (i, 0, 0)),
        out_shape=jax.ShapeDtypeStruct((VIEWS, 2 * ROWS, COLUMNS), F32),
        compiler_params=pltpu.CompilerParams(vmem_limit_bytes=32 << 20),
    )(first, field)


def spread_kernel(first_ref, update_ref, field_ref, out_ref):
    layers = field_ref.shape[1]
    update = shifted(update_ref[0].astype(F32), first_ref[0], True)
    for k in range(layers):
        for part in range(2):
            out_ref[part, k] = field_ref[part, k] + update[part * ROWS : (part + 1) * ROWS]
        if k < layers - 1:
            update = shifted(update, 1, True)


def spread(first, update, field):
    layers = field.shape[1]
    block = pl.BlockSpec((2, layers, ROWS, COLUMNS), lambda i: (0, 0, i, 0))
    return pl.pallas_call(
        spread_kernel,
        grid=(VIEWS,),
        in_specs=[SMEM, pl.BlockSpec((1, 2 * ROWS, COLUMNS), lambda i: (i, 0, 0)), block],
        out_specs=block,
        out_shape=jax.ShapeDtypeStruct(field.shape, F32),
        compiler_params=pltpu.CompilerParams(vmem_limit_bytes=32 << 20),
    )(first, update, field)


def dot(left, right):
    return jnp.dot(left, right, preferred_element_type=F32)


def visit_kernel(off_ref, b0, b1, b2, b3, b4, probe_ref, fore_ref, back_ref, amp_ref, out_ref, band, upd, num):
    step = pl.program_id(0)

    @pl.when(step == 0)
    def _():
        for b, ref in enumerate((b0, b1, b2, b3, b4)):
            for v in range(VIEWS):
                x = ref[v].astype(F32)
                first = b * SLAB + v * ROWS
                for part in range(2):
                    for t in range(TILES):
                        band[part, t, first : first + ROWS, :] = x[part * ROWS : (part + 1) * ROWS, t * LANES : (t + 1) * LANES]
        upd[...] = jnp.zeros_like(upd)
        num[...] = jnp.zeros_like(num)

    lane = lax.broadcasted_iota(jnp.int32, (FRAME, LANES), 1)

    def corner(j):
        p = step * PER_STEP + j
        r, c = off_ref[p, 0], off_ref[p, 1]
        q, m = c // LANES, c % LANES
        return r, (q, q + 1, jnp.minimum(q + 2, TILES - 1)), m

    def patch_of(part, r, q, m):
        turn = (LANES - m) % LANES
        tiles = [pltpu.roll(band[part, t, pl.ds(r, FRAME), :], turn, 1) for t in q]
        keep = lane < LANES - m
        return jnp.concatenate([jnp.where(keep, tiles[0], tiles[1]), jnp.where(keep, tiles[1], tiles[2])], 1)

    def add_to(part, value, r, q, m):
        left = pltpu.roll(value[:, :LANES], m, 1)
        right = pltpu.roll(value[:, LANES:], m, 1)
        keep = lane >= m
        terms = [jnp.where(keep, left, 0.0), jnp.where(keep, right, left), jnp.where(keep, 0.0, right)]
        for t, x in zip(q, terms):
            upd[part, t, pl.ds(r, FRAME), :] += x

    pr, pi = probe_ref[0], probe_ref[1]
    corners = [corner(j) for j in range(PER_STEP)]
    stage = []
    for r, q, m in corners:
        a, b = patch_of(0, r, q, m), patch_of(1, r, q, m)
        stage.append((a, b, pr * a - pi * b, pr * b + pi * a))
    half = [dot(fore_ref[...], jnp.concatenate([er, ei], 0).astype(BF16)) for _, _, er, ei in stage]
    half = [jnp.concatenate([h[:FRAME], h[FRAME:]], 1).astype(BF16) for h in half]
    far = [dot(h, back_ref[...]) for h in half]
    fixed = []
    for j, f in enumerate(far):
        fr, fi = f[:, :FRAME], f[:, FRAME:]
        factor = amp_ref[j] * lax.rsqrt(fr * fr + fi * fi + 0.25)
        fixed.append(jnp.concatenate([fr * factor, fi * factor], 1).astype(BF16))
    back = [dot(g, fore_ref[...]) for g in fixed]
    back = [jnp.concatenate([h[:, :FRAME], h[:, FRAME:]], 0).astype(BF16) for h in back]
    new = [dot(back_ref[...], h) for h in back]
    for (r, q, m), (a, b, er, ei), n in zip(corners, stage, new):
        dr, di = n[:FRAME] - er, n[FRAME:] - ei
        add_to(0, pr * dr + pi * di, r, q, m)
        add_to(1, pr * di - pi * dr, r, q, m)
        num[0] += a * dr + b * di
        num[1] += a * di - b * dr
        num[2] += a * a + b * b

    @pl.when(step == pl.num_programs(0) - 1)
    def _():
        peak = jnp.max(pr * pr + pi * pi) + 1e-06
        scale = 0.5 / jnp.full((2 * ROWS, COLUMNS), peak, F32)
        for v in range(VIEWS):
            for b in range(BLOCKS):
                rows = slice(b * SLAB + v * ROWS, b * SLAB + (v + 1) * ROWS)
                x = [jnp.concatenate([upd[part, t, rows, :] for t in range(TILES)], 1) for part in range(2)]
                out_ref[v, b * 2 * ROWS : (b + 1) * 2 * ROWS, :] = (jnp.concatenate(x, 0) * scale).astype(BF16)
            first = v * (FRAME // VIEWS)
            planes = [
                jnp.concatenate([num[k, first + g * ROWS : first + (g + 1) * ROWS, :] for g in range(4)], 1) for k in range(3)
            ]
            out_ref[v, 80:112, :] = jnp.concatenate(planes + [jnp.zeros_like(planes[0])], 0).astype(BF16)


def visit_all(corners, bands, probe, amplitude):
    count = amplitude.shape[0]
    fore, back = dft_blocks(FRAME)
    amp_spec = pl.BlockSpec((PER_STEP, FRAME, FRAME), lambda i: (i, 0, 0))
    return pl.pallas_call(
        visit_kernel,
        grid=(count // PER_STEP,),
        in_specs=[SMEM] + [VMEM] * 8 + [amp_spec],
        out_specs=VMEM,
        out_shape=jax.ShapeDtypeStruct((VIEWS, 112, COLUMNS), BF16),
        scratch_shapes=[
            pltpu.VMEM((2, TILES, BAND, LANES), F32),
            pltpu.VMEM((2, TILES, BAND, LANES), F32),
            pltpu.VMEM((3, FRAME, FRAME), F32),
        ],
        compiler_params=pltpu.CompilerParams(vmem_limit_bytes=48 << 20),
    )(corners, *bands, probe, fore, back, amplitude)


def passed_along(value, steps):
    count = lax.axis_size("slab")
    first, last = (max(0, -steps), min(count, count - steps))
    return lax.ppermute(value, "slab", [(source, source + steps) for source in range(first, last)])


def on_device(object_field, probe, amplitude, offsets):
    layers = object_field.shape[1]
    first = (lax.axis_index("view") * layers).astype(jnp.int32).reshape(1)
    corners = offsets - jnp.stack([lax.axis_index("slab") * SLAB, 0]).astype(jnp.int32)
    partial = project(first, object_field)
    got = lax.all_to_all(partial, "view", 0, 0, tiled=True)
    piece = jnp.sum(got, axis=0).astype(BF16)
    band = lax.all_gather(piece, "view", axis=0)
    bands = [band] + [passed_along(band, -k) for k in range(1, BLOCKS)]
    terms = visit_all(corners, bands, probe, amplitude)
    got = lax.all_to_all(terms, "view", 0, 0, tiled=True)
    sums = jnp.sum(got.astype(F32), axis=0)
    update = sums[: 2 * ROWS]
    for k in range(1, BLOCKS):
        update = update + passed_along(sums[k * 2 * ROWS : (k + 1) * 2 * ROWS], k)
    totals = sums[80:104]
    for k in (1, 2, 4, 8):
        totals = totals + lax.ppermute(totals, "slab", [(i, i ^ k) for i in range(lax.axis_size("slab"))])
    ratio = (totals[:16].reshape(2, ROWS, 4, FRAME) / totals[16:].reshape(1, ROWS, 4, FRAME)).reshape(16, COLUMNS)
    whole = lax.all_gather(jnp.concatenate([update.astype(BF16), ratio.astype(BF16)], 0), "view", axis=0)
    object_new = spread(first, whole[:, :16], object_field)
    ratios = whole[:, 16:].astype(F32).reshape(VIEWS, 2, ROWS, 4, FRAME)
    probe_step = ratios.transpose(1, 0, 3, 2, 4).reshape(2, FRAME, FRAME)
    return object_new, probe_step


def solution(mesh):
    return jax.shard_map(
        on_device,
        mesh=mesh,
        in_specs=(P(None, "view", "slab", None), P(), P(("slab", "view"), None, None), P(("slab", "view"), None)),
        out_specs=(P(None, "view", "slab", None), P()),
        check_vma=False,
    )
```

time: 1630 us -> 193 us (0.12)
  matrix products: 789 us -> 0 us
  local copies, waits for them, and re-layouts: 331 us -> 4.4 us
  waiting for transfers between devices: 228 us -> 29.5 us
  other arithmetic: 109 us -> 0.58 us
  loops' own time: 86.6 us -> 0 us
  Pallas kernels: 0 us -> 58 us
  blocking collectives: 30.2 us -> 58.6 us
    dot_general x512 -> x0, matrix products: 789 us -> none  [real_dot(): jnp.dot(left, right, precision=lax.Precision.HIGHEST, preferred_element_t...]
    dynamic_update_slice x32 -> x0, local copies, waits for them, and re-layouts: 194 us -> none  [visit(): update = lax.dynamic_update_slice(update, current + object_term, starts)]
    psum x2 -> x0, waiting for transfers between devices: 181 us -> none  [the longest x1 124 us: on_device(): totals = lax.psum((numer, denom), ('slab', 'view'))]
    gather x96 -> x0, local copies, waits for them, and re-layouts: 98.3 us -> none
    another operation x3 -> x0, loops' own time: 86.6 us -> none  [the longest x1 86.5 us: on_device(): (update, numer, denom), _ = lax.scan(visit, start, (offsets, amplitude))]
    add x66 -> x4, other arithmetic: 64.1 us -> 0.05 us  [on_device(): totals + lax.ppermute(totals, 'slab', [(i, i ^ k) for i in range(lax.axis...]
    pallas_call x0 -> x3, Pallas kernels: none -> 58 us  [the longest x1 35.9 us: visit_all(): pl.pallas_call(visit_kernel, grid=(count // PER_STEP,), in_specs=[SMEM] +...]
    convert_element_type x32 -> x2, other arithmetic: 38.3 us -> 0.04 us  [the longest x1 0.03 us: on_device(): update.astype(BF16)]
  transfers between devices with their start and end apart: 10 -> 13, of which waited for: 8 -> 6; matrix products, arithmetic and copies ran while one was open for 0% -> 0% of each run, Pallas kernels for 0% -> 0%
where the time goes in v1:
time: 193 us
  blocking collectives  58.6 us (30%)
  Pallas kernels  58 us (30%)
  starting transfers between devices  40.6 us (21%)
  waiting for transfers between devices  29.5 us (15%)
  local copies, waits for them, and re-layouts  4.4 us (2%)
    pallas_call x1, Pallas kernels, visit_all(): pl.pallas_call(visit_kernel, grid=(count // PER_STEP,), in_specs=[SMEM] +...  35.9 us
    all_to_all x1, blocking collectives, on_device(): got = lax.all_to_all(terms, 'view', 0, 0, tiled=True)  27.1 us
    all_gather x1, blocking collectives, on_device(): lax.all_gather(jnp.concatenate([update.astype(BF16), ratio.astype(BF16)],...  18 us
    ppermute x8, starting transfers between devices, passed_along(): lax.ppermute(value, 'slab', [(source, source + steps) for source in range...  17.7 us
    ppermute x4, starting transfers between devices, on_device(): lax.ppermute(totals, 'slab', [(i, i ^ k) for i in range(lax.axis_size('sl...  16 us
    all_gather x1, blocking collectives, on_device(): band = lax.all_gather(piece, 'view', axis=0)  13.5 us
    ppermute x8, waiting for transfers between devices, passed_along(): lax.ppermute(value, 'slab', [(source, source + steps) for source in range...  12.4 us
    pallas_call x1, Pallas kernels, spread(): pl.pallas_call(spread_kernel, grid=(VIEWS,), in_specs=[SMEM, pl.BlockSpec...  11.1 us
  transfers between devices with their start and end apart: 13, of which 6 were waited for; matrix products, arithmetic and copies ran while one was open for 0% of the time, Pallas kernels for 0%

profile of v1, /device:TPU:1, one launch (start us, length us, event | category | flops | bytes accessed | tf_op | source)
XLA Modules:
  0.0 192.6 jit_solution(10118528568363243549)
XLA Ops:
  0.6 0.0 copy-start
  0.6 3.4 %copy-done = f32[2,16,64,1024]{3,2,1,0:T(8,128)S(1)} copy-done((f32[2,16,64,1024]{3,2,1,0:T(8,128)S(1)}, f32[2,16,64,1024]{3,2,1,0:T(8,128)}, u32[]{:S(2)}) %copy-start) | copy-done | bytes 8388632
  4.0 0.0 copy-start.4
  4.0 0.0 copy-start.1
  4.0 0.0 copy-start.2
  4.0 0.0 copy-start.3
  4.0 11.1 %shard_map.77 = f32[8,16,1024]{2,1,0:T(8,128)} custom-call(s32[1]{0:T(128)} %bitcast.first_ref, f32[2,16,64,1024]{3,2,1,0:T(8,128)S(1)} %copy-done), custom_call_target="tpu_custom_call" | custom-call | tf_op jit(solution)/shard_map/pallas_call | solution.py:61
  15.1 6.8 %all-to-all-start = ((f32[8,16,1024]{2,1,0:T(8,128)}), f32[8,16,1024]{2,1,0:T(8,128)S(1)}, u32[]{:S(2)}, u32[]{:S(2)}) async-start(f32[8,16,1024]{2,1,0:T(8,128)} %shard_map.77), calls=%async_computation | async-start | bytes 1048576 | tf_op jit(solution)/shard_map/all_to_all | solution.py:206
  21.9 9.5 %all-to-all-done = f32[8,16,1024]{2,1,0:T(8,128)S(1)} async-done(((f32[8,16,1024]{2,1,0:T(8,128)}), f32[8,16,1024]{2,1,0:T(8,128)S(1)}, u32[]{:S(2)}, u32[]{:S(2)}) %all-to-all-start) | async-done | bytes 524320 | tf_op jit(solution)/shard_map/all_to_all | solution.py:206
  31.4 13.5 %all-gather = bf16[128,1024]{1,0:T(8,128)(2,1)S(1)} all-gather(bf16[16,1024]{1,0:T(8,128)(2,1)S(1)} %reduce_sum.18), channel_id=2, replica_groups=mesh['slab'=16,'view'=8] {'view'}, dimensions={0}, use_global_device_ids=true | all-gather | bytes 294912 | tf_op jit(solution)/shard_map/all_gather | solution.py:208
  45.0 1.3 collective-permute-start.3
  46.3 1.3 collective-permute-start.2
  47.6 1.3 collective-permute-start.1
  48.9 1.3 collective-permute-start
  50.2 0.1 pad_add_fusion
  50.2 0.0 copy-done.4
  50.2 0.1 copy.10
  50.3 0.0 slice-start
  50.3 0.0 slice-start.1
  50.4 4.3 %collective-permute-done.3.b4 = bf16[8,16,1024]{2,1,0:T(8,128)(2,1)S(1)} collective-permute-done((bf16[8,16,1024]{2,1,0:T(8,128)(2,1)S(1)}, bf16[8,16,1024]{2,1,0:T(8,128)(2,1)S(1)}, u32[]{:S(2)}, u32[]{:S(2)}) %collective-permute-start.3) | collective-permute-done | bytes 262176 | tf_op jit(solution)/shard_map/ppermute | solution.py:198
  54.6 8.1 %collective-permute-done.2.b3 = bf16[8,16,1024]{2,1,0:T(8,128)(2,1)S(1)} collective-permute-done((bf16[8,16,1024]{2,1,0:T(8,128)(2,1)S(1)}, bf16[8,16,1024]{2,1,0:T(8,128)(2,1)S(1)}, u32[]{:S(2)}, u32[]{:S(2)}) %collective-permute-start.2) | collective-permute-done | bytes 262176 | tf_op jit(solution)/shard_map/ppermute | solution.py:198
  62.7 0.0 collective-permute-done.1.b2
  62.7 0.0 collective-permute-done.b1
  62.7 0.0 copy-done.1
  62.7 0.0 copy-done.2
  62.8 0.0 copy-done.3
  62.8 35.9 %shard_map.78 = bf16[8,112,1024]{2,1,0:T(8,128)(2,1)S(1)} custom-call(s32[32,2]{1,0:T(8,128)S(1)} %broadcast_subtract_fusion.off_ref, bf16[8,16,1024]{2,1,0:T(8,128)(2,1)S(1)} %bitcast.17, bf16[8,16,1024]{2,1,0:T(8,128)(2,1)S(1)} %collective-permute-done.b1, bf16[8,16,1024]{2,1,0:T(8,128)(2,1)S(1)} %collective-permute-done.1.b2, ...), custom_call_target="tpu_custom_call" | custom-call | tf_op jit(solution)/shard_map/pallas_call | solution.py:180
  98.6 27.1 %all_to_all.10 = bf16[8,112,1024]{2,1,0:T(8,128)(2,1)S(1)} all-to-all(bf16[8,112,1024]{2,1,0:T(8,128)(2,1)S(1)} %shard_map.78), channel_id=1, replica_groups=mesh['slab'=16,'view'=8] {'view'}, dimensions={0} | all-to-all | bytes 3670016 | tf_op jit(solution)/shard_map/all_to_all | solution.py:211
  125.8 0.3 convert_reduce_fusion
  126.1 2.9 %collective-permute-start.8 = (f32[24,1024]{1,0:T(8,128)S(1)}, f32[24,1024]{1,0:T(8,128)S(1)}, u32[]{:S(2)}, u32[]{:S(2)}) collective-permute-start(f32[24,1024]{1,0:T(8,128)S(1)} %slice.45), channel_id=1, source_target_pairs={{0,8},{8,0},{16,24},{24,16},{32,40},{40,32},{48,56},{56,48},{64,72... | collective-permute-start | bytes 294920 | tf_op jit(solution)/shard_map/ppermute | solution.py:218
  129.0 2.0 %collective-permute-done.8 = f32[24,1024]{1,0:T(8,128)S(1)} collective-permute-done((f32[24,1024]{1,0:T(8,128)S(1)}, f32[24,1024]{1,0:T(8,128)S(1)}, u32[]{:S(2)}, u32[]{:S(2)}) %collective-permute-start.8) | collective-permute-done | bytes 98336 | tf_op jit(solution)/shard_map/ppermute | solution.py:218
  131.0 9.7 %collective-permute-start.9 = (f32[24,1024]{1,0:T(8,128)S(1)}, f32[24,1024]{1,0:T(8,128)S(1)}, u32[]{:S(2)}, u32[]{:S(2)}) collective-permute-start(f32[24,1024]{1,0:T(8,128)S(1)} %slice_add_fusion.1), channel_id=1, source_target_pairs={{0,16},{8,24},{16,0},{24,8},{32,48},{40,56},{48,32},{56,40},{64,80... | collective-permute-start | bytes 294920 | tf_op jit(solution)/shard_map/ppermute | solution.py:218
  140.7 2.5 %collective-permute-done.9 = f32[24,1024]{1,0:T(8,128)S(1)} collective-permute-done((f32[24,1024]{1,0:T(8,128)S(1)}, f32[24,1024]{1,0:T(8,128)S(1)}, u32[]{:S(2)}, u32[]{:S(2)}) %collective-permute-start.9) | collective-permute-done | bytes 98336 | tf_op jit(solution)/shard_map/ppermute | solution.py:218
  143.2 1.3 collective-permute-start.10
  144.5 2.3 %collective-permute-start.4 = (f32[16,1024]{1,0:T(8,128)S(1)}, f32[16,1024]{1,0:T(8,128)S(1)}, u32[]{:S(2)}, u32[]{:S(2)}) collective-permute-start(f32[16,1024]{1,0:T(8,128)S(1)} %get-tuple-element.4), channel_id=1, source_target_pairs={{0,8},{8,16},{16,24},{24,32},{32,40},{40,48},{48,56},{56,64},{64,7... | collective-permute-start | bytes 196616 | tf_op jit(solution)/shard_map/ppermute | solution.py:198
  146.8 2.1 %collective-permute-start.7 = (f32[16,1024]{1,0:T(8,128)S(1)}, f32[16,1024]{1,0:T(8,128)S(1)}, u32[]{:S(2)}, u32[]{:S(2)}) collective-permute-start(f32[16,1024]{1,0:T(8,128)S(1)} %get-tuple-element.5), channel_id=1, source_target_pairs={{0,32},{8,40},{16,48},{24,56},{32,64},{40,72},{48,80},{56,88},{64,... | collective-permute-start | bytes 196616 | tf_op jit(solution)/shard_map/ppermute | solution.py:198
  149.0 4.9 %collective-permute-start.6 = (f32[16,1024]{1,0:T(8,128)S(1)}, f32[16,1024]{1,0:T(8,128)S(1)}, u32[]{:S(2)}, u32[]{:S(2)}) collective-permute-start(f32[16,1024]{1,0:T(8,128)S(1)} %get-tuple-element.6), channel_id=1, source_target_pairs={{0,24},{8,32},{16,40},{24,48},{32,56},{40,64},{48,72},{56,80},{64,... | collective-permute-start | bytes 196616 | tf_op jit(solution)/shard_map/ppermute | solution.py:198
  153.9 3.2 %collective-permute-start.5 = (f32[16,1024]{1,0:T(8,128)S(1)}, f32[16,1024]{1,0:T(8,128)S(1)}, u32[]{:S(2)}, u32[]{:S(2)}) collective-permute-start(f32[16,1024]{1,0:T(8,128)S(1)} %get-tuple-element.7), channel_id=1, source_target_pairs={{0,16},{8,24},{16,32},{24,40},{32,48},{40,56},{48,64},{56,72},{64,... | collective-permute-start | bytes 196616 | tf_op jit(solution)/shard_map/ppermute | solution.py:198
  157.1 0.0 collective-permute-done.10
  157.2 2.1 %collective-permute-start.11 = (f32[24,1024]{1,0:T(8,128)S(1)}, f32[24,1024]{1,0:T(8,128)S(1)}, u32[]{:S(2)}, u32[]{:S(2)}) collective-permute-start(f32[24,1024]{1,0:T(8,128)S(1)} %add.30), channel_id=1, source_target_pairs={{0,64},{8,72},{16,80},{24,88},{32,96},{40,104},{48,112},{56,120},{... | collective-permute-start | bytes 294920 | tf_op jit(solution)/shard_map/ppermute | solution.py:218
  159.3 0.0 collective-permute-done.4
  159.3 0.0 collective-permute-done.7
  159.3 0.0 collective-permute-done.6
  159.3 0.0 collective-permute-done.5
  159.3 3.2 %collective-permute-done.11 = f32[24,1024]{1,0:T(8,128)S(1)} collective-permute-done((f32[24,1024]{1,0:T(8,128)S(1)}, f32[24,1024]{1,0:T(8,128)S(1)}, u32[]{:S(2)}, u32[]{:S(2)}) %collective-permute-start.11) | collective-permute-done | bytes 98336 | tf_op jit(solution)/shard_map/ppermute | solution.py:218
  162.6 18.0 %all-gather.1 = bf16[256,1024]{1,0:T(8,128)(2,1)S(1)} all-gather(bf16[32,1024]{1,0:T(8,128)(2,1)S(1)} %pad_maximum_fusion), channel_id=3, replica_groups=mesh['slab'=16,'view'=8] {'view'}, dimensions={0}, use_global_device_ids=true | all-gather | bytes 589824 | tf_op jit(solution)/shard_map/all_gather | solution.py:220
  180.7 0.8 copy.12
  181.5 0.0 slice-done
  181.5 0.0 slice-done.1
  181.5 11.1 %shard_map.79 = f32[2,16,64,1024]{3,2,1,0:T(8,128)} custom-call(s32[1]{0:T(128)} %bitcast.first_ref, bf16[8,16,1024]{2,1,0:T(8,128)(2,1)S(1)} %get-tuple-element.3.update_ref, f32[2,16,64,1024]{3,2,1,0:T(8,128)S(1)} %bitcast.12), custom_call_target="tpu_custom_call" | custom-call | tf_op jit(solution)/shard_map/pallas_call | solution.py:84
  (16 shorter events, 0.3 us)
Async XLA Ops:
  0.6 3.4 %copy-start = (f32[2,16,64,1024]{3,2,1,0:T(8,128)S(1)}, f32[2,16,64,1024]{3,2,1,0:T(8,128)}, u32[]{:S(2)}) copy-start(f32[2,16,64,1024]{3,2,1,0:T(8,128)} %field_ref.3) | copy-start | bytes 25165828
  4.0 46.2 %copy-start.4 = (s32[32,2]{0,1:T(2,128)S(1)}, s32[32,2]{0,1:T(2,128)}, u32[]{:S(2)}) copy-start(s32[32,2]{0,1:T(2,128)} %param.9) | copy-start | bytes 772
  4.0 58.7 %copy-start.1 = (f32[2,256,256]{2,1,0:T(8,128)S(1)}, f32[2,256,256]{2,1,0:T(8,128)}, u32[]{:S(2)}) copy-start(f32[2,256,256]{2,1,0:T(8,128)} %probe_ref.1) | copy-start | bytes 1572868
  4.0 58.7 %copy-start.2 = (bf16[512,512]{1,0:T(8,128)(2,1)S(1)}, bf16[512,512]{1,0:T(8,128)(2,1)}, u32[]{:S(2)}) copy-start(bf16[512,512]{1,0:T(8,128)(2,1)} %constant.22.clone.back_ref) | copy-start | bytes 1572868
  4.0 58.7 %copy-start.3 = (bf16[512,512]{1,0:T(8,128)(2,1)S(1)}, bf16[512,512]{1,0:T(8,128)(2,1)}, u32[]{:S(2)}) copy-start(bf16[512,512]{1,0:T(8,128)(2,1)} %constant.21.clone.fore_ref) | copy-start | bytes 1572868
  15.1 16.3 %all-to-all-start = ((f32[8,16,1024]{2,1,0:T(8,128)}), f32[8,16,1024]{2,1,0:T(8,128)S(1)}, u32[]{:S(2)}, u32[]{:S(2)}) async-start(f32[8,16,1024]{2,1,0:T(8,128)} %shard_map.77), calls=%async_computation | async-start | bytes 1048576 | tf_op jit(solution)/shard_map/all_to_all | solution.py:206
  45.0 9.6 %collective-permute-start.3 = (bf16[8,16,1024]{2,1,0:T(8,128)(2,1)S(1)}, bf16[8,16,1024]{2,1,0:T(8,128)(2,1)S(1)}, u32[]{:S(2)}, u32[]{:S(2)}) collective-permute-start(bf16[8,16,1024]{2,1,0:T(8,128)(2,1)S(1)} %bitcast.13), channel_id=1, source_target_pairs={{32,0},{40,8},{48,16},{56,24},{64,32},{72,40},{80,48},{88,56},{96,... | collective-permute-start | bytes 786440 | tf_op jit(solution)/shard_map/ppermute | solution.py:198
  46.3 16.5 %collective-permute-start.2 = (bf16[8,16,1024]{2,1,0:T(8,128)(2,1)S(1)}, bf16[8,16,1024]{2,1,0:T(8,128)(2,1)S(1)}, u32[]{:S(2)}, u32[]{:S(2)}) collective-permute-start(bf16[8,16,1024]{2,1,0:T(8,128)(2,1)S(1)} %bitcast.14), channel_id=1, source_target_pairs={{24,0},{32,8},{40,16},{48,24},{56,32},{64,40},{72,48},{80,56},{88,... | collective-permute-start | bytes 786440 | tf_op jit(solution)/shard_map/ppermute | solution.py:198
  47.6 15.2 %collective-permute-start.1 = (bf16[8,16,1024]{2,1,0:T(8,128)(2,1)S(1)}, bf16[8,16,1024]{2,1,0:T(8,128)(2,1)S(1)}, u32[]{:S(2)}, u32[]{:S(2)}) collective-permute-start(bf16[8,16,1024]{2,1,0:T(8,128)(2,1)S(1)} %bitcast.15), channel_id=1, source_target_pairs={{16,0},{24,8},{32,16},{40,24},{48,32},{56,40},{64,48},{72,56},{80,... | collective-permute-start | bytes 786440 | tf_op jit(solution)/shard_map/ppermute | solution.py:198
  48.9 13.9 %collective-permute-start = (bf16[8,16,1024]{2,1,0:T(8,128)(2,1)S(1)}, bf16[8,16,1024]{2,1,0:T(8,128)(2,1)S(1)}, u32[]{:S(2)}, u32[]{:S(2)}) collective-permute-start(bf16[8,16,1024]{2,1,0:T(8,128)(2,1)S(1)} %bitcast.16), channel_id=1, source_target_pairs={{8,0},{16,8},{24,16},{32,24},{40,32},{48,40},{56,48},{64,56},{72,6... | collective-permute-start | bytes 786440 | tf_op jit(solution)/shard_map/ppermute | solution.py:198
  50.3 131.2 %slice-start = ((s8[8388608]{0:T(1024)(128)(4,1)}), s8[4194304]{0:T(1024)(128)(4,1)S(1)}, s32[]{:S(2)}) async-start(s8[8388608]{0:T(1024)(128)(4,1)} %bitcast.11), calls=%async_computation.2 | async-start | bytes 8388608
  50.3 131.2 %slice-start.1 = ((s8[8388608]{0:T(1024)(128)(4,1)}), s8[4194304]{0:T(1024)(128)(4,1)S(1)}, s32[]{:S(2)}) async-start(s8[8388608]{0:T(1024)(128)(4,1)} %bitcast.11), calls=%async_computation.3 | async-start | bytes 8388608
  126.1 4.9 %collective-permute-start.8 = (f32[24,1024]{1,0:T(8,128)S(1)}, f32[24,1024]{1,0:T(8,128)S(1)}, u32[]{:S(2)}, u32[]{:S(2)}) collective-permute-start(f32[24,1024]{1,0:T(8,128)S(1)} %slice.45), channel_id=1, source_target_pairs={{0,8},{8,0},{16,24},{24,16},{32,40},{40,32},{48,56},{56,48},{64,72... | collective-permute-start | bytes 294920 | tf_op jit(solution)/shard_map/ppermute | solution.py:218
  131.0 12.2 %collective-permute-start.9 = (f32[24,1024]{1,0:T(8,128)S(1)}, f32[24,1024]{1,0:T(8,128)S(1)}, u32[]{:S(2)}, u32[]{:S(2)}) collective-permute-start(f32[24,1024]{1,0:T(8,128)S(1)} %slice_add_fusion.1), channel_id=1, source_target_pairs={{0,16},{8,24},{16,0},{24,8},{32,48},{40,56},{48,32},{56,40},{64,80... | collective-permute-start | bytes 294920 | tf_op jit(solution)/shard_map/ppermute | solution.py:218
  143.2 13.9 %collective-permute-start.10 = (f32[24,1024]{1,0:T(8,128)S(1)}, f32[24,1024]{1,0:T(8,128)S(1)}, u32[]{:S(2)}, u32[]{:S(2)}) collective-permute-start(f32[24,1024]{1,0:T(8,128)S(1)} %add.29), channel_id=1, source_target_pairs={{0,32},{8,40},{16,48},{24,56},{32,0},{40,8},{48,16},{56,24},{64,96... | collective-permute-start | bytes 294920 | tf_op jit(solution)/shard_map/ppermute | solution.py:218
  144.5 14.8 %collective-permute-start.4 = (f32[16,1024]{1,0:T(8,128)S(1)}, f32[16,1024]{1,0:T(8,128)S(1)}, u32[]{:S(2)}, u32[]{:S(2)}) collective-permute-start(f32[16,1024]{1,0:T(8,128)S(1)} %get-tuple-element.4), channel_id=1, source_target_pairs={{0,8},{8,16},{16,24},{24,32},{32,40},{40,48},{48,56},{56,64},{64,7... | collective-permute-start | bytes 196616 | tf_op jit(solution)/shard_map/ppermute | solution.py:198
  146.8 12.5 %collective-permute-start.7 = (f32[16,1024]{1,0:T(8,128)S(1)}, f32[16,1024]{1,0:T(8,128)S(1)}, u32[]{:S(2)}, u32[]{:S(2)}) collective-permute-start(f32[16,1024]{1,0:T(8,128)S(1)} %get-tuple-element.5), channel_id=1, source_target_pairs={{0,32},{8,40},{16,48},{24,56},{32,64},{40,72},{48,80},{56,88},{64,... | collective-permute-start | bytes 196616 | tf_op jit(solution)/shard_map/ppermute | solution.py:198
  149.0 10.3 %collective-permute-start.6 = (f32[16,1024]{1,0:T(8,128)S(1)}, f32[16,1024]{1,0:T(8,128)S(1)}, u32[]{:S(2)}, u32[]{:S(2)}) collective-permute-start(f32[16,1024]{1,0:T(8,128)S(1)} %get-tuple-element.6), channel_id=1, source_target_pairs={{0,24},{8,32},{16,40},{24,48},{32,56},{40,64},{48,72},{56,80},{64,... | collective-permute-start | bytes 196616 | tf_op jit(solution)/shard_map/ppermute | solution.py:198
  153.9 5.4 %collective-permute-start.5 = (f32[16,1024]{1,0:T(8,128)S(1)}, f32[16,1024]{1,0:T(8,128)S(1)}, u32[]{:S(2)}, u32[]{:S(2)}) collective-permute-start(f32[16,1024]{1,0:T(8,128)S(1)} %get-tuple-element.7), channel_id=1, source_target_pairs={{0,16},{8,24},{16,32},{24,40},{32,48},{40,56},{48,64},{56,72},{64,... | collective-permute-start | bytes 196616 | tf_op jit(solution)/shard_map/ppermute | solution.py:198
  157.2 5.4 %collective-permute-start.11 = (f32[24,1024]{1,0:T(8,128)S(1)}, f32[24,1024]{1,0:T(8,128)S(1)}, u32[]{:S(2)}, u32[]{:S(2)}) collective-permute-start(f32[24,1024]{1,0:T(8,128)S(1)} %add.30), channel_id=1, source_target_pairs={{0,64},{8,72},{16,80},{24,88},{32,96},{40,104},{48,112},{56,120},{... | collective-permute-start | bytes 294920 | tf_op jit(solution)/shard_map/ppermute | solution.py:218

commit v2 on v1

v2 whole, which is shorter than its diff:
```python
import functools
import math

import jax
import jax.numpy as jnp
import ml_dtypes
import numpy as np
from jax import lax
from jax.experimental import pallas as pl
from jax.experimental.pallas import tpu as pltpu
from jax.sharding import PartitionSpec as P

F32 = jnp.float32
BF16 = jnp.bfloat16
FRAME = 256
LANES = 128
SLAB = 64
VIEWS = 8
ROWS = SLAB // VIEWS
COLUMNS = 1024
TILES = COLUMNS // LANES
BLOCKS = 5
BAND = BLOCKS * SLAB
PER_STEP = 4
SUMS = BLOCKS * SLAB + 4 * 4 * ROWS
VMEM = pl.BlockSpec(memory_space=pltpu.VMEM)
SMEM = pl.BlockSpec(memory_space=pltpu.SMEM)


def dft_blocks(order):
    index = np.arange(order, dtype=np.int32)
    product = index[:, None] * index[None, :] % order
    angle = product.astype(np.float32) * np.float32(-2.0 * math.pi / order)
    factor = np.float32(1.0 / math.sqrt(order))
    c, s = np.cos(angle) * factor, np.sin(angle) * factor
    fore = np.block([[c, -s], [s, c]]).astype(ml_dtypes.bfloat16)
    back = np.block([[c, s], [-s, c]]).astype(ml_dtypes.bfloat16)
    return fore, back


def tiles_of(value):
    return [value[:, t * LANES : (t + 1) * LANES] for t in range(TILES)]


def to_right(tiles, steps):
    lane = lax.broadcasted_iota(jnp.int32, tiles[0].shape, 1)
    turned = [pltpu.roll(x, steps, 1) for x in tiles]
    return [jnp.where(lane >= steps, x, before) for x, before in zip(turned, [jnp.zeros_like(tiles[0])] + turned)]


def to_left(tiles, steps):
    lane = lax.broadcasted_iota(jnp.int32, tiles[0].shape, 1)
    turned = [pltpu.roll(x, (LANES - steps) % LANES, 1) for x in tiles]
    return [jnp.where(lane < LANES - steps, x, after) for x, after in zip(turned, turned[1:] + [jnp.zeros_like(tiles[0])])]


def chunk_at(place, half, j):
    return 4 * ((place[1] + half) % 2) + (place[0] + 4 - j) % 4


def project_kernel(place, field_ref, out_ref):
    layers = field_ref.shape[1]
    values = [tiles_of(jnp.concatenate([field_ref[0, k], field_ref[1, k]], 0)) for k in range(layers)]
    steps = 1
    while len(values) > 1:
        moved = [to_right(x, steps) for x in values[1::2]]
        values = [[a + b for a, b in zip(x, y)] for x, y in zip(values[0::2], moved)]
        steps *= 2
    for t, x in enumerate(to_right(values[0], place[2])):
        out_ref[0, :, t * LANES : (t + 1) * LANES] = x


def project(place, field, half):
    layers = field.shape[1]
    return pl.pallas_call(
        project_kernel,
        grid_spec=pltpu.PrefetchScalarGridSpec(
            num_scalar_prefetch=1,
            grid=(4,),
            in_specs=[pl.BlockSpec((2, layers, ROWS, COLUMNS), lambda i, place: (0, 0, chunk_at(place, half, 4 - i), 0))],
            out_specs=pl.BlockSpec((1, 2 * ROWS, COLUMNS), lambda i, place: (i, 0, 0)),
        ),
        out_shape=jax.ShapeDtypeStruct((4, 2 * ROWS, COLUMNS), F32),
        compiler_params=pltpu.CompilerParams(vmem_limit_bytes=60 << 20),
        cost_estimate=pl.CostEstimate(flops=layers * 4 * 16 * 1024 * 6, bytes_accessed=(4 << 20) + (256 << 10), transcendentals=0),
    )(place, field)


def spread_kernel(place, mine_ref, theirs_ref, field_ref, out_ref):
    layers = field_ref.shape[1]
    half, j = pl.program_id(0), pl.program_id(1)
    rows = pl.ds(pl.multiple_of(j * 2 * ROWS, 2 * ROWS), 2 * ROWS)
    update = jnp.where(half == 0, mine_ref[rows, :].astype(F32), theirs_ref[rows, :].astype(F32))
    base = to_left(tiles_of(update), place[2])
    for k in range(layers):
        for t, x in enumerate(to_left(base, k) if k else base):
            for part in range(2):
                columns = slice(t * LANES, (t + 1) * LANES)
                out_ref[part, k, :, columns] = field_ref[part, k, :, columns] + x[part * ROWS : (part + 1) * ROWS]


def spread(place, mine, theirs, field):
    layers = field.shape[1]
    block = pl.BlockSpec((2, layers, ROWS, COLUMNS), lambda i, j, place: (0, 0, chunk_at(place, i, j), 0))
    return pl.pallas_call(
        spread_kernel,
        grid_spec=pltpu.PrefetchScalarGridSpec(
            num_scalar_prefetch=1, grid=(2, 4), in_specs=[VMEM, VMEM, block], out_specs=block
        ),
        out_shape=jax.ShapeDtypeStruct(field.shape, F32),
        compiler_params=pltpu.CompilerParams(vmem_limit_bytes=32 << 20),
        cost_estimate=pl.CostEstimate(flops=layers * 8 * 16 * 1024 * 4, bytes_accessed=16 << 20, transcendentals=0),
    )(place, mine, theirs, field)


def join_kernel(place, mine_ref, theirs_ref, out_ref):
    for half, ref in enumerate((mine_ref, theirs_ref)):
        for j in range(4):
            first = chunk_at(place, half, j) * (FRAME // VIEWS)
            for part in range(2):
                x = ref[j * 2 * ROWS : (j + 1) * 2 * ROWS, :][part * ROWS : (part + 1) * ROWS]
                for g in range(4):
                    rows = pl.ds(pl.multiple_of(first + g * ROWS, ROWS), ROWS)
                    out_ref[part, rows, :] = x[:, g * FRAME : (g + 1) * FRAME].astype(F32)


def join(place, mine, theirs):
    return pl.pallas_call(
        join_kernel,
        in_specs=[SMEM, VMEM, VMEM],
        out_specs=VMEM,
        out_shape=jax.ShapeDtypeStruct((2, FRAME, FRAME), F32),
        cost_estimate=pl.CostEstimate(flops=1000, bytes_accessed=1 << 20, transcendentals=0),
    )(place, mine, theirs)


def dot(left, right):
    return jnp.dot(left, right, preferred_element_type=F32)


def visit_kernel(place, off_ref, *refs):
    bands, (probe_ref, fore_ref, back_ref, amp_ref, mine_ref, theirs_ref, band, upd, num) = refs[:10], refs[10:]
    step = pl.program_id(0)

    @pl.when(step == 0)
    def _():
        for i, ref in enumerate(bands):
            for j in range(4):
                x = ref[j * 2 * ROWS : (j + 1) * 2 * ROWS, :].astype(F32)
                first = pl.multiple_of(i % BLOCKS * SLAB + chunk_at(place, i // BLOCKS, j) * ROWS, ROWS)
                for part in range(2):
                    for t in range(TILES):
                        band[part, t, pl.ds(first, ROWS), :] = x[part * ROWS : (part + 1) * ROWS, t * LANES : (t + 1) * LANES]
        upd[...] = jnp.zeros_like(upd)
        num[...] = jnp.zeros_like(num)

    lane = lax.broadcasted_iota(jnp.int32, (FRAME, LANES), 1)

    def corner(j):
        p = step * PER_STEP + j
        r, c = off_ref[p, 0], off_ref[p, 1]
        q, m = c // LANES, c % LANES
        return r, (q, q + 1, jnp.minimum(q + 2, TILES - 1)), m

    def patch_of(part, r, q, m):
        turn = (LANES - m) % LANES
        tiles = [pltpu.roll(band[part, t, pl.ds(r, FRAME), :], turn, 1) for t in q]
        keep = lane < LANES - m
        return jnp.concatenate([jnp.where(keep, tiles[0], tiles[1]), jnp.where(keep, tiles[1], tiles[2])], 1)

    def add_to(part, value, r, q, m):
        left = pltpu.roll(value[:, :LANES], m, 1)
        right = pltpu.roll(value[:, LANES:], m, 1)
        keep = lane >= m
        terms = [jnp.where(keep, left, 0.0), jnp.where(keep, right, left), jnp.where(keep, 0.0, right)]
        for t, x in zip(q, terms):
            upd[part, t, pl.ds(r, FRAME), :] += x

    pr, pi = probe_ref[0], probe_ref[1]
    corners = [corner(j) for j in range(PER_STEP)]
    stage = []
    for r, q, m in corners:
        a, b = patch_of(0, r, q, m), patch_of(1, r, q, m)
        stage.append((a, b, pr * a - pi * b, pr * b + pi * a))
    half = [dot(fore_ref[...], jnp.concatenate([er, ei], 0).astype(BF16)) for _, _, er, ei in stage]
    half = [jnp.concatenate([h[:FRAME], h[FRAME:]], 1).astype(BF16) for h in half]
    far = [dot(h, back_ref[...]) for h in half]
    fixed = []
    for j, f in enumerate(far):
        fr, fi = f[:, :FRAME], f[:, FRAME:]
        factor = amp_ref[j] * lax.rsqrt(fr * fr + fi * fi + 0.25)
        fixed.append(jnp.concatenate([fr * factor, fi * factor], 1).astype(BF16))
    back = [dot(g, fore_ref[...]) for g in fixed]
    back = [jnp.concatenate([h[:, :FRAME], h[:, FRAME:]], 0).astype(BF16) for h in back]
    new = [dot(back_ref[...], h) for h in back]
    for (r, q, m), (a, b, er, ei), n in zip(corners, stage, new):
        dr, di = n[:FRAME] - er, n[FRAME:] - ei
        add_to(0, pr * dr + pi * di, r, q, m)
        add_to(1, pr * di - pi * dr, r, q, m)
        num[0] += a * dr + b * di
        num[1] += a * di - b * dr
        num[2] += a * a + b * b

    @pl.when(step == pl.num_programs(0) - 1)
    def _():
        peak = jnp.max(pr * pr + pi * pi) + 1e-06
        scale = 0.5 / jnp.full((2 * ROWS, COLUMNS), peak, F32)
        for half, ref in enumerate((mine_ref, theirs_ref)):
            for e in range(4):
                chunk = chunk_at(place, half, 4 - e)
                for b in range(BLOCKS):
                    rows = pl.ds(pl.multiple_of(b * SLAB + chunk * ROWS, ROWS), ROWS)
                    x = [jnp.concatenate([upd[part, t, rows, :] for t in range(TILES)], 1) for part in range(2)]
                    first = (b * 4 + e) * 2 * ROWS
                    ref[first : first + 2 * ROWS, :] = (jnp.concatenate(x, 0) * scale).astype(BF16)
                planes = []
                for k in range(3):
                    rows = [pl.ds(pl.multiple_of(chunk * 4 * ROWS + g * ROWS, ROWS), ROWS) for g in range(4)]
                    planes.append(jnp.concatenate([num[k, x, :] for x in rows], 1))
                first = 4 * 2 * ROWS * BLOCKS + e * 4 * ROWS
                ref[first : first + 4 * ROWS, :] = jnp.concatenate(planes + [jnp.zeros_like(planes[0])], 0).astype(BF16)


def visit_all(place, corners, bands, probe, amplitude):
    count = amplitude.shape[0]
    fore, back = dft_blocks(FRAME)
    amp_spec = pl.BlockSpec((PER_STEP, FRAME, FRAME), lambda i: (i, 0, 0))
    return pl.pallas_call(
        visit_kernel,
        grid=(count // PER_STEP,),
        in_specs=[SMEM, SMEM] + [VMEM] * 13 + [amp_spec],
        out_specs=[VMEM] * 2,
        out_shape=[jax.ShapeDtypeStruct((SUMS, COLUMNS), BF16)] * 2,
        scratch_shapes=[
            pltpu.VMEM((2, TILES, BAND, LANES), F32),
            pltpu.VMEM((2, TILES, BAND, LANES), F32),
            pltpu.VMEM((3, FRAME, FRAME), F32),
        ],
        compiler_params=pltpu.CompilerParams(vmem_limit_bytes=48 << 20),
        cost_estimate=pl.CostEstimate(flops=count * 16 * 2 * FRAME**3, bytes_accessed=16 << 20, transcendentals=0),
    )(place, corners, *bands, probe, fore, back, amplitude)


def slab_along(value, steps):
    count = lax.axis_size("slab")
    first, last = (max(0, -steps), min(count, count - steps))
    return lax.ppermute(value, "slab", [(source, source + steps) for source in range(first, last)])


def slab_swap(value, bit):
    return lax.ppermute(value, "slab", [(i, i ^ bit) for i in range(lax.axis_size("slab"))])


def z_along(value, steps):
    return lax.ppermute(value, "view", [(i, (i + 2 * steps) % VIEWS) for i in range(VIEWS)])


def core_swap(value):
    return lax.ppermute(value, "view", [(i, i ^ 1) for i in range(VIEWS)])


def z_sum(value):
    return value[0] + z_along(value[1], 1) + z_along(value[2], 2) + z_along(value[3], 3)


def z_gather(value):
    return jnp.concatenate([value] + [z_along(value, d) for d in (1, 2, 3)], 0)


def on_device(object_field, probe, amplitude, offsets):
    layers = object_field.shape[1]
    view = lax.axis_index("view")
    place = jnp.stack([view // 2, view % 2, view * layers]).astype(jnp.int32)
    corners = offsets - jnp.stack([lax.axis_index("slab") * SLAB, 0]).astype(jnp.int32)

    received = core_swap(project(place, object_field, 1))
    piece = z_sum(project(place, object_field, 0) + received).astype(BF16)
    mine = z_gather(piece)
    bands = [mine] + [slab_along(mine, -k) for k in range(1, BLOCKS)]
    bands = bands + [core_swap(x) for x in bands]

    mine, theirs = visit_all(place, corners, bands, probe, amplitude)
    both = mine.astype(F32) + core_swap(theirs).astype(F32)
    terms = [both[k * SLAB : (k + 1) * SLAB] for k in range(BLOCKS)]
    update = terms[0]
    for k in range(1, BLOCKS):
        update = update + slab_along(terms[k].astype(BF16), k).astype(F32)
    update = z_gather(z_sum(update.reshape(4, 2 * ROWS, COLUMNS)).astype(BF16))
    object_new = spread(place, update, core_swap(update), object_field)

    totals = z_sum(both[BLOCKS * SLAB :].reshape(4, 4 * ROWS, COLUMNS)[:, : 3 * ROWS])
    for bit in (1, 2, 4, 8):
        totals = totals + slab_swap(totals, bit)
    ratio = (totals[: 2 * ROWS].reshape(2, ROWS, COLUMNS) / totals[2 * ROWS :]).reshape(2 * ROWS, COLUMNS)
    ratio = z_gather(ratio.astype(BF16))
    probe_step = join(place, ratio, core_swap(ratio))
    return object_new, probe_step


def solution(mesh):
    return jax.shard_map(
        on_device,
        mesh=mesh,
        in_specs=(P(None, "view", "slab", None), P(), P(("slab", "view"), None, None), P(("slab", "view"), None)),
        out_specs=(P(None, "view", "slab", None), P()),
        check_vma=False,
    )
```

time: 193 us -> 156 us (0.81)
  blocking collectives: 58.6 us -> 0 us
  starting transfers between devices: 40.6 us -> 73.8 us
  waiting for transfers between devices: 29.5 us -> 18.3 us
  local copies, waits for them, and re-layouts: 4.4 us -> 0.89 us
    ppermute x12 -> x39, starting transfers between devices: 33.8 us -> 73.8 us  [the longest x8 23 us: slab_along(): lax.ppermute(value, 'slab', [(source, source + steps) for source in range...]
    all_gather x2 -> x0, blocking collectives: 31.5 us -> none  [the longest x1 18 us: on_device(): lax.all_gather(jnp.concatenate([update.astype(BF16), ratio.astype(BF16)],...]
    all_to_all x1 -> x0, blocking collectives: 27.1 us -> none  [on_device(): got = lax.all_to_all(terms, 'view', 0, 0, tiled=True)]
    all_to_all x1 -> x0, waiting for transfers between devices: 9.48 us -> none  [on_device(): got = lax.all_to_all(partial, 'view', 0, 0, tiled=True)]
    all_to_all x1 -> x0, starting transfers between devices: 6.81 us -> none  [on_device(): got = lax.all_to_all(partial, 'view', 0, 0, tiled=True)]
    unnamed x15 -> x19, local copies, waits for them, and re-layouts: 3.49 us -> 0.77 us
    ppermute x12 -> x39, waiting for transfers between devices: 20.1 us -> 18.3 us  [the longest x18 9.49 us: z_along(): lax.ppermute(value, 'view', [(i, (i + 2 * steps) % VIEWS) for i in range(...]
    pallas_call x3 -> x5, Pallas kernels: 58 us -> 58.8 us  [the longest x1 39.9 us: visit_all(): pl.pallas_call(visit_kernel, grid=(count // PER_STEP,), in_specs=[SMEM, S...]
  transfers between devices with their start and end apart: 13 -> 39, of which waited for: 6 -> 11; matrix products, arithmetic and copies ran while one was open for 0% -> 0% of each run, Pallas kernels for 0% -> 8%
where the time goes in v2:
time: 156 us; the launch traced here: 155 us
  starting transfers between devices  73.8 us (47%)
  Pallas kernels  58.8 us (38%)
  waiting for transfers between devices  18.3 us (12%)
  other arithmetic  2.35 us (2%)
    pallas_call x1, Pallas kernels, visit_all(): pl.pallas_call(visit_kernel, grid=(count // PER_STEP,), in_specs=[SMEM, S...  39.9 us
    ppermute x8, starting transfers between devices, slab_along(): lax.ppermute(value, 'slab', [(source, source + steps) for source in range...  23 us
    ppermute x9, starting transfers between devices, core_swap(): return lax.ppermute(value, 'view', [(i, i ^ 1) for i in range(VIEWS)])  22.3 us
    ppermute x18, starting transfers between devices, z_along(): lax.ppermute(value, 'view', [(i, (i + 2 * steps) % VIEWS) for i in range(...  20.6 us
    pallas_call x2, Pallas kernels, project(): pl.pallas_call(project_kernel, grid_spec=pltpu.PrefetchScalarGridSpec(num...  10.7 us
    ppermute x18, waiting for transfers between devices, z_along(): lax.ppermute(value, 'view', [(i, (i + 2 * steps) % VIEWS) for i in range(...  9.49 us
    ppermute x4, starting transfers between devices, slab_swap(): lax.ppermute(value, 'slab', [(i, i ^ bit) for i in range(lax.axis_size('s...  7.88 us
    pallas_call x1, Pallas kernels, spread(): pl.pallas_call(spread_kernel, grid_spec=pltpu.PrefetchScalarGridSpec(num_...  6.27 us
  transfers between devices with their start and end apart: 39, of which 11 were waited for; matrix products, arithmetic and copies ran while one was open for 0% of the time, Pallas kernels for 8%

profile of v2, /device:TPU:1, one launch (start us, length us, event | category | flops | bytes accessed | tf_op | source)
XLA Modules:
  0.0 155.1 jit_solution(12698481812924233740)
XLA Ops:
  0.6 0.6 pad_add_fusion.place
  1.3 5.4 %shard_map.78 = f32[4,16,1024]{2,1,0:T(8,128)} custom-call(s32[3]{0:T(128)} %pad_add_fusion.place, f32[2,16,64,1024]{3,2,1,0:T(8,128)} %field_ref.5), custom_call_target="tpu_custom_call" | custom-call | flops 6291456 | bytes 4456448 | tf_op jit(solution)/shard_map/pallas_call | solution.py:75
  6.7 0.0 copy-start.3
  6.7 1.5 collective-permute-start
  8.2 5.4 %shard_map.77 = f32[4,16,1024]{2,1,0:T(8,128)} custom-call(s32[3]{0:T(128)} %pad_add_fusion.place, f32[2,16,64,1024]{3,2,1,0:T(8,128)} %field_ref.5), custom_call_target="tpu_custom_call" | custom-call | flops 6291456 | bytes 4456448 | tf_op jit(solution)/shard_map/pallas_call | solution.py:75
  13.6 1.0 add.63
  14.6 1.8 %collective-permute-start.1 = (f32[16,1024]{1,0:T(8,128)S(1)}, f32[16,1024]{1,0:T(8,128)S(1)}, u32[]{:S(2)}, u32[]{:S(2)}) collective-permute-start(f32[16,1024]{1,0:T(8,128)S(1)} %get-tuple-element.18), channel_id=1, source_target_pairs={{0,2},{1,3},{2,4},{3,5},{4,6},{5,7},{6,0},{7,1},{8,10},{9,11},{10,... | collective-permute-start | bytes 196616 | tf_op jit(solution)/shard_map/ppermute | solution.py:255
  16.4 2.2 %collective-permute-start.3 = (f32[16,1024]{1,0:T(8,128)S(1)}, f32[16,1024]{1,0:T(8,128)S(1)}, u32[]{:S(2)}, u32[]{:S(2)}) collective-permute-start(f32[16,1024]{1,0:T(8,128)S(1)} %get-tuple-element.19), channel_id=1, source_target_pairs={{0,6},{1,7},{2,0},{3,1},{4,2},{5,3},{6,4},{7,5},{8,14},{9,15},{10,... | collective-permute-start | bytes 196616 | tf_op jit(solution)/shard_map/ppermute | solution.py:255
  18.6 1.2 collective-permute-start.2
  19.8 1.0 collective-permute-done.1
  20.8 2.4 %collective-permute-done.2 = f32[16,1024]{1,0:T(8,128)S(1)} collective-permute-done((f32[16,1024]{1,0:T(8,128)S(1)}, f32[16,1024]{1,0:T(8,128)S(1)}, u32[]{:S(2)}, u32[]{:S(2)}) %collective-permute-start.2) | collective-permute-done | bytes 65568 | tf_op jit(solution)/shard_map/ppermute | solution.py:255
  23.2 1.5 collective-permute-start.6
  24.7 0.6 collective-permute-start.5
  25.3 0.1 collective-permute-start.4
  25.4 0.7 collective-permute-done.6
  26.1 2.9 %collective-permute-done.5 = bf16[16,1024]{1,0:T(8,128)(2,1)S(1)} collective-permute-done((bf16[16,1024]{1,0:T(8,128)(2,1)S(1)}, bf16[16,1024]{1,0:T(8,128)(2,1)S(1)}, u32[]{:S(2)}, u32[]{:S(2)}) %collective-permute-start.5) | collective-permute-done | bytes 32800 | tf_op jit(solution)/shard_map/ppermute | solution.py:255
  28.9 0.4 collective-permute-done.4
  29.3 1.3 collective-permute-start.10
  30.6 1.3 collective-permute-start.9
  31.9 1.3 collective-permute-start.8
  33.2 1.3 collective-permute-start.7
  34.5 0.1 copy.9
  34.6 0.1 pad_add_fusion.1
  34.7 3.3 %collective-permute-start.11 = (bf16[64,1024]{1,0:T(8,128)(2,1)S(1)}, bf16[64,1024]{1,0:T(8,128)(2,1)S(1)}, u32[]{:S(2)}, u32[]{:S(2)}) collective-permute-start(bf16[64,1024]{1,0:T(8,128)(2,1)S(1)} %pad_maximum_fusion.refs_0_), channel_id=1, source_target_pairs={{0,1},{1,0},{2,3},{3,2},{4,5},{5,4},{6,7},{7,6},{8,9},{9,8},{10,11... | collective-permute-start | bytes 393224 | tf_op jit(solution)/shard_map/ppermute | solution.py:259
  38.0 1.5 collective-permute-start.15
  39.5 2.5 %collective-permute-start.14 = (bf16[64,1024]{1,0:T(8,128)(2,1)S(1)}, bf16[64,1024]{1,0:T(8,128)(2,1)S(1)}, u32[]{:S(2)}, u32[]{:S(2)}) collective-permute-start(bf16[64,1024]{1,0:T(8,128)(2,1)S(1)} %collective-permute-done.9.refs_3_), channel_id=1, source_target_pairs={{0,1},{1,0},{2,3},{3,2},{4,5},{5,4},{6,7},{7,6},{8,9},{9,8},{10,11... | collective-permute-start | bytes 393224 | tf_op jit(solution)/shard_map/ppermute | solution.py:259
  42.0 1.6 %collective-permute-start.13 = (bf16[64,1024]{1,0:T(8,128)(2,1)S(1)}, bf16[64,1024]{1,0:T(8,128)(2,1)S(1)}, u32[]{:S(2)}, u32[]{:S(2)}) collective-permute-start(bf16[64,1024]{1,0:T(8,128)(2,1)S(1)} %collective-permute-done.8.refs_2_), channel_id=1, source_target_pairs={{0,1},{1,0},{2,3},{3,2},{4,5},{5,4},{6,7},{7,6},{8,9},{9,8},{10,11... | collective-permute-start | bytes 393224 | tf_op jit(solution)/shard_map/ppermute | solution.py:259
  43.6 0.0 collective-permute-start.12
  43.6 0.0 slice-start.1
  43.6 0.9 collective-permute-done.13.refs_7_
  44.6 0.4 collective-permute-done.12.refs_6_
  45.0 39.9 %shard_map.79 = (bf16[448,1024]{1,0:T(8,128)(2,1)S(1)}, bf16[448,1024]{1,0:T(8,128)(2,1)S(1)}) custom-call(s32[3]{0:T(128)S(1)} %copy-done, s32[32,2]{1,0:T(8,128)S(1)} %broadcast_subtract_fusion.off_ref, bf16[64,1024]{1,0:T(8,128)(2,1)S(1)} %pad_maximum_fusion.refs_0_, bf16[64,1024]{1,0:T(8,128)(2,1)S(1)} %collective-permute-done.7.refs_1_, ...), custom_call_target="tpu_custom_call" | custom-call | flops 17179869184 | bytes 16777216 | tf_op jit(solution)/shard_map/pallas_call | solution.py:228
  84.9 0.2 collective-permute-start.16
  85.1 2.4 %collective-permute-done.16 = bf16[448,1024]{1,0:T(8,128)(2,1)S(1)} collective-permute-done((bf16[448,1024]{1,0:T(8,128)(2,1)S(1)}, bf16[448,1024]{1,0:T(8,128)(2,1)S(1)}, u32[]{:S(2)}, u32[]{:S(2)}) %collective-permute-start.16) | collective-permute-done | bytes 917536 | tf_op jit(solution)/shard_map/ppermute | solution.py:259
  87.4 0.4 fusion.14
  87.9 0.1 collective-permute-start.28
  88.0 2.7 %collective-permute-start.30 = (f32[24,1024]{1,0:T(8,128)S(1)}, f32[24,1024]{1,0:T(8,128)S(1)}, u32[]{:S(2)}, u32[]{:S(2)}) collective-permute-start(f32[24,1024]{1,0:T(8,128)S(1)} %get-tuple-element.13), channel_id=1, source_target_pairs={{0,6},{1,7},{2,0},{3,1},{4,2},{5,3},{6,4},{7,5},{8,14},{9,15},{10,... | collective-permute-start | bytes 294920 | tf_op jit(solution)/shard_map/ppermute | solution.py:255
  90.7 0.2 collective-permute-start.29
  90.8 4.3 %collective-permute-start.17 = (bf16[64,1024]{1,0:T(8,128)(2,1)S(1)}, bf16[64,1024]{1,0:T(8,128)(2,1)S(1)}, u32[]{:S(2)}, u32[]{:S(2)}) collective-permute-start(bf16[64,1024]{1,0:T(8,128)(2,1)S(1)} %get-tuple-element.8), channel_id=1, source_target_pairs={{0,8},{8,16},{16,24},{24,32},{32,40},{40,48},{48,56},{56,64},{64,7... | collective-permute-start | bytes 393224 | tf_op jit(solution)/shard_map/ppermute | solution.py:247
  95.1 5.3 %collective-permute-start.20 = (bf16[64,1024]{1,0:T(8,128)(2,1)S(1)}, bf16[64,1024]{1,0:T(8,128)(2,1)S(1)}, u32[]{:S(2)}, u32[]{:S(2)}) collective-permute-start(bf16[64,1024]{1,0:T(8,128)(2,1)S(1)} %get-tuple-element.9), channel_id=1, source_target_pairs={{0,32},{8,40},{16,48},{24,56},{32,64},{40,72},{48,80},{56,88},{64,... | collective-permute-start | bytes 393224 | tf_op jit(solution)/shard_map/ppermute | solution.py:247
  100.4 5.9 %collective-permute-start.19 = (bf16[64,1024]{1,0:T(8,128)(2,1)S(1)}, bf16[64,1024]{1,0:T(8,128)(2,1)S(1)}, u32[]{:S(2)}, u32[]{:S(2)}) collective-permute-start(bf16[64,1024]{1,0:T(8,128)(2,1)S(1)} %get-tuple-element.10), channel_id=1, source_target_pairs={{0,24},{8,32},{16,40},{24,48},{32,56},{40,64},{48,72},{56,80},{64,... | collective-permute-start | bytes 393224 | tf_op jit(solution)/shard_map/ppermute | solution.py:247
  106.3 2.4 %collective-permute-start.18 = (bf16[64,1024]{1,0:T(8,128)(2,1)S(1)}, bf16[64,1024]{1,0:T(8,128)(2,1)S(1)}, u32[]{:S(2)}, u32[]{:S(2)}) collective-permute-start(bf16[64,1024]{1,0:T(8,128)(2,1)S(1)} %get-tuple-element.11), channel_id=1, source_target_pairs={{0,16},{8,24},{16,32},{24,40},{32,48},{40,56},{48,64},{56,72},{64,... | collective-permute-start | bytes 393224 | tf_op jit(solution)/shard_map/ppermute | solution.py:247
  108.8 3.6 %collective-permute-start.31 = (f32[24,1024]{1,0:T(8,128)S(1)}, f32[24,1024]{1,0:T(8,128)S(1)}, u32[]{:S(2)}, u32[]{:S(2)}) collective-permute-start(f32[24,1024]{1,0:T(8,128)S(1)} %fusion.5), channel_id=1, source_target_pairs={{0,8},{8,0},{16,24},{24,16},{32,40},{40,32},{48,56},{56,48},{64,72... | collective-permute-start | bytes 294920 | tf_op jit(solution)/shard_map/ppermute | solution.py:251
  112.4 3.1 %collective-permute-done.31 = f32[24,1024]{1,0:T(8,128)S(1)} collective-permute-done((f32[24,1024]{1,0:T(8,128)S(1)}, f32[24,1024]{1,0:T(8,128)S(1)}, u32[]{:S(2)}, u32[]{:S(2)}) %collective-permute-start.31) | collective-permute-done | bytes 98336 | tf_op jit(solution)/shard_map/ppermute | solution.py:251
  115.5 2.9 %collective-permute-start.32 = (f32[24,1024]{1,0:T(8,128)S(1)}, f32[24,1024]{1,0:T(8,128)S(1)}, u32[]{:S(2)}, u32[]{:S(2)}) collective-permute-start(f32[24,1024]{1,0:T(8,128)S(1)} %add.78), channel_id=1, source_target_pairs={{0,16},{8,24},{16,0},{24,8},{32,48},{40,56},{48,32},{56,40},{64,80... | collective-permute-start | bytes 294920 | tf_op jit(solution)/shard_map/ppermute | solution.py:251
  118.4 0.1 fusion.2
  118.5 2.1 %collective-permute-done.32 = f32[24,1024]{1,0:T(8,128)S(1)} collective-permute-done((f32[24,1024]{1,0:T(8,128)S(1)}, f32[24,1024]{1,0:T(8,128)S(1)}, u32[]{:S(2)}, u32[]{:S(2)}) %collective-permute-start.32) | collective-permute-done | bytes 98336 | tf_op jit(solution)/shard_map/ppermute | solution.py:251
  120.6 0.5 collective-permute-start.33
  121.1 0.6 collective-permute-start.21
  121.6 2.2 %collective-permute-start.23 = (f32[16,1024]{1,0:T(8,128)S(1)}, f32[16,1024]{1,0:T(8,128)S(1)}, u32[]{:S(2)}, u32[]{:S(2)}) collective-permute-start(f32[16,1024]{1,0:T(8,128)S(1)} %get-tuple-element.16), channel_id=1, source_target_pairs={{0,6},{1,7},{2,0},{3,1},{4,2},{5,3},{6,4},{7,5},{8,14},{9,15},{10,... | collective-permute-start | bytes 196616 | tf_op jit(solution)/shard_map/ppermute | solution.py:255
  123.8 1.5 collective-permute-start.22
  125.4 0.9 collective-permute-start.34
  126.3 2.1 %collective-permute-done.22 = f32[16,1024]{1,0:T(8,128)S(1)} collective-permute-done((f32[16,1024]{1,0:T(8,128)S(1)}, f32[16,1024]{1,0:T(8,128)S(1)}, u32[]{:S(2)}, u32[]{:S(2)}) %collective-permute-start.22) | collective-permute-done | bytes 65568 | tf_op jit(solution)/shard_map/ppermute | solution.py:255
  128.4 0.5 collective-permute-start.26
  129.0 1.2 collective-permute-start.25
  130.2 0.8 collective-permute-start.24
  131.0 2.0 %collective-permute-start.37 = (bf16[16,1024]{1,0:T(8,128)(2,1)S(1)}, bf16[16,1024]{1,0:T(8,128)(2,1)S(1)}, u32[]{:S(2)}, u32[]{:S(2)}) collective-permute-start(bf16[16,1024]{1,0:T(8,128)(2,1)S(1)} %fusion.6), channel_id=1, source_target_pairs={{0,6},{1,7},{2,0},{3,1},{4,2},{5,3},{6,4},{7,5},{8,14},{9,15},{10,... | collective-permute-start | bytes 98312 | tf_op jit(solution)/shard_map/ppermute | solution.py:255
  133.0 0.8 collective-permute-start.36
  133.8 0.8 collective-permute-start.35
  134.6 8.0 %collective-permute-start.27 = (bf16[64,1024]{1,0:T(8,128)(2,1)S(1)}, bf16[64,1024]{1,0:T(8,128)(2,1)S(1)}, u32[]{:S(2)}, u32[]{:S(2)}) collective-permute-start(bf16[64,1024]{1,0:T(8,128)(2,1)S(1)} %pad_maximum_fusion.1.mine_ref), channel_id=1, source_target_pairs={{0,1},{1,0},{2,3},{3,2},{4,5},{5,4},{6,7},{7,6},{8,9},{9,8},{10,11... | collective-permute-start | bytes 393224 | tf_op jit(solution)/shard_map/ppermute | solution.py:259
  142.6 3.8 %collective-permute-start.38 = (bf16[64,1024]{1,0:T(8,128)(2,1)S(1)}, bf16[64,1024]{1,0:T(8,128)(2,1)S(1)}, u32[]{:S(2)}, u32[]{:S(2)}) collective-permute-start(bf16[64,1024]{1,0:T(8,128)(2,1)S(1)} %pad_maximum_fusion.2.mine_ref), channel_id=1, source_target_pairs={{0,1},{1,0},{2,3},{3,2},{4,5},{5,4},{6,7},{7,6},{8,9},{9,8},{10,11... | collective-permute-start | bytes 393224 | tf_op jit(solution)/shard_map/ppermute | solution.py:259
  146.4 6.3 %shard_map.80 = f32[2,16,64,1024]{3,2,1,0:T(8,128)} custom-call(s32[3]{0:T(128)S(1)} %copy-done, bf16[64,1024]{1,0:T(8,128)(2,1)S(1)} %pad_maximum_fusion.1.mine_ref, bf16[64,1024]{1,0:T(8,128)(2,1)S(1)} %collective-permute-done.27.theirs_ref, f32[2,16,64,1024]{3,2,1,0:T(8,128)S(1)} %bitcast.38), custom_call_target="tpu_custom_call" | custom-call | flops 8388608 | bytes 16777216 | tf_op jit(solution)/shard_map/pallas_call | solution.py:105
  152.6 0.6 copy-done.5
  153.3 1.8 %shard_map.81 = f32[2,256,256]{2,1,0:T(8,128)} custom-call(s32[3]{0:T(128)} %pad_add_fusion.place, bf16[64,1024]{1,0:T(8,128)(2,1)} %copy-done.4, bf16[64,1024]{1,0:T(8,128)(2,1)} %copy-done.5), custom_call_target="tpu_custom_call" | custom-call | flops 1000 | bytes 1048576 | tf_op jit(solution)/shard_map/pallas_call | solution.py:128
  (62 shorter events, 0.4 us)
Async XLA Ops:
  6.7 27.9 %copy-start.6 = (s32[32,2]{0,1:T(2,128)S(1)}, s32[32,2]{0,1:T(2,128)}, u32[]{:S(2)}) copy-start(s32[32,2]{0,1:T(2,128)} %param.9) | copy-start | bytes 772
  6.7 38.3 %copy-start = (s32[3]{0:T(128)S(1)}, s32[3]{0:T(128)}, u32[]{:S(2)}) copy-start(s32[3]{0:T(128)} %pad_add_fusion.place) | copy-start | bytes 40
  6.7 38.3 %copy-start.1 = (f32[2,256,256]{2,1,0:T(8,128)S(1)}, f32[2,256,256]{2,1,0:T(8,128)}, u32[]{:S(2)}) copy-start(f32[2,256,256]{2,1,0:T(8,128)} %refs_10_.1) | copy-start | bytes 1572868
  6.7 38.3 %copy-start.2 = (bf16[512,512]{1,0:T(8,128)(2,1)S(1)}, bf16[512,512]{1,0:T(8,128)(2,1)}, u32[]{:S(2)}) copy-start(bf16[512,512]{1,0:T(8,128)(2,1)} %constant.44.clone.refs_12_) | copy-start | bytes 1572868
  6.7 38.3 %copy-start.3 = (bf16[512,512]{1,0:T(8,128)(2,1)S(1)}, bf16[512,512]{1,0:T(8,128)(2,1)}, u32[]{:S(2)}) copy-start(bf16[512,512]{1,0:T(8,128)(2,1)} %constant.43.clone.refs_11_) | copy-start | bytes 1572868
  6.7 6.9 %collective-permute-start = (f32[4,16,1024]{2,1,0:T(8,128)}, f32[4,16,1024]{2,1,0:T(8,128)S(1)}, u32[]{:S(2)}, u32[]{:S(2)}) collective-permute-start(f32[4,16,1024]{2,1,0:T(8,128)} %shard_map.78), channel_id=1, source_target_pairs={{0,1},{1,0},{2,3},{3,2},{4,5},{5,4},{6,7},{7,6},{8,9},{9,8},{10,11... | collective-permute-start | bytes 786440 | tf_op jit(solution)/shard_map/ppermute | solution.py:259
  14.6 6.2 %collective-permute-start.1 = (f32[16,1024]{1,0:T(8,128)S(1)}, f32[16,1024]{1,0:T(8,128)S(1)}, u32[]{:S(2)}, u32[]{:S(2)}) collective-permute-start(f32[16,1024]{1,0:T(8,128)S(1)} %get-tuple-element.18), channel_id=1, source_target_pairs={{0,2},{1,3},{2,4},{3,5},{4,6},{5,7},{6,0},{7,1},{8,10},{9,11},{10,... | collective-permute-start | bytes 196616 | tf_op jit(solution)/shard_map/ppermute | solution.py:255
  16.4 4.4 %collective-permute-start.3 = (f32[16,1024]{1,0:T(8,128)S(1)}, f32[16,1024]{1,0:T(8,128)S(1)}, u32[]{:S(2)}, u32[]{:S(2)}) collective-permute-start(f32[16,1024]{1,0:T(8,128)S(1)} %get-tuple-element.19), channel_id=1, source_target_pairs={{0,6},{1,7},{2,0},{3,1},{4,2},{5,3},{6,4},{7,5},{8,14},{9,15},{10,... | collective-permute-start | bytes 196616 | tf_op jit(solution)/shard_map/ppermute | solution.py:255
  18.6 4.6 %collective-permute-start.2 = (f32[16,1024]{1,0:T(8,128)S(1)}, f32[16,1024]{1,0:T(8,128)S(1)}, u32[]{:S(2)}, u32[]{:S(2)}) collective-permute-start(f32[16,1024]{1,0:T(8,128)S(1)} %get-tuple-element.20), channel_id=1, source_target_pairs={{0,4},{1,5},{2,6},{3,7},{4,0},{5,1},{6,2},{7,3},{8,12},{9,13},{10,... | collective-permute-start | bytes 196616 | tf_op jit(solution)/shard_map/ppermute | solution.py:255
  23.2 2.8 %collective-permute-start.6 = (bf16[16,1024]{1,0:T(8,128)(2,1)S(1)}, bf16[16,1024]{1,0:T(8,128)(2,1)S(1)}, u32[]{:S(2)}, u32[]{:S(2)}) collective-permute-start(bf16[16,1024]{1,0:T(8,128)(2,1)S(1)} %fusion.13), channel_id=1, source_target_pairs={{0,6},{1,7},{2,0},{3,1},{4,2},{5,3},{6,4},{7,5},{8,14},{9,15},{10,... | collective-permute-start | bytes 98312 | tf_op jit(solution)/shard_map/ppermute | solution.py:255
  24.7 4.3 %collective-permute-start.5 = (bf16[16,1024]{1,0:T(8,128)(2,1)S(1)}, bf16[16,1024]{1,0:T(8,128)(2,1)S(1)}, u32[]{:S(2)}, u32[]{:S(2)}) collective-permute-start(bf16[16,1024]{1,0:T(8,128)(2,1)S(1)} %fusion.13), channel_id=1, source_target_pairs={{0,4},{1,5},{2,6},{3,7},{4,0},{5,1},{6,2},{7,3},{8,12},{9,13},{10,... | collective-permute-start | bytes 98312 | tf_op jit(solution)/shard_map/ppermute | solution.py:255
  25.3 4.0 %collective-permute-start.4 = (bf16[16,1024]{1,0:T(8,128)(2,1)S(1)}, bf16[16,1024]{1,0:T(8,128)(2,1)S(1)}, u32[]{:S(2)}, u32[]{:S(2)}) collective-permute-start(bf16[16,1024]{1,0:T(8,128)(2,1)S(1)} %fusion.13), channel_id=1, source_target_pairs={{0,2},{1,3},{2,4},{3,5},{4,6},{5,7},{6,0},{7,1},{8,10},{9,11},{10,... | collective-permute-start | bytes 98312 | tf_op jit(solution)/shard_map/ppermute | solution.py:255
  29.3 8.7 %collective-permute-start.10 = (bf16[64,1024]{1,0:T(8,128)(2,1)S(1)}, bf16[64,1024]{1,0:T(8,128)(2,1)S(1)}, u32[]{:S(2)}, u32[]{:S(2)}) collective-permute-start(bf16[64,1024]{1,0:T(8,128)(2,1)S(1)} %pad_maximum_fusion.refs_0_), channel_id=1, source_target_pairs={{32,0},{40,8},{48,16},{56,24},{64,32},{72,40},{80,48},{88,56},{96,... | collective-permute-start | bytes 393224 | tf_op jit(solution)/shard_map/ppermute | solution.py:247
  30.6 8.9 %collective-permute-start.9 = (bf16[64,1024]{1,0:T(8,128)(2,1)S(1)}, bf16[64,1024]{1,0:T(8,128)(2,1)S(1)}, u32[]{:S(2)}, u32[]{:S(2)}) collective-permute-start(bf16[64,1024]{1,0:T(8,128)(2,1)S(1)} %pad_maximum_fusion.refs_0_), channel_id=1, source_target_pairs={{24,0},{32,8},{40,16},{48,24},{56,32},{64,40},{72,48},{80,56},{88,... | collective-permute-start | bytes 393224 | tf_op jit(solution)/shard_map/ppermute | solution.py:247
  31.9 10.1 %collective-permute-start.8 = (bf16[64,1024]{1,0:T(8,128)(2,1)S(1)}, bf16[64,1024]{1,0:T(8,128)(2,1)S(1)}, u32[]{:S(2)}, u32[]{:S(2)}) collective-permute-start(bf16[64,1024]{1,0:T(8,128)(2,1)S(1)} %pad_maximum_fusion.refs_0_), channel_id=1, source_target_pairs={{16,0},{24,8},{32,16},{40,24},{48,32},{56,40},{64,48},{72,56},{80,... | collective-permute-start | bytes 393224 | tf_op jit(solution)/shard_map/ppermute | solution.py:247
  33.2 10.4 %collective-permute-start.7 = (bf16[64,1024]{1,0:T(8,128)(2,1)S(1)}, bf16[64,1024]{1,0:T(8,128)(2,1)S(1)}, u32[]{:S(2)}, u32[]{:S(2)}) collective-permute-start(bf16[64,1024]{1,0:T(8,128)(2,1)S(1)} %pad_maximum_fusion.refs_0_), channel_id=1, source_target_pairs={{8,0},{16,8},{24,16},{32,24},{40,32},{48,40},{56,48},{64,56},{72,6... | collective-permute-start | bytes 393224 | tf_op jit(solution)/shard_map/ppermute | solution.py:247
  34.7 8.9 %collective-permute-start.11 = (bf16[64,1024]{1,0:T(8,128)(2,1)S(1)}, bf16[64,1024]{1,0:T(8,128)(2,1)S(1)}, u32[]{:S(2)}, u32[]{:S(2)}) collective-permute-start(bf16[64,1024]{1,0:T(8,128)(2,1)S(1)} %pad_maximum_fusion.refs_0_), channel_id=1, source_target_pairs={{0,1},{1,0},{2,3},{3,2},{4,5},{5,4},{6,7},{7,6},{8,9},{9,8},{10,11... | collective-permute-start | bytes 393224 | tf_op jit(solution)/shard_map/ppermute | solution.py:259
  38.0 5.6 %collective-permute-start.15 = (bf16[64,1024]{1,0:T(8,128)(2,1)S(1)}, bf16[64,1024]{1,0:T(8,128)(2,1)S(1)}, u32[]{:S(2)}, u32[]{:S(2)}) collective-permute-start(bf16[64,1024]{1,0:T(8,128)(2,1)S(1)} %collective-permute-done.10.refs_4_), channel_id=1, source_target_pairs={{0,1},{1,0},{2,3},{3,2},{4,5},{5,4},{6,7},{7,6},{8,9},{9,8},{10,11... | collective-permute-start | bytes 393224 | tf_op jit(solution)/shard_map/ppermute | solution.py:259
  39.5 4.2 %collective-permute-start.14 = (bf16[64,1024]{1,0:T(8,128)(2,1)S(1)}, bf16[64,1024]{1,0:T(8,128)(2,1)S(1)}, u32[]{:S(2)}, u32[]{:S(2)}) collective-permute-start(bf16[64,1024]{1,0:T(8,128)(2,1)S(1)} %collective-permute-done.9.refs_3_), channel_id=1, source_target_pairs={{0,1},{1,0},{2,3},{3,2},{4,5},{5,4},{6,7},{7,6},{8,9},{9,8},{10,11... | collective-permute-start | bytes 393224 | tf_op jit(solution)/shard_map/ppermute | solution.py:259
  42.0 2.6 %collective-permute-start.13 = (bf16[64,1024]{1,0:T(8,128)(2,1)S(1)}, bf16[64,1024]{1,0:T(8,128)(2,1)S(1)}, u32[]{:S(2)}, u32[]{:S(2)}) collective-permute-start(bf16[64,1024]{1,0:T(8,128)(2,1)S(1)} %collective-permute-done.8.refs_2_), channel_id=1, source_target_pairs={{0,1},{1,0},{2,3},{3,2},{4,5},{5,4},{6,7},{7,6},{8,9},{9,8},{10,11... | collective-permute-start | bytes 393224 | tf_op jit(solution)/shard_map/ppermute | solution.py:259
  43.6 1.3 collective-permute-start.12
  43.6 102.8 %slice-start = ((s8[8388608]{0:T(1024)(128)(4,1)}), s8[4194304]{0:T(1024)(128)(4,1)S(1)}, s32[]{:S(2)}) async-start(s8[8388608]{0:T(1024)(128)(4,1)} %bitcast.37), calls=%async_computation | async-start | bytes 8388608
  43.6 102.7 %slice-start.1 = ((s8[8388608]{0:T(1024)(128)(4,1)}), s8[4194304]{0:T(1024)(128)(4,1)S(1)}, s32[]{:S(2)}) async-start(s8[8388608]{0:T(1024)(128)(4,1)} %bitcast.37), calls=%async_computation.1 | async-start | bytes 8388608
  84.9 2.6 %collective-permute-start.16 = (bf16[448,1024]{1,0:T(8,128)(2,1)S(1)}, bf16[448,1024]{1,0:T(8,128)(2,1)S(1)}, u32[]{:S(2)}, u32[]{:S(2)}) collective-permute-start(bf16[448,1024]{1,0:T(8,128)(2,1)S(1)} %get-tuple-element.5), channel_id=1, source_target_pairs={{0,1},{1,0},{2,3},{3,2},{4,5},{5,4},{6,7},{7,6},{8,9},{9,8},{10,11... | collective-permute-start | bytes 2752520 | tf_op jit(solution)/shard_map/ppermute | solution.py:259
  87.9 12.5 %collective-permute-start.28 = (f32[24,1024]{1,0:T(8,128)S(1)}, f32[24,1024]{1,0:T(8,128)S(1)}, u32[]{:S(2)}, u32[]{:S(2)}) collective-permute-start(f32[24,1024]{1,0:T(8,128)S(1)} %get-tuple-element.12), channel_id=1, source_target_pairs={{0,2},{1,3},{2,4},{3,5},{4,6},{5,7},{6,0},{7,1},{8,10},{9,11},{10,... | collective-permute-start | bytes 294920 | tf_op jit(solution)/shard_map/ppermute | solution.py:255
  88.0 18.3 %collective-permute-start.30 = (f32[24,1024]{1,0:T(8,128)S(1)}, f32[24,1024]{1,0:T(8,128)S(1)}, u32[]{:S(2)}, u32[]{:S(2)}) collective-permute-start(f32[24,1024]{1,0:T(8,128)S(1)} %get-tuple-element.13), channel_id=1, source_target_pairs={{0,6},{1,7},{2,0},{3,1},{4,2},{5,3},{6,4},{7,5},{8,14},{9,15},{10,... | collective-permute-start | bytes 294920 | tf_op jit(solution)/shard_map/ppermute | solution.py:255
  90.7 18.1 %collective-permute-start.29 = (f32[24,1024]{1,0:T(8,128)S(1)}, f32[24,1024]{1,0:T(8,128)S(1)}, u32[]{:S(2)}, u32[]{:S(2)}) collective-permute-start(f32[24,1024]{1,0:T(8,128)S(1)} %get-tuple-element.14), channel_id=1, source_target_pairs={{0,4},{1,5},{2,6},{3,7},{4,0},{5,1},{6,2},{7,3},{8,12},{9,13},{10,... | collective-permute-start | bytes 294920 | tf_op jit(solution)/shard_map/ppermute | solution.py:255
  90.8 27.5 %collective-permute-start.17 = (bf16[64,1024]{1,0:T(8,128)(2,1)S(1)}, bf16[64,1024]{1,0:T(8,128)(2,1)S(1)}, u32[]{:S(2)}, u32[]{:S(2)}) collective-permute-start(bf16[64,1024]{1,0:T(8,128)(2,1)S(1)} %get-tuple-element.8), channel_id=1, source_target_pairs={{0,8},{8,16},{16,24},{24,32},{32,40},{40,48},{48,56},{56,64},{64,7... | collective-permute-start | bytes 393224 | tf_op jit(solution)/shard_map/ppermute | solution.py:247
  95.1 23.2 %collective-permute-start.20 = (bf16[64,1024]{1,0:T(8,128)(2,1)S(1)}, bf16[64,1024]{1,0:T(8,128)(2,1)S(1)}, u32[]{:S(2)}, u32[]{:S(2)}) collective-permute-start(bf16[64,1024]{1,0:T(8,128)(2,1)S(1)} %get-tuple-element.9), channel_id=1, source_target_pairs={{0,32},{8,40},{16,48},{24,56},{32,64},{40,72},{48,80},{56,88},{64,... | collective-permute-start | bytes 393224 | tf_op jit(solution)/shard_map/ppermute | solution.py:247
  100.4 18.0 %collective-permute-start.19 = (bf16[64,1024]{1,0:T(8,128)(2,1)S(1)}, bf16[64,1024]{1,0:T(8,128)(2,1)S(1)}, u32[]{:S(2)}, u32[]{:S(2)}) collective-permute-start(bf16[64,1024]{1,0:T(8,128)(2,1)S(1)} %get-tuple-element.10), channel_id=1, source_target_pairs={{0,24},{8,32},{16,40},{24,48},{32,56},{40,64},{48,72},{56,80},{64,... | collective-permute-start | bytes 393224 | tf_op jit(solution)/shard_map/ppermute | solution.py:247
  106.3 12.1 %collective-permute-start.18 = (bf16[64,1024]{1,0:T(8,128)(2,1)S(1)}, bf16[64,1024]{1,0:T(8,128)(2,1)S(1)}, u32[]{:S(2)}, u32[]{:S(2)}) collective-permute-start(bf16[64,1024]{1,0:T(8,128)(2,1)S(1)} %get-tuple-element.11), channel_id=1, source_target_pairs={{0,16},{8,24},{16,32},{24,40},{32,48},{40,56},{48,64},{56,72},{64,... | collective-permute-start | bytes 393224 | tf_op jit(solution)/shard_map/ppermute | solution.py:247
  108.8 6.7 %collective-permute-start.31 = (f32[24,1024]{1,0:T(8,128)S(1)}, f32[24,1024]{1,0:T(8,128)S(1)}, u32[]{:S(2)}, u32[]{:S(2)}) collective-permute-start(f32[24,1024]{1,0:T(8,128)S(1)} %fusion.5), channel_id=1, source_target_pairs={{0,8},{8,0},{16,24},{24,16},{32,40},{40,32},{48,56},{56,48},{64,72... | collective-permute-start | bytes 294920 | tf_op jit(solution)/shard_map/ppermute | solution.py:251
  115.5 5.1 %collective-permute-start.32 = (f32[24,1024]{1,0:T(8,128)S(1)}, f32[24,1024]{1,0:T(8,128)S(1)}, u32[]{:S(2)}, u32[]{:S(2)}) collective-permute-start(f32[24,1024]{1,0:T(8,128)S(1)} %add.78), channel_id=1, source_target_pairs={{0,16},{8,24},{16,0},{24,8},{32,48},{40,56},{48,32},{56,40},{64,80... | collective-permute-start | bytes 294920 | tf_op jit(solution)/shard_map/ppermute | solution.py:251
  120.6 4.8 %collective-permute-start.33 = (f32[24,1024]{1,0:T(8,128)S(1)}, f32[24,1024]{1,0:T(8,128)S(1)}, u32[]{:S(2)}, u32[]{:S(2)}) collective-permute-start(f32[24,1024]{1,0:T(8,128)S(1)} %add.79), channel_id=1, source_target_pairs={{0,32},{8,40},{16,48},{24,56},{32,0},{40,8},{48,16},{56,24},{64,96... | collective-permute-start | bytes 294920 | tf_op jit(solution)/shard_map/ppermute | solution.py:251
  121.1 5.2 %collective-permute-start.21 = (f32[16,1024]{1,0:T(8,128)S(1)}, f32[16,1024]{1,0:T(8,128)S(1)}, u32[]{:S(2)}, u32[]{:S(2)}) collective-permute-start(f32[16,1024]{1,0:T(8,128)S(1)} %get-tuple-element.15), channel_id=1, source_target_pairs={{0,2},{1,3},{2,4},{3,5},{4,6},{5,7},{6,0},{7,1},{8,10},{9,11},{10,... | collective-permute-start | bytes 196616 | tf_op jit(solution)/shard_map/ppermute | solution.py:255
  121.6 4.6 %collective-permute-start.23 = (f32[16,1024]{1,0:T(8,128)S(1)}, f32[16,1024]{1,0:T(8,128)S(1)}, u32[]{:S(2)}, u32[]{:S(2)}) collective-permute-start(f32[16,1024]{1,0:T(8,128)S(1)} %get-tuple-element.16), channel_id=1, source_target_pairs={{0,6},{1,7},{2,0},{3,1},{4,2},{5,3},{6,4},{7,5},{8,14},{9,15},{10,... | collective-permute-start | bytes 196616 | tf_op jit(solution)/shard_map/ppermute | solution.py:255
  123.8 4.6 %collective-permute-start.22 = (f32[16,1024]{1,0:T(8,128)S(1)}, f32[16,1024]{1,0:T(8,128)S(1)}, u32[]{:S(2)}, u32[]{:S(2)}) collective-permute-start(f32[16,1024]{1,0:T(8,128)S(1)} %get-tuple-element.17), channel_id=1, source_target_pairs={{0,4},{1,5},{2,6},{3,7},{4,0},{5,1},{6,2},{7,3},{8,12},{9,13},{10,... | collective-permute-start | bytes 196616 | tf_op jit(solution)/shard_map/ppermute | solution.py:255
  125.4 5.6 %collective-permute-start.34 = (f32[24,1024]{1,0:T(8,128)S(1)}, f32[24,1024]{1,0:T(8,128)S(1)}, u32[]{:S(2)}, u32[]{:S(2)}) collective-permute-start(f32[24,1024]{1,0:T(8,128)S(1)} %add.80), channel_id=1, source_target_pairs={{0,64},{8,72},{16,80},{24,88},{32,96},{40,104},{48,112},{56,120},{... | collective-permute-start | bytes 294920 | tf_op jit(solution)/shard_map/ppermute | solution.py:251
  128.4 5.3 %collective-permute-start.26 = (bf16[16,1024]{1,0:T(8,128)(2,1)S(1)}, bf16[16,1024]{1,0:T(8,128)(2,1)S(1)}, u32[]{:S(2)}, u32[]{:S(2)}) collective-permute-start(bf16[16,1024]{1,0:T(8,128)(2,1)S(1)} %fusion.9), channel_id=1, source_target_pairs={{0,6},{1,7},{2,0},{3,1},{4,2},{5,3},{6,4},{7,5},{8,14},{9,15},{10,... | collective-permute-start | bytes 98312 | tf_op jit(solution)/shard_map/ppermute | solution.py:255
  129.0 5.6 %collective-permute-start.25 = (bf16[16,1024]{1,0:T(8,128)(2,1)S(1)}, bf16[16,1024]{1,0:T(8,128)(2,1)S(1)}, u32[]{:S(2)}, u32[]{:S(2)}) collective-permute-start(bf16[16,1024]{1,0:T(8,128)(2,1)S(1)} %fusion.9), channel_id=1, source_target_pairs={{0,4},{1,5},{2,6},{3,7},{4,0},{5,1},{6,2},{7,3},{8,12},{9,13},{10,... | collective-permute-start | bytes 98312 | tf_op jit(solution)/shard_map/ppermute | solution.py:255
  130.2 4.4 %collective-permute-start.24 = (bf16[16,1024]{1,0:T(8,128)(2,1)S(1)}, bf16[16,1024]{1,0:T(8,128)(2,1)S(1)}, u32[]{:S(2)}, u32[]{:S(2)}) collective-permute-start(bf16[16,1024]{1,0:T(8,128)(2,1)S(1)} %fusion.9), channel_id=1, source_target_pairs={{0,2},{1,3},{2,4},{3,5},{4,6},{5,7},{6,0},{7,1},{8,10},{9,11},{10,... | collective-permute-start | bytes 98312 | tf_op jit(solution)/shard_map/ppermute | solution.py:255
  131.0 11.6 %collective-permute-start.37 = (bf16[16,1024]{1,0:T(8,128)(2,1)S(1)}, bf16[16,1024]{1,0:T(8,128)(2,1)S(1)}, u32[]{:S(2)}, u32[]{:S(2)}) collective-permute-start(bf16[16,1024]{1,0:T(8,128)(2,1)S(1)} %fusion.6), channel_id=1, source_target_pairs={{0,6},{1,7},{2,0},{3,1},{4,2},{5,3},{6,4},{7,5},{8,14},{9,15},{10,... | collective-permute-start | bytes 98312 | tf_op jit(solution)/shard_map/ppermute | solution.py:255
  133.0 9.6 %collective-permute-start.36 = (bf16[16,1024]{1,0:T(8,128)(2,1)S(1)}, bf16[16,1024]{1,0:T(8,128)(2,1)S(1)}, u32[]{:S(2)}, u32[]{:S(2)}) collective-permute-start(bf16[16,1024]{1,0:T(8,128)(2,1)S(1)} %fusion.6), channel_id=1, source_target_pairs={{0,4},{1,5},{2,6},{3,7},{4,0},{5,1},{6,2},{7,3},{8,12},{9,13},{10,... | collective-permute-start | bytes 98312 | tf_op jit(solution)/shard_map/ppermute | solution.py:255
  133.8 8.8 %collective-permute-start.35 = (bf16[16,1024]{1,0:T(8,128)(2,1)S(1)}, bf16[16,1024]{1,0:T(8,128)(2,1)S(1)}, u32[]{:S(2)}, u32[]{:S(2)}) collective-permute-start(bf16[16,1024]{1,0:T(8,128)(2,1)S(1)} %fusion.6), channel_id=1, source_target_pairs={{0,2},{1,3},{2,4},{3,5},{4,6},{5,7},{6,0},{7,1},{8,10},{9,11},{10,... | collective-permute-start | bytes 98312 | tf_op jit(solution)/shard_map/ppermute | solution.py:255
  134.6 11.8 %collective-permute-start.27 = (bf16[64,1024]{1,0:T(8,128)(2,1)S(1)}, bf16[64,1024]{1,0:T(8,128)(2,1)S(1)}, u32[]{:S(2)}, u32[]{:S(2)}) collective-permute-start(bf16[64,1024]{1,0:T(8,128)(2,1)S(1)} %pad_maximum_fusion.1.mine_ref), channel_id=1, source_target_pairs={{0,1},{1,0},{2,3},{3,2},{4,5},{5,4},{6,7},{7,6},{8,9},{9,8},{10,11... | collective-permute-start | bytes 393224 | tf_op jit(solution)/shard_map/ppermute | solution.py:259
  142.6 10.1 %copy-start.4 = (bf16[64,1024]{1,0:T(8,128)(2,1)}, bf16[64,1024]{1,0:T(8,128)(2,1)S(1)}, u32[]{:S(2)}) copy-start(bf16[64,1024]{1,0:T(8,128)(2,1)S(1)} %pad_maximum_fusion.2.mine_ref) | copy-start | bytes 393220
  142.6 10.1 %collective-permute-start.38 = (bf16[64,1024]{1,0:T(8,128)(2,1)S(1)}, bf16[64,1024]{1,0:T(8,128)(2,1)S(1)}, u32[]{:S(2)}, u32[]{:S(2)}) collective-permute-start(bf16[64,1024]{1,0:T(8,128)(2,1)S(1)} %pad_maximum_fusion.2.mine_ref), channel_id=1, source_target_pairs={{0,1},{1,0},{2,3},{3,2},{4,5},{5,4},{6,7},{7,6},{8,9},{9,8},{10,11... | collective-permute-start | bytes 393224 | tf_op jit(solution)/shard_map/ppermute | solution.py:259
  152.6 0.6 copy-start.5

commit v3 on v2

v3 whole, which is shorter than its diff:
```python
import functools
import math

import jax
import jax.numpy as jnp
import ml_dtypes
import numpy as np
from jax import lax
from jax.experimental import pallas as pl
from jax.experimental.pallas import tpu as pltpu
from jax.sharding import PartitionSpec as P

F32 = jnp.float32
BF16 = jnp.bfloat16
FRAME = 256
LANES = 128
SLAB = 64
VIEWS = 8
ROWS = SLAB // VIEWS
COLUMNS = 1024
TILES = COLUMNS // LANES
BLOCKS = 5
BAND = BLOCKS * SLAB
PER_STEP = 8
SUMS = BLOCKS * SLAB + 4 * 3 * ROWS
VMEM = pl.BlockSpec(memory_space=pltpu.VMEM)
SMEM = pl.BlockSpec(memory_space=pltpu.SMEM)


def dft_blocks(order):
    index = np.arange(order, dtype=np.int32)
    product = index[:, None] * index[None, :] % order
    angle = product.astype(np.float32) * np.float32(-2.0 * math.pi / order)
    factor = np.float32(1.0 / math.sqrt(order))
    c, s = np.cos(angle) * factor, np.sin(angle) * factor
    fore = np.block([[c, -s], [s, c]]).astype(ml_dtypes.bfloat16)
    back = np.block([[c, s], [-s, c]]).astype(ml_dtypes.bfloat16)
    return fore, back


def tiles_of(value):
    return [value[:, t * LANES : (t + 1) * LANES] for t in range(TILES)]


def to_right(tiles, steps):
    lane = lax.broadcasted_iota(jnp.int32, tiles[0].shape, 1)
    turned = [pltpu.roll(x, steps, 1) for x in tiles]
    return [jnp.where(lane >= steps, x, before) for x, before in zip(turned, [jnp.zeros_like(tiles[0])] + turned)]


def to_left(tiles, steps):
    lane = lax.broadcasted_iota(jnp.int32, tiles[0].shape, 1)
    turned = [pltpu.roll(x, (LANES - steps) % LANES, 1) for x in tiles]
    return [jnp.where(lane < LANES - steps, x, after) for x, after in zip(turned, turned[1:] + [jnp.zeros_like(tiles[0])])]


def chunk_at(place, half, e):
    return 4 * ((place[1] + half) % 2) + (place[0] + e) % 4


def rows_at(place, half, i):
    return pl.ds(pl.multiple_of((4 * ((place[1] + half) % 2) + i) * ROWS, ROWS), ROWS)


def project_kernel(half, place, field_ref, out_ref, held, sems):
    layers = field_ref.shape[1]
    copies = []
    for e in range(4):
        rows = pl.ds(pl.multiple_of(chunk_at(place, half, e) * ROWS, ROWS), ROWS)
        copies.append(pltpu.make_async_copy(field_ref.at[:, :, rows, :], held.at[e], sems.at[e]))
        copies[-1].start()
    for e in range(4):
        copies[e].wait()
        values = [tiles_of(jnp.concatenate([held[e, 0, k], held[e, 1, k]], 0)) for k in range(layers)]
        steps = 1
        while len(values) > 1:
            moved = [to_right(x, steps) for x in values[1::2]]
            values = [[a + b for a, b in zip(x, y)] for x, y in zip(values[0::2], moved)]
            steps *= 2
        for t, x in enumerate(to_right(values[0], place[2])):
            out_ref[e, :, t * LANES : (t + 1) * LANES] = x


def project(place, field, half):
    layers = field.shape[1]
    return pl.pallas_call(
        functools.partial(project_kernel, half),
        in_specs=[SMEM, pl.BlockSpec(memory_space=pl.ANY)],
        out_specs=VMEM,
        out_shape=jax.ShapeDtypeStruct((4, 2 * ROWS, COLUMNS), F32),
        scratch_shapes=[pltpu.VMEM((4, 2, layers, ROWS, COLUMNS), F32), pltpu.SemaphoreType.DMA((4,))],
        compiler_params=pltpu.CompilerParams(vmem_limit_bytes=60 << 20),
        cost_estimate=pl.CostEstimate(flops=layers * 4 * 16 * 1024 * 6, bytes_accessed=12 << 20, transcendentals=0),
    )(place, field)


def spread_kernel(place, mine_ref, theirs_ref, field_ref, out_ref, held, sems):
    layers = field_ref.shape[1]
    copies = []
    for half, ref in enumerate((mine_ref, theirs_ref)):
        for i in range(4):
            rows, slot = rows_at(place, half, i), half * 4 + i
            base = to_left(tiles_of(ref[i * 2 * ROWS : (i + 1) * 2 * ROWS, :].astype(F32)), place[2])
            for k in range(layers):
                for t, x in enumerate(to_left(base, k) if k else base):
                    columns = slice(t * LANES, (t + 1) * LANES)
                    for part in range(2):
                        held[slot, part, k, :, columns] = field_ref[part, k, rows, columns] + x[part * ROWS : (part + 1) * ROWS]
            copies.append(pltpu.make_async_copy(held.at[slot], out_ref.at[:, :, rows, :], sems.at[slot]))
            copies[-1].start()
    for copy in copies:
        copy.wait()


def spread(place, mine, theirs, field):
    layers = field.shape[1]
    return pl.pallas_call(
        spread_kernel,
        in_specs=[SMEM, VMEM, VMEM, VMEM],
        out_specs=pl.BlockSpec(memory_space=pl.ANY),
        out_shape=jax.ShapeDtypeStruct(field.shape, F32),
        scratch_shapes=[pltpu.VMEM((VIEWS, 2, layers, ROWS, COLUMNS), F32), pltpu.SemaphoreType.DMA((VIEWS,))],
        compiler_params=pltpu.CompilerParams(vmem_limit_bytes=40 << 20),
        cost_estimate=pl.CostEstimate(flops=layers * 8 * 16 * 1024 * 4, bytes_accessed=16 << 20, transcendentals=0),
    )(place, mine, theirs, field)


def join_kernel(place, mine_ref, theirs_ref, out_ref):
    for half, ref in enumerate((mine_ref, theirs_ref)):
        for j in range(4):
            first = chunk_at(place, half, 4 - j) * (FRAME // VIEWS)
            for part in range(2):
                x = ref[j * 2 * ROWS : (j + 1) * 2 * ROWS, :][part * ROWS : (part + 1) * ROWS]
                for g in range(4):
                    rows = pl.ds(pl.multiple_of(first + g * ROWS, ROWS), ROWS)
                    out_ref[part, rows, :] = x[:, g * FRAME : (g + 1) * FRAME].astype(F32)


def join(place, mine, theirs):
    return pl.pallas_call(
        join_kernel,
        in_specs=[SMEM, VMEM, VMEM],
        out_specs=VMEM,
        out_shape=jax.ShapeDtypeStruct((2, FRAME, FRAME), F32),
        cost_estimate=pl.CostEstimate(flops=1000, bytes_accessed=1 << 20, transcendentals=0),
    )(place, mine, theirs)


def dot(left, right):
    return jnp.dot(left, right, preferred_element_type=F32)


def visit_kernel(place, off_ref, *refs):
    bands, (theirs_band, probe_ref, fore_ref, back_ref, amp_ref, mine_ref, theirs_ref, band, upd, num) = refs[:BLOCKS], refs[BLOCKS:]
    step = pl.program_id(0)

    @pl.when(step == 0)
    def _():
        for i in range(2 * BLOCKS):
            half, block = i // BLOCKS, i % BLOCKS
            for j in range(4):
                first = (block * 4 * half + j) * 2 * ROWS
                x = (theirs_band if half else bands[block])[first : first + 2 * ROWS, :].astype(F32)
                first = pl.multiple_of(block * SLAB + chunk_at(place, half, 4 - j) * ROWS, ROWS)
                for part in range(2):
                    for t in range(TILES):
                        band[part, t, pl.ds(first, ROWS), :] = x[part * ROWS : (part + 1) * ROWS, t * LANES : (t + 1) * LANES]
        upd[...] = jnp.zeros_like(upd)
        num[...] = jnp.zeros_like(num)

    lane = lax.broadcasted_iota(jnp.int32, (FRAME, LANES), 1)

    def corner(j):
        p = step * PER_STEP + j
        r, c = off_ref[p, 0], off_ref[p, 1]
        q, m = c // LANES, c % LANES
        return r, (q, q + 1, jnp.minimum(q + 2, TILES - 1)), m

    def patch_of(part, r, q, m):
        turn = (LANES - m) % LANES
        tiles = [pltpu.roll(band[part, t, pl.ds(r, FRAME), :], turn, 1) for t in q]
        keep = lane < LANES - m
        return jnp.concatenate([jnp.where(keep, tiles[0], tiles[1]), jnp.where(keep, tiles[1], tiles[2])], 1)

    def add_to(part, value, r, q, m):
        left = pltpu.roll(value[:, :LANES], m, 1)
        right = pltpu.roll(value[:, LANES:], m, 1)
        keep = lane >= m
        terms = [jnp.where(keep, left, 0.0), jnp.where(keep, right, left), jnp.where(keep, 0.0, right)]
        for t, x in zip(q, terms):
            upd[part, t, pl.ds(r, FRAME), :] += x

    pr, pi = probe_ref[0], probe_ref[1]
    corners = [corner(j) for j in range(PER_STEP)]
    kept = [dict() for _ in range(PER_STEP)]

    def enter(j, at):
        r, q, m = corners[j]
        at["a"], at["b"] = a, b = patch_of(0, r, q, m), patch_of(1, r, q, m)
        at["er"], at["ei"] = pr * a - pi * b, pr * b + pi * a

    def rows_out(j, at):
        h = dot(fore_ref[...], jnp.concatenate([at["er"], at["ei"]], 0).astype(BF16))
        at["half"] = jnp.concatenate([h[:FRAME], h[FRAME:]], 1).astype(BF16)

    def columns_out(j, at):
        at["far"] = dot(at["half"], back_ref[...])

    def fix(j, at):
        fr, fi = at["far"][:, :FRAME], at["far"][:, FRAME:]
        factor = amp_ref[j] * lax.rsqrt(fr * fr + fi * fi + 0.25)
        at["fixed"] = jnp.concatenate([fr * factor, fi * factor], 1).astype(BF16)

    def columns_back(j, at):
        h = dot(at["fixed"], fore_ref[...])
        at["back"] = jnp.concatenate([h[:, :FRAME], h[:, FRAME:]], 0).astype(BF16)

    def rows_back(j, at):
        at["new"] = dot(back_ref[...], at["back"])

    def leave(j, at):
        a, b = at["a"], at["b"]
        dr, di = at["new"][:FRAME] - at["er"], at["new"][FRAME:] - at["ei"]
        r, q, m = corners[j]
        add_to(0, pr * dr + pi * di, r, q, m)
        add_to(1, pr * di - pi * dr, r, q, m)
        num[0] += a * dr + b * di
        num[1] += a * di - b * dr
        num[2] += a * a + b * b

    stages = (enter, rows_out, columns_out, fix, columns_back, rows_back, leave)
    for tick in range(2 * (PER_STEP - 1) + len(stages)):
        due = [(tick - 2 * j, j) for j in range(PER_STEP) if 0 <= tick - 2 * j < len(stages)]
        for k, j in due:
            stages[k](j, kept[j])

    @pl.when(step == pl.num_programs(0) - 1)
    def _():
        peak = jnp.max(pr * pr + pi * pi) + 1e-06
        scale = 0.5 / jnp.full((2 * ROWS, COLUMNS), peak, F32)
        for half, ref in enumerate((mine_ref, theirs_ref)):
            for i in range(4):
                for b in range(BLOCKS):
                    rows = pl.ds(pl.multiple_of(b * SLAB + (4 * ((place[1] + half) % 2) + i) * ROWS, ROWS), ROWS)
                    x = [jnp.concatenate([upd[part, t, rows, :] for t in range(TILES)], 1) for part in range(2)]
                    first = (b * 4 + i) * 2 * ROWS
                    ref[first : first + 2 * ROWS, :] = (jnp.concatenate(x, 0) * scale).astype(BF16)
            planes = []
            for e in range(4):
                for k in range(3):
                    first = chunk_at(place, half, e) * 4 * ROWS
                    rows = [pl.ds(pl.multiple_of(first + g * ROWS, ROWS), ROWS) for g in range(4)]
                    planes.append(jnp.concatenate([num[k, x, :] for x in rows], 1))
            ref[BLOCKS * SLAB : SUMS, :] = jnp.concatenate(planes, 0).astype(BF16)


def visit_all(place, corners, bands, others, probe, amplitude):
    count = amplitude.shape[0]
    fore, back = dft_blocks(FRAME)
    amp_spec = pl.BlockSpec((PER_STEP, FRAME, FRAME), lambda i: (i, 0, 0))
    return pl.pallas_call(
        visit_kernel,
        grid=(count // PER_STEP,),
        in_specs=[SMEM, SMEM] + [VMEM] * 9 + [amp_spec],
        out_specs=[VMEM] * 2,
        out_shape=[jax.ShapeDtypeStruct((SUMS, COLUMNS), BF16)] * 2,
        scratch_shapes=[
            pltpu.VMEM((2, TILES, BAND, LANES), F32),
            pltpu.VMEM((2, TILES, BAND, LANES), F32),
            pltpu.VMEM((3, FRAME, FRAME), F32),
        ],
        compiler_params=pltpu.CompilerParams(vmem_limit_bytes=48 << 20),
        cost_estimate=pl.CostEstimate(flops=count * 16 * 2 * FRAME**3, bytes_accessed=16 << 20, transcendentals=0),
    )(place, corners, *bands, others, probe, fore, back, amplitude)


def slab_along(value, steps):
    count = lax.axis_size("slab")
    first, last = (max(0, -steps), min(count, count - steps))
    return lax.ppermute(value, "slab", [(source, source + steps) for source in range(first, last)])


def slab_ring(value, axis, steps):
    moves = []
    for i in range(lax.axis_size("slab")):
        y, x = divmod(i, 4)
        moves.append((i, 4 * y + (x + steps) % 4 if axis == 0 else 4 * ((y + steps) % 4) + x))
    return lax.ppermute(value, "slab", moves)


def ring_sum(value, axis):
    one, two, three = (slab_ring(value, axis, k) for k in (1, 2, 3))
    return (value + two) + (one + three)


def z_along(value, steps):
    return lax.ppermute(value, "view", [(i, (i + 2 * steps) % VIEWS) for i in range(VIEWS)])


def core_swap(value):
    return lax.ppermute(value, "view", [(i, i ^ 1) for i in range(VIEWS)])


def z_sum(value):
    return value[0] + z_along(value[1], 1) + z_along(value[2], 2) + z_along(value[3], 3)


def z_gather(value):
    return jnp.concatenate([value] + [z_along(value, d) for d in (1, 2, 3)], 0)


def on_device(object_field, probe, amplitude, offsets):
    layers = object_field.shape[1]
    view = lax.axis_index("view")
    place = jnp.stack([view // 2, view % 2, view * layers]).astype(jnp.int32)
    corners = offsets - jnp.stack([lax.axis_index("slab") * SLAB, 0]).astype(jnp.int32)

    received = core_swap(project(place, object_field, 1))
    piece = z_sum(project(place, object_field, 0) + received).astype(BF16)
    mine = z_gather(piece)
    bands = [mine] + [slab_along(mine, -k) for k in range(1, BLOCKS)]
    others = core_swap(jnp.concatenate(bands, 0))

    mine, theirs = visit_all(place, corners, bands, others, probe, amplitude)
    both = mine.astype(F32) + core_swap(theirs).astype(F32)
    update = both[:SLAB]
    for k in range(1, BLOCKS):
        update = update + slab_along(both[k * SLAB : (k + 1) * SLAB].astype(BF16), k).astype(F32)
    totals = z_sum(both[BLOCKS * SLAB :].reshape(4, 3 * ROWS, COLUMNS))
    update, totals = lax.optimization_barrier((update, totals))
    sent = update.astype(BF16)
    update = update + sum(z_along(sent, d).astype(F32) for d in (1, 2, 3))
    totals = ring_sum(totals, 0)
    update, totals = lax.optimization_barrier((update, totals))
    update_there = core_swap(update)
    totals = ring_sum(totals, 1)
    ratio = (totals[: 2 * ROWS].reshape(2, ROWS, COLUMNS) / totals[2 * ROWS :]).reshape(2 * ROWS, COLUMNS)
    update_there, ratio = lax.optimization_barrier((update_there, ratio))
    ratio = z_gather(ratio.astype(BF16))
    object_new = spread(place, update, update_there, object_field)
    object_new, ratio = lax.optimization_barrier((object_new, ratio))
    probe_step = join(place, ratio, core_swap(ratio))
    return object_new, probe_step


def solution(mesh):
    return jax.shard_map(
        on_device,
        mesh=mesh,
        in_specs=(P(None, "view", "slab", None), P(), P(("slab", "view"), None, None), P(("slab", "view"), None)),
        out_specs=(P(None, "view", "slab", None), P()),
        check_vma=False,
    )
```

time: 156 us -> 150 us (0.962)
  Pallas kernels: 58.8 us -> 51.1 us
  starting transfers between devices: 73.8 us -> 66.6 us
  local copies, waits for them, and re-layouts: 0.89 us -> 5.38 us
  waiting for transfers between devices: 18.3 us -> 22.3 us
    ppermute x9 -> x5, starting transfers between devices: 22.3 us -> 16.4 us  [core_swap(): return lax.ppermute(value, 'view', [(i, i ^ 1) for i in range(VIEWS)])]
    ppermute x18 -> x15, starting transfers between devices: 20.6 us -> 15.5 us  [z_along(): lax.ppermute(value, 'view', [(i, (i + 2 * steps) % VIEWS) for i in range(...]
    ppermute x8, waiting for transfers between devices: 0.02 us -> 4.42 us  [slab_along(): lax.ppermute(value, 'slab', [(source, source + steps) for source in range...]
    unnamed x19 -> x25, local copies, waits for them, and re-layouts: 0.77 us -> 4.64 us
    pallas_call x1, Pallas kernels: 39.9 us -> 36.1 us  [visit_all(): pl.pallas_call(visit_kernel, grid=(count // PER_STEP,), in_specs=[SMEM, S...]
    pallas_call x3, Pallas kernels: 17 us -> 13.2 us  [the longest x2 8.89 us: project(): pl.pallas_call(functools.partial(project_kernel, half), in_specs=[SMEM, p...]
    ppermute x4 -> x6, waiting for transfers between devices: 5.16 us -> 1.9 us  [slab_ring(): return lax.ppermute(value, 'slab', moves)]
    ppermute x4 -> x6, starting transfers between devices: 7.88 us -> 11.1 us  [slab_ring(): return lax.ppermute(value, 'slab', moves)]
  transfers between devices with their start and end apart: 39 -> 34, of which waited for: 11 -> 14; matrix products, arithmetic and copies ran while one was open for 0% -> 3% of each run, Pallas kernels for 8% -> 6%
where the time goes in v3:
time: 150 us; the launch traced here: 149 us
  starting transfers between devices  66.6 us (44%)
  Pallas kernels  51.1 us (34%)
  waiting for transfers between devices  22.3 us (15%)
  local copies, waits for them, and re-layouts  5.38 us (4%)
  other arithmetic  3.1 us (2%)
    pallas_call x1, Pallas kernels, visit_all(): pl.pallas_call(visit_kernel, grid=(count // PER_STEP,), in_specs=[SMEM, S...  36.1 us
    ppermute x8, starting transfers between devices, slab_along(): lax.ppermute(value, 'slab', [(source, source + steps) for source in range...  23.6 us
    ppermute x5, starting transfers between devices, core_swap(): return lax.ppermute(value, 'view', [(i, i ^ 1) for i in range(VIEWS)])  16.4 us
    ppermute x15, starting transfers between devices, z_along(): lax.ppermute(value, 'view', [(i, (i + 2 * steps) % VIEWS) for i in range(...  15.5 us
    ppermute x6, starting transfers between devices, slab_ring(): return lax.ppermute(value, 'slab', moves)  11.1 us
    ppermute x15, waiting for transfers between devices, z_along(): lax.ppermute(value, 'view', [(i, (i + 2 * steps) % VIEWS) for i in range(...  9.78 us
    pallas_call x2, Pallas kernels, project(): pl.pallas_call(functools.partial(project_kernel, half), in_specs=[SMEM, p...  8.89 us
    ppermute x5, waiting for transfers between devices, core_swap(): return lax.ppermute(value, 'view', [(i, i ^ 1) for i in range(VIEWS)])  6.2 us
  transfers between devices with their start and end apart: 34, of which 14 were waited for; matrix products, arithmetic and copies ran while one was open for 3% of the time, Pallas kernels for 6%

profile of v3, /device:TPU:1, one launch (start us, length us, event | category | flops | bytes accessed | tf_op | source)
XLA Modules:
  0.0 149.5 jit_solution(5215557211660863509)
XLA Ops:
  0.6 0.7 pad_add_fusion.place
  1.3 4.4 %shard_map.78 = f32[4,16,1024]{2,1,0:T(8,128)} custom-call(s32[3]{0:T(128)} %pad_add_fusion.place, f32[2,16,64,1024]{3,2,1,0:T(8,128)} %field_ref.5), custom_call_target="tpu_custom_call" | custom-call | flops 6291456 | bytes 12582912 | tf_op jit(solution)/shard_map/pallas_call | solution.py:86
  5.8 1.5 %collective-permute-start = (f32[4,16,1024]{2,1,0:T(8,128)}, f32[4,16,1024]{2,1,0:T(8,128)S(1)}, u32[]{:S(2)}, u32[]{:S(2)}) collective-permute-start(f32[4,16,1024]{2,1,0:T(8,128)} %shard_map.78), channel_id=1, source_target_pairs={{0,1},{1,0},{2,3},{3,2},{4,5},{5,4},{6,7},{7,6},{8,9},{9,8},{10,11... | collective-permute-start | bytes 786440 | tf_op jit(solution)/shard_map/ppermute | solution.py:301
  7.3 4.4 %shard_map.77 = f32[4,16,1024]{2,1,0:T(8,128)} custom-call(s32[3]{0:T(128)} %pad_add_fusion.place, f32[2,16,64,1024]{3,2,1,0:T(8,128)} %field_ref.5), custom_call_target="tpu_custom_call" | custom-call | flops 6291456 | bytes 12582912 | tf_op jit(solution)/shard_map/pallas_call | solution.py:86
  11.8 1.1 add.69
  12.9 1.8 %collective-permute-start.1 = (f32[16,1024]{1,0:T(8,128)S(1)}, f32[16,1024]{1,0:T(8,128)S(1)}, u32[]{:S(2)}, u32[]{:S(2)}) collective-permute-start(f32[16,1024]{1,0:T(8,128)S(1)} %get-tuple-element.33), channel_id=1, source_target_pairs={{0,2},{1,3},{2,4},{3,5},{4,6},{5,7},{6,0},{7,1},{8,10},{9,11},{10,... | collective-permute-start | bytes 196616 | tf_op jit(solution)/shard_map/ppermute | solution.py:297
  14.7 2.2 %collective-permute-start.3 = (f32[16,1024]{1,0:T(8,128)S(1)}, f32[16,1024]{1,0:T(8,128)S(1)}, u32[]{:S(2)}, u32[]{:S(2)}) collective-permute-start(f32[16,1024]{1,0:T(8,128)S(1)} %get-tuple-element.34), channel_id=1, source_target_pairs={{0,6},{1,7},{2,0},{3,1},{4,2},{5,3},{6,4},{7,5},{8,14},{9,15},{10,... | collective-permute-start | bytes 196616 | tf_op jit(solution)/shard_map/ppermute | solution.py:297
  16.9 1.2 collective-permute-start.2
  18.1 1.1 collective-permute-done.1
  19.3 2.2 %collective-permute-done.2 = f32[16,1024]{1,0:T(8,128)S(1)} collective-permute-done((f32[16,1024]{1,0:T(8,128)S(1)}, f32[16,1024]{1,0:T(8,128)S(1)}, u32[]{:S(2)}, u32[]{:S(2)}) %collective-permute-start.2) | collective-permute-done | bytes 65568 | tf_op jit(solution)/shard_map/ppermute | solution.py:297
  21.5 0.6 constant_dynamic-update-slice_fusion.7
  22.2 1.4 collective-permute-start.6
  23.5 0.8 collective-permute-start.5
  24.3 0.6 collective-permute-done.6
  24.9 2.9 %collective-permute-done.5 = bf16[16,1024]{1,0:T(8,128)(2,1)S(1)} collective-permute-done((bf16[16,1024]{1,0:T(8,128)(2,1)S(1)}, bf16[16,1024]{1,0:T(8,128)(2,1)S(1)}, u32[]{:S(2)}, u32[]{:S(2)}) %collective-permute-start.5) | collective-permute-done | bytes 32800 | tf_op jit(solution)/shard_map/ppermute | solution.py:297
  27.8 0.5 collective-permute-done.4
  28.3 1.3 collective-permute-start.10
  29.6 1.3 collective-permute-start.9
  30.9 1.3 collective-permute-start.8
  32.2 1.3 collective-permute-start.7
  33.5 0.6 constant_dynamic-update-slice_fusion.6
  34.1 0.6 constant_dynamic-update-slice_fusion.5
  34.8 0.6 constant_dynamic-update-slice_fusion.4
  35.4 2.6 %collective-permute-done.7.refs_1_ = bf16[64,1024]{1,0:T(8,128)(2,1)S(1)} collective-permute-done((bf16[64,1024]{1,0:T(8,128)(2,1)S(1)}, bf16[64,1024]{1,0:T(8,128)(2,1)S(1)}, u32[]{:S(2)}, u32[]{:S(2)}) %collective-permute-start.7) | collective-permute-done | bytes 131104 | tf_op jit(solution)/shard_map/ppermute | solution.py:280
  37.9 0.7 constant_dynamic-update-slice_fusion.3
  38.6 0.7 constant_dynamic-update-slice_fusion.2
  39.3 0.7 constant_dynamic-update-slice_fusion.1
  39.9 0.7 constant_dynamic-update-slice_fusion
  40.6 4.3 %collective-permute-start.11 = (bf16[320,1024]{1,0:T(8,128)(2,1)}, bf16[320,1024]{1,0:T(8,128)(2,1)S(1)}, u32[]{:S(2)}, u32[]{:S(2)}) collective-permute-start(bf16[320,1024]{1,0:T(8,128)(2,1)} %constant_dynamic-update-slice_fusion), channel_id=1, source_target_pairs={{0,1},{1,0},{2,3},{3,2},{4,5},{5,4},{6,7},{7,6},{8,9},{9,8},{10,11... | collective-permute-start | bytes 1966088 | tf_op jit(solution)/shard_map/ppermute | solution.py:301
  44.9 0.1 copy.9
  45.0 1.8 %collective-permute-done.11.refs_5_ = bf16[320,1024]{1,0:T(8,128)(2,1)S(1)} collective-permute-done((bf16[320,1024]{1,0:T(8,128)(2,1)}, bf16[320,1024]{1,0:T(8,128)(2,1)S(1)}, u32[]{:S(2)}, u32[]{:S(2)}) %collective-permute-start.11) | collective-permute-done | bytes 655392 | tf_op jit(solution)/shard_map/ppermute | solution.py:301
  46.8 36.1 %shard_map.79 = (bf16[416,1024]{1,0:T(8,128)(2,1)S(1)}, bf16[416,1024]{1,0:T(8,128)(2,1)S(1)}) custom-call(s32[3]{0:T(128)S(1)} %copy-done, s32[32,2]{1,0:T(8,128)S(1)} %broadcast_subtract_fusion.off_ref, bf16[64,1024]{1,0:T(8,128)(2,1)S(1)} %pad_maximum_fusion.refs_0_, bf16[64,1024]{1,0:T(8,128)(2,1)S(1)} %collective-permute-done.7.refs_1_, ...), custom_call_target="tpu_custom_call" | custom-call | flops 17179869184 | bytes 16777216 | tf_op jit(solution)/shard_map/pallas_call | solution.py:261
  82.9 0.1 collective-permute-start.12
  83.0 2.4 %collective-permute-done.12 = bf16[416,1024]{1,0:T(8,128)(2,1)S(1)} collective-permute-done((bf16[416,1024]{1,0:T(8,128)(2,1)S(1)}, bf16[416,1024]{1,0:T(8,128)(2,1)S(1)}, u32[]{:S(2)}, u32[]{:S(2)}) %collective-permute-start.12) | collective-permute-done | bytes 852000 | tf_op jit(solution)/shard_map/ppermute | solution.py:301
  85.4 0.3 fusion.9
  85.8 0.1 collective-permute-start.17
  85.8 1.7 %collective-permute-start.18 = (f32[24,1024]{1,0:T(8,128)S(1)}, f32[24,1024]{1,0:T(8,128)S(1)}, u32[]{:S(2)}, u32[]{:S(2)}) collective-permute-start(f32[24,1024]{1,0:T(8,128)S(1)} %get-tuple-element.25), channel_id=1, source_target_pairs={{0,4},{1,5},{2,6},{3,7},{4,0},{5,1},{6,2},{7,3},{8,12},{9,13},{10,... | collective-permute-start | bytes 294920 | tf_op jit(solution)/shard_map/ppermute | solution.py:297
  87.5 1.6 %collective-permute-start.19 = (f32[24,1024]{1,0:T(8,128)S(1)}, f32[24,1024]{1,0:T(8,128)S(1)}, u32[]{:S(2)}, u32[]{:S(2)}) collective-permute-start(f32[24,1024]{1,0:T(8,128)S(1)} %get-tuple-element.26), channel_id=1, source_target_pairs={{0,6},{1,7},{2,0},{3,1},{4,2},{5,3},{6,4},{7,5},{8,14},{9,15},{10,... | collective-permute-start | bytes 294920 | tf_op jit(solution)/shard_map/ppermute | solution.py:297
  89.2 4.5 %collective-permute-start.13 = (bf16[64,1024]{1,0:T(8,128)(2,1)S(1)}, bf16[64,1024]{1,0:T(8,128)(2,1)S(1)}, u32[]{:S(2)}, u32[]{:S(2)}) collective-permute-start(bf16[64,1024]{1,0:T(8,128)(2,1)S(1)} %get-tuple-element.29), channel_id=1, source_target_pairs={{0,8},{8,16},{16,24},{24,32},{32,40},{40,48},{48,56},{56,64},{64,7... | collective-permute-start | bytes 393224 | tf_op jit(solution)/shard_map/ppermute | solution.py:280
  93.7 5.6 %collective-permute-start.16 = (bf16[64,1024]{1,0:T(8,128)(2,1)S(1)}, bf16[64,1024]{1,0:T(8,128)(2,1)S(1)}, u32[]{:S(2)}, u32[]{:S(2)}) collective-permute-start(bf16[64,1024]{1,0:T(8,128)(2,1)S(1)} %get-tuple-element.30), channel_id=1, source_target_pairs={{0,32},{8,40},{16,48},{24,56},{32,64},{40,72},{48,80},{56,88},{64,... | collective-permute-start | bytes 393224 | tf_op jit(solution)/shard_map/ppermute | solution.py:280
  99.4 5.9 %collective-permute-start.15 = (bf16[64,1024]{1,0:T(8,128)(2,1)S(1)}, bf16[64,1024]{1,0:T(8,128)(2,1)S(1)}, u32[]{:S(2)}, u32[]{:S(2)}) collective-permute-start(bf16[64,1024]{1,0:T(8,128)(2,1)S(1)} %get-tuple-element.31), channel_id=1, source_target_pairs={{0,24},{8,32},{16,40},{24,48},{32,56},{40,64},{48,72},{56,80},{64,... | collective-permute-start | bytes 393224 | tf_op jit(solution)/shard_map/ppermute | solution.py:280
  105.2 2.3 %collective-permute-start.14 = (bf16[64,1024]{1,0:T(8,128)(2,1)S(1)}, bf16[64,1024]{1,0:T(8,128)(2,1)S(1)}, u32[]{:S(2)}, u32[]{:S(2)}) collective-permute-start(bf16[64,1024]{1,0:T(8,128)(2,1)S(1)} %get-tuple-element.32), channel_id=1, source_target_pairs={{0,16},{8,24},{16,32},{24,40},{32,48},{40,56},{48,64},{56,72},{64,... | collective-permute-start | bytes 393224 | tf_op jit(solution)/shard_map/ppermute | solution.py:280
  107.7 1.8 %collective-permute-done.14 = bf16[64,1024]{1,0:T(8,128)(2,1)S(1)} collective-permute-done((bf16[64,1024]{1,0:T(8,128)(2,1)S(1)}, bf16[64,1024]{1,0:T(8,128)(2,1)S(1)}, u32[]{:S(2)}, u32[]{:S(2)}) %collective-permute-start.14) | collective-permute-done | bytes 131104 | tf_op jit(solution)/shard_map/ppermute | solution.py:280
  109.5 0.1 fusion.2
  109.6 6.0 %collective-permute-start.25 = (f32[24,1024]{1,0:T(8,128)S(1)}, f32[24,1024]{1,0:T(8,128)S(1)}, u32[]{:S(2)}, u32[]{:S(2)}) collective-permute-start(f32[24,1024]{1,0:T(8,128)S(1)} %fusion.4), channel_id=1, source_target_pairs={{0,24},{8,0},{16,8},{24,16},{32,56},{40,32},{48,40},{56,48},{64,88... | collective-permute-start | bytes 294920 | tf_op jit(solution)/shard_map/ppermute | solution.py:288
  115.6 1.3 collective-permute-start.23
  116.9 0.1 collective-permute-start.22
  117.0 1.7 %collective-permute-start.21 = (bf16[64,1024]{1,0:T(8,128)(2,1)S(1)}, bf16[64,1024]{1,0:T(8,128)(2,1)S(1)}, u32[]{:S(2)}, u32[]{:S(2)}) collective-permute-start(bf16[64,1024]{1,0:T(8,128)(2,1)S(1)} %convert_element_type.47), channel_id=1, source_target_pairs={{0,4},{1,5},{2,6},{3,7},{4,0},{5,1},{6,2},{7,3},{8,12},{9,13},{10,... | collective-permute-start | bytes 393224 | tf_op jit(solution)/shard_map/ppermute | solution.py:297
  118.7 0.8 collective-permute-start.20
  119.5 1.9 %collective-permute-done.24 = f32[24,1024]{1,0:T(8,128)S(1)} collective-permute-done((f32[24,1024]{1,0:T(8,128)S(1)}, f32[24,1024]{1,0:T(8,128)S(1)}, u32[]{:S(2)}, u32[]{:S(2)}) %collective-permute-start.24) | collective-permute-done | bytes 98336 | tf_op jit(solution)/shard_map/ppermute | solution.py:288
  121.4 1.0 collective-permute-done.21
  122.4 1.4 collective-permute-done.20
  123.9 2.4 %collective-permute-start.29 = (f32[24,1024]{1,0:T(8,128)S(1)}, f32[24,1024]{1,0:T(8,128)S(1)}, u32[]{:S(2)}, u32[]{:S(2)}) collective-permute-start(f32[24,1024]{1,0:T(8,128)S(1)} %add_add_fusion.2), channel_id=1, source_target_pairs={{0,96},{8,104},{16,112},{24,120},{32,0},{40,8},{48,16},{56,24},{64... | collective-permute-start | bytes 294920 | tf_op jit(solution)/shard_map/ppermute | solution.py:288
  126.3 1.4 collective-permute-start.27
  127.7 4.5 %collective-permute-start.26 = (f32[64,1024]{1,0:T(8,128)S(1)}, f32[64,1024]{1,0:T(8,128)S(1)}, u32[]{:S(2)}, u32[]{:S(2)}) collective-permute-start(f32[64,1024]{1,0:T(8,128)S(1)} %add_add_fusion.mine_ref), channel_id=1, source_target_pairs={{0,1},{1,0},{2,3},{3,2},{4,5},{5,4},{6,7},{7,6},{8,9},{9,8},{10,11... | collective-permute-start | bytes 786440 | tf_op jit(solution)/shard_map/ppermute | solution.py:301
  132.3 1.1 collective-permute-done.26.theirs_ref
  133.4 1.0 collective-permute-start.32
  134.4 0.7 collective-permute-start.31
  135.0 0.6 collective-permute-start.30
  135.6 4.3 %shard_map.80 = f32[2,16,64,1024]{3,2,1,0:T(8,128)} custom-call(s32[3]{0:T(128)S(1)} %copy-done, f32[64,1024]{1,0:T(8,128)S(1)} %add_add_fusion.mine_ref, f32[64,1024]{1,0:T(8,128)S(1)} %collective-permute-done.26.theirs_ref, f32[2,16,64,1024]{3,2,1,0:T(8,128)S(1)} %bitcast.24), custom_call_target="tpu_custom_call" | custom-call | flops 8388608 | bytes 16777216 | tf_op jit(solution)/shard_map/pallas_call | solution.py:117
  140.0 6.0 %collective-permute-start.33 = (bf16[64,1024]{1,0:T(8,128)(2,1)S(1)}, bf16[64,1024]{1,0:T(8,128)(2,1)S(1)}, u32[]{:S(2)}, u32[]{:S(2)}) collective-permute-start(bf16[64,1024]{1,0:T(8,128)(2,1)S(1)} %pad_maximum_fusion.1.mine_ref), channel_id=1, source_target_pairs={{0,1},{1,0},{2,3},{3,2},{4,5},{5,4},{6,7},{7,6},{8,9},{9,8},{10,11... | collective-permute-start | bytes 393224 | tf_op jit(solution)/shard_map/ppermute | solution.py:301
  146.0 1.0 collective-permute-done.33.theirs_ref
  147.0 0.7 copy-done.5
  147.7 1.8 %shard_map.81 = f32[2,256,256]{2,1,0:T(8,128)} custom-call(s32[3]{0:T(128)} %pad_add_fusion.place, bf16[64,1024]{1,0:T(8,128)(2,1)} %copy-done.4, bf16[64,1024]{1,0:T(8,128)(2,1)} %copy-done.5), custom_call_target="tpu_custom_call" | custom-call | flops 1000 | bytes 1048576 | tf_op jit(solution)/shard_map/pallas_call | solution.py:140
  (55 shorter events, 0.5 us)
Async XLA Ops:
  5.8 6.0 %collective-permute-start = (f32[4,16,1024]{2,1,0:T(8,128)}, f32[4,16,1024]{2,1,0:T(8,128)S(1)}, u32[]{:S(2)}, u32[]{:S(2)}) collective-permute-start(f32[4,16,1024]{2,1,0:T(8,128)} %shard_map.78), channel_id=1, source_target_pairs={{0,1},{1,0},{2,3},{3,2},{4,5},{5,4},{6,7},{7,6},{8,9},{9,8},{10,11... | collective-permute-start | bytes 786440 | tf_op jit(solution)/shard_map/ppermute | solution.py:301
  11.7 33.2 %copy-start.6 = (s32[32,2]{0,1:T(2,128)S(1)}, s32[32,2]{0,1:T(2,128)}, u32[]{:S(2)}) copy-start(s32[32,2]{0,1:T(2,128)} %param.9) | copy-start | bytes 772
  11.7 35.1 %copy-start = (s32[3]{0:T(128)S(1)}, s32[3]{0:T(128)}, u32[]{:S(2)}) copy-start(s32[3]{0:T(128)} %pad_add_fusion.place) | copy-start | bytes 40
  11.7 35.1 %copy-start.1 = (f32[2,256,256]{2,1,0:T(8,128)S(1)}, f32[2,256,256]{2,1,0:T(8,128)}, u32[]{:S(2)}) copy-start(f32[2,256,256]{2,1,0:T(8,128)} %refs_6_.1) | copy-start | bytes 1572868
  11.7 35.1 %copy-start.2 = (bf16[512,512]{1,0:T(8,128)(2,1)S(1)}, bf16[512,512]{1,0:T(8,128)(2,1)}, u32[]{:S(2)}) copy-start(bf16[512,512]{1,0:T(8,128)(2,1)} %constant.44.clone.refs_8_) | copy-start | bytes 1572868
  11.8 35.1 %copy-start.3 = (bf16[512,512]{1,0:T(8,128)(2,1)S(1)}, bf16[512,512]{1,0:T(8,128)(2,1)}, u32[]{:S(2)}) copy-start(bf16[512,512]{1,0:T(8,128)(2,1)} %constant.43.clone.refs_7_) | copy-start | bytes 1572868
  12.9 6.4 %collective-permute-start.1 = (f32[16,1024]{1,0:T(8,128)S(1)}, f32[16,1024]{1,0:T(8,128)S(1)}, u32[]{:S(2)}, u32[]{:S(2)}) collective-permute-start(f32[16,1024]{1,0:T(8,128)S(1)} %get-tuple-element.33), channel_id=1, source_target_pairs={{0,2},{1,3},{2,4},{3,5},{4,6},{5,7},{6,0},{7,1},{8,10},{9,11},{10,... | collective-permute-start | bytes 196616 | tf_op jit(solution)/shard_map/ppermute | solution.py:297
  14.7 4.6 %collective-permute-start.3 = (f32[16,1024]{1,0:T(8,128)S(1)}, f32[16,1024]{1,0:T(8,128)S(1)}, u32[]{:S(2)}, u32[]{:S(2)}) collective-permute-start(f32[16,1024]{1,0:T(8,128)S(1)} %get-tuple-element.34), channel_id=1, source_target_pairs={{0,6},{1,7},{2,0},{3,1},{4,2},{5,3},{6,4},{7,5},{8,14},{9,15},{10,... | collective-permute-start | bytes 196616 | tf_op jit(solution)/shard_map/ppermute | solution.py:297
  16.9 4.6 %collective-permute-start.2 = (f32[16,1024]{1,0:T(8,128)S(1)}, f32[16,1024]{1,0:T(8,128)S(1)}, u32[]{:S(2)}, u32[]{:S(2)}) collective-permute-start(f32[16,1024]{1,0:T(8,128)S(1)} %get-tuple-element.35), channel_id=1, source_target_pairs={{0,4},{1,5},{2,6},{3,7},{4,0},{5,1},{6,2},{7,3},{8,12},{9,13},{10,... | collective-permute-start | bytes 196616 | tf_op jit(solution)/shard_map/ppermute | solution.py:297
  22.2 2.8 %collective-permute-start.6 = (bf16[16,1024]{1,0:T(8,128)(2,1)S(1)}, bf16[16,1024]{1,0:T(8,128)(2,1)S(1)}, u32[]{:S(2)}, u32[]{:S(2)}) collective-permute-start(bf16[16,1024]{1,0:T(8,128)(2,1)S(1)} %get-tuple-element.23), channel_id=1, source_target_pairs={{0,6},{1,7},{2,0},{3,1},{4,2},{5,3},{6,4},{7,5},{8,14},{9,15},{10,... | collective-permute-start | bytes 98312 | tf_op jit(solution)/shard_map/ppermute | solution.py:297
  23.5 4.3 %collective-permute-start.5 = (bf16[16,1024]{1,0:T(8,128)(2,1)S(1)}, bf16[16,1024]{1,0:T(8,128)(2,1)S(1)}, u32[]{:S(2)}, u32[]{:S(2)}) collective-permute-start(bf16[16,1024]{1,0:T(8,128)(2,1)S(1)} %get-tuple-element.23), channel_id=1, source_target_pairs={{0,4},{1,5},{2,6},{3,7},{4,0},{5,1},{6,2},{7,3},{8,12},{9,13},{10,... | collective-permute-start | bytes 98312 | tf_op jit(solution)/shard_map/ppermute | solution.py:297
  24.3 4.0 %collective-permute-start.4 = (bf16[16,1024]{1,0:T(8,128)(2,1)S(1)}, bf16[16,1024]{1,0:T(8,128)(2,1)S(1)}, u32[]{:S(2)}, u32[]{:S(2)}) collective-permute-start(bf16[16,1024]{1,0:T(8,128)(2,1)S(1)} %get-tuple-element.23), channel_id=1, source_target_pairs={{0,2},{1,3},{2,4},{3,5},{4,6},{5,7},{6,0},{7,1},{8,10},{9,11},{10,... | collective-permute-start | bytes 98312 | tf_op jit(solution)/shard_map/ppermute | solution.py:297
  28.3 11.6 %collective-permute-start.10 = (bf16[64,1024]{1,0:T(8,128)(2,1)S(1)}, bf16[64,1024]{1,0:T(8,128)(2,1)S(1)}, u32[]{:S(2)}, u32[]{:S(2)}) collective-permute-start(bf16[64,1024]{1,0:T(8,128)(2,1)S(1)} %pad_maximum_fusion.refs_0_), channel_id=1, source_target_pairs={{32,0},{40,8},{48,16},{56,24},{64,32},{72,40},{80,48},{88,56},{96,... | collective-permute-start | bytes 393224 | tf_op jit(solution)/shard_map/ppermute | solution.py:280
  29.6 9.6 %collective-permute-start.9 = (bf16[64,1024]{1,0:T(8,128)(2,1)S(1)}, bf16[64,1024]{1,0:T(8,128)(2,1)S(1)}, u32[]{:S(2)}, u32[]{:S(2)}) collective-permute-start(bf16[64,1024]{1,0:T(8,128)(2,1)S(1)} %pad_maximum_fusion.refs_0_), channel_id=1, source_target_pairs={{24,0},{32,8},{40,16},{48,24},{56,32},{64,40},{72,48},{80,56},{88,... | collective-permute-start | bytes 393224 | tf_op jit(solution)/shard_map/ppermute | solution.py:280
  30.9 7.7 %collective-permute-start.8 = (bf16[64,1024]{1,0:T(8,128)(2,1)S(1)}, bf16[64,1024]{1,0:T(8,128)(2,1)S(1)}, u32[]{:S(2)}, u32[]{:S(2)}) collective-permute-start(bf16[64,1024]{1,0:T(8,128)(2,1)S(1)} %pad_maximum_fusion.refs_0_), channel_id=1, source_target_pairs={{16,0},{24,8},{32,16},{40,24},{48,32},{56,40},{64,48},{72,56},{80,... | collective-permute-start | bytes 393224 | tf_op jit(solution)/shard_map/ppermute | solution.py:280
  32.2 5.7 %collective-permute-start.7 = (bf16[64,1024]{1,0:T(8,128)(2,1)S(1)}, bf16[64,1024]{1,0:T(8,128)(2,1)S(1)}, u32[]{:S(2)}, u32[]{:S(2)}) collective-permute-start(bf16[64,1024]{1,0:T(8,128)(2,1)S(1)} %pad_maximum_fusion.refs_0_), channel_id=1, source_target_pairs={{8,0},{16,8},{24,16},{32,24},{40,32},{48,40},{56,48},{64,56},{72,6... | collective-permute-start | bytes 393224 | tf_op jit(solution)/shard_map/ppermute | solution.py:280
  40.6 6.2 %collective-permute-start.11 = (bf16[320,1024]{1,0:T(8,128)(2,1)}, bf16[320,1024]{1,0:T(8,128)(2,1)S(1)}, u32[]{:S(2)}, u32[]{:S(2)}) collective-permute-start(bf16[320,1024]{1,0:T(8,128)(2,1)} %constant_dynamic-update-slice_fusion), channel_id=1, source_target_pairs={{0,1},{1,0},{2,3},{3,2},{4,5},{5,4},{6,7},{7,6},{8,9},{9,8},{10,11... | collective-permute-start | bytes 1966088 | tf_op jit(solution)/shard_map/ppermute | solution.py:301
  45.0 90.6 %slice-start = ((s8[8388608]{0:T(1024)(128)(4,1)}), s8[4194304]{0:T(1024)(128)(4,1)S(1)}, s32[]{:S(2)}) async-start(s8[8388608]{0:T(1024)(128)(4,1)} %bitcast.23), calls=%async_computation | async-start | bytes 8388608
  45.0 90.6 %slice-start.1 = ((s8[8388608]{0:T(1024)(128)(4,1)}), s8[4194304]{0:T(1024)(128)(4,1)S(1)}, s32[]{:S(2)}) async-start(s8[8388608]{0:T(1024)(128)(4,1)} %bitcast.23), calls=%async_computation.1 | async-start | bytes 8388608
  82.9 2.5 %collective-permute-start.12 = (bf16[416,1024]{1,0:T(8,128)(2,1)S(1)}, bf16[416,1024]{1,0:T(8,128)(2,1)S(1)}, u32[]{:S(2)}, u32[]{:S(2)}) collective-permute-start(bf16[416,1024]{1,0:T(8,128)(2,1)S(1)} %get-tuple-element.13), channel_id=1, source_target_pairs={{0,1},{1,0},{2,3},{3,2},{4,5},{5,4},{6,7},{7,6},{8,9},{9,8},{10,11... | collective-permute-start | bytes 2555912 | tf_op jit(solution)/shard_map/ppermute | solution.py:301
  85.8 13.6 %collective-permute-start.17 = (f32[24,1024]{1,0:T(8,128)S(1)}, f32[24,1024]{1,0:T(8,128)S(1)}, u32[]{:S(2)}, u32[]{:S(2)}) collective-permute-start(f32[24,1024]{1,0:T(8,128)S(1)} %get-tuple-element.24), channel_id=1, source_target_pairs={{0,2},{1,3},{2,4},{3,5},{4,6},{5,7},{6,0},{7,1},{8,10},{9,11},{10,... | collective-permute-start | bytes 294920 | tf_op jit(solution)/shard_map/ppermute | solution.py:297
  85.8 19.4 %collective-permute-start.18 = (f32[24,1024]{1,0:T(8,128)S(1)}, f32[24,1024]{1,0:T(8,128)S(1)}, u32[]{:S(2)}, u32[]{:S(2)}) collective-permute-start(f32[24,1024]{1,0:T(8,128)S(1)} %get-tuple-element.25), channel_id=1, source_target_pairs={{0,4},{1,5},{2,6},{3,7},{4,0},{5,1},{6,2},{7,3},{8,12},{9,13},{10,... | collective-permute-start | bytes 294920 | tf_op jit(solution)/shard_map/ppermute | solution.py:297
  87.5 20.1 %collective-permute-start.19 = (f32[24,1024]{1,0:T(8,128)S(1)}, f32[24,1024]{1,0:T(8,128)S(1)}, u32[]{:S(2)}, u32[]{:S(2)}) collective-permute-start(f32[24,1024]{1,0:T(8,128)S(1)} %get-tuple-element.26), channel_id=1, source_target_pairs={{0,6},{1,7},{2,0},{3,1},{4,2},{5,3},{6,4},{7,5},{8,14},{9,15},{10,... | collective-permute-start | bytes 294920 | tf_op jit(solution)/shard_map/ppermute | solution.py:297
  89.2 18.5 %collective-permute-start.13 = (bf16[64,1024]{1,0:T(8,128)(2,1)S(1)}, bf16[64,1024]{1,0:T(8,128)(2,1)S(1)}, u32[]{:S(2)}, u32[]{:S(2)}) collective-permute-start(bf16[64,1024]{1,0:T(8,128)(2,1)S(1)} %get-tuple-element.29), channel_id=1, source_target_pairs={{0,8},{8,16},{16,24},{24,32},{32,40},{40,48},{48,56},{56,64},{64,7... | collective-permute-start | bytes 393224 | tf_op jit(solution)/shard_map/ppermute | solution.py:280
  93.7 13.9 %collective-permute-start.16 = (bf16[64,1024]{1,0:T(8,128)(2,1)S(1)}, bf16[64,1024]{1,0:T(8,128)(2,1)S(1)}, u32[]{:S(2)}, u32[]{:S(2)}) collective-permute-start(bf16[64,1024]{1,0:T(8,128)(2,1)S(1)} %get-tuple-element.30), channel_id=1, source_target_pairs={{0,32},{8,40},{16,48},{24,56},{32,64},{40,72},{48,80},{56,88},{64,... | collective-permute-start | bytes 393224 | tf_op jit(solution)/shard_map/ppermute | solution.py:280
  99.4 8.3 %collective-permute-start.15 = (bf16[64,1024]{1,0:T(8,128)(2,1)S(1)}, bf16[64,1024]{1,0:T(8,128)(2,1)S(1)}, u32[]{:S(2)}, u32[]{:S(2)}) collective-permute-start(bf16[64,1024]{1,0:T(8,128)(2,1)S(1)} %get-tuple-element.31), channel_id=1, source_target_pairs={{0,24},{8,32},{16,40},{24,48},{32,56},{40,64},{48,72},{56,80},{64,... | collective-permute-start | bytes 393224 | tf_op jit(solution)/shard_map/ppermute | solution.py:280
  105.2 4.3 %collective-permute-start.14 = (bf16[64,1024]{1,0:T(8,128)(2,1)S(1)}, bf16[64,1024]{1,0:T(8,128)(2,1)S(1)}, u32[]{:S(2)}, u32[]{:S(2)}) collective-permute-start(bf16[64,1024]{1,0:T(8,128)(2,1)S(1)} %get-tuple-element.32), channel_id=1, source_target_pairs={{0,16},{8,24},{16,32},{24,40},{32,48},{40,56},{48,64},{56,72},{64,... | collective-permute-start | bytes 393224 | tf_op jit(solution)/shard_map/ppermute | solution.py:280
  109.6 9.1 %collective-permute-start.25 = (f32[24,1024]{1,0:T(8,128)S(1)}, f32[24,1024]{1,0:T(8,128)S(1)}, u32[]{:S(2)}, u32[]{:S(2)}) collective-permute-start(f32[24,1024]{1,0:T(8,128)S(1)} %fusion.4), channel_id=1, source_target_pairs={{0,24},{8,0},{16,8},{24,16},{32,56},{40,32},{48,40},{56,48},{64,88... | collective-permute-start | bytes 294920 | tf_op jit(solution)/shard_map/ppermute | solution.py:288
  115.6 5.7 %collective-permute-start.24 = (f32[24,1024]{1,0:T(8,128)S(1)}, f32[24,1024]{1,0:T(8,128)S(1)}, u32[]{:S(2)}, u32[]{:S(2)}) collective-permute-start(f32[24,1024]{1,0:T(8,128)S(1)} %fusion.4), channel_id=1, source_target_pairs={{0,8},{8,16},{16,24},{24,0},{32,40},{40,48},{48,56},{56,32},{64,72... | collective-permute-start | bytes 294920 | tf_op jit(solution)/shard_map/ppermute | solution.py:288
  115.6 5.7 %collective-permute-start.23 = (f32[24,1024]{1,0:T(8,128)S(1)}, f32[24,1024]{1,0:T(8,128)S(1)}, u32[]{:S(2)}, u32[]{:S(2)}) collective-permute-start(f32[24,1024]{1,0:T(8,128)S(1)} %fusion.4), channel_id=1, source_target_pairs={{0,16},{8,24},{16,0},{24,8},{32,48},{40,56},{48,32},{56,40},{64,80... | collective-permute-start | bytes 294920 | tf_op jit(solution)/shard_map/ppermute | solution.py:288
  116.9 4.5 %collective-permute-start.22 = (bf16[64,1024]{1,0:T(8,128)(2,1)S(1)}, bf16[64,1024]{1,0:T(8,128)(2,1)S(1)}, u32[]{:S(2)}, u32[]{:S(2)}) collective-permute-start(bf16[64,1024]{1,0:T(8,128)(2,1)S(1)} %convert_element_type.47), channel_id=1, source_target_pairs={{0,6},{1,7},{2,0},{3,1},{4,2},{5,3},{6,4},{7,5},{8,14},{9,15},{10,... | collective-permute-start | bytes 393224 | tf_op jit(solution)/shard_map/ppermute | solution.py:297
  117.0 5.4 %collective-permute-start.21 = (bf16[64,1024]{1,0:T(8,128)(2,1)S(1)}, bf16[64,1024]{1,0:T(8,128)(2,1)S(1)}, u32[]{:S(2)}, u32[]{:S(2)}) collective-permute-start(bf16[64,1024]{1,0:T(8,128)(2,1)S(1)} %convert_element_type.47), channel_id=1, source_target_pairs={{0,4},{1,5},{2,6},{3,7},{4,0},{5,1},{6,2},{7,3},{8,12},{9,13},{10,... | collective-permute-start | bytes 393224 | tf_op jit(solution)/shard_map/ppermute | solution.py:297
  118.7 5.1 %collective-permute-start.20 = (bf16[64,1024]{1,0:T(8,128)(2,1)S(1)}, bf16[64,1024]{1,0:T(8,128)(2,1)S(1)}, u32[]{:S(2)}, u32[]{:S(2)}) collective-permute-start(bf16[64,1024]{1,0:T(8,128)(2,1)S(1)} %convert_element_type.47), channel_id=1, source_target_pairs={{0,2},{1,3},{2,4},{3,5},{4,6},{5,7},{6,0},{7,1},{8,10},{9,11},{10,... | collective-permute-start | bytes 393224 | tf_op jit(solution)/shard_map/ppermute | solution.py:297
  123.9 8.3 %collective-permute-start.29 = (f32[24,1024]{1,0:T(8,128)S(1)}, f32[24,1024]{1,0:T(8,128)S(1)}, u32[]{:S(2)}, u32[]{:S(2)}) collective-permute-start(f32[24,1024]{1,0:T(8,128)S(1)} %add_add_fusion.2), channel_id=1, source_target_pairs={{0,96},{8,104},{16,112},{24,120},{32,0},{40,8},{48,16},{56,24},{64... | collective-permute-start | bytes 294920 | tf_op jit(solution)/shard_map/ppermute | solution.py:288
  126.3 5.9 %collective-permute-start.28 = (f32[24,1024]{1,0:T(8,128)S(1)}, f32[24,1024]{1,0:T(8,128)S(1)}, u32[]{:S(2)}, u32[]{:S(2)}) collective-permute-start(f32[24,1024]{1,0:T(8,128)S(1)} %add_add_fusion.2), channel_id=1, source_target_pairs={{0,32},{8,40},{16,48},{24,56},{32,64},{40,72},{48,80},{56,88},{64,... | collective-permute-start | bytes 294920 | tf_op jit(solution)/shard_map/ppermute | solution.py:288
  126.3 5.9 %collective-permute-start.27 = (f32[24,1024]{1,0:T(8,128)S(1)}, f32[24,1024]{1,0:T(8,128)S(1)}, u32[]{:S(2)}, u32[]{:S(2)}) collective-permute-start(f32[24,1024]{1,0:T(8,128)S(1)} %add_add_fusion.2), channel_id=1, source_target_pairs={{0,64},{8,72},{16,80},{24,88},{32,96},{40,104},{48,112},{56,120},{... | collective-permute-start | bytes 294920 | tf_op jit(solution)/shard_map/ppermute | solution.py:288
  127.7 5.7 %collective-permute-start.26 = (f32[64,1024]{1,0:T(8,128)S(1)}, f32[64,1024]{1,0:T(8,128)S(1)}, u32[]{:S(2)}, u32[]{:S(2)}) collective-permute-start(f32[64,1024]{1,0:T(8,128)S(1)} %add_add_fusion.mine_ref), channel_id=1, source_target_pairs={{0,1},{1,0},{2,3},{3,2},{4,5},{5,4},{6,7},{7,6},{8,9},{9,8},{10,11... | collective-permute-start | bytes 786440 | tf_op jit(solution)/shard_map/ppermute | solution.py:301
  133.4 6.6 %collective-permute-start.32 = (bf16[16,1024]{1,0:T(8,128)(2,1)S(1)}, bf16[16,1024]{1,0:T(8,128)(2,1)S(1)}, u32[]{:S(2)}, u32[]{:S(2)}) collective-permute-start(bf16[16,1024]{1,0:T(8,128)(2,1)S(1)} %slice_divide_fusion), channel_id=1, source_target_pairs={{0,6},{1,7},{2,0},{3,1},{4,2},{5,3},{6,4},{7,5},{8,14},{9,15},{10,... | collective-permute-start | bytes 98312 | tf_op jit(solution)/shard_map/ppermute | solution.py:297
  134.4 5.6 %collective-permute-start.31 = (bf16[16,1024]{1,0:T(8,128)(2,1)S(1)}, bf16[16,1024]{1,0:T(8,128)(2,1)S(1)}, u32[]{:S(2)}, u32[]{:S(2)}) collective-permute-start(bf16[16,1024]{1,0:T(8,128)(2,1)S(1)} %slice_divide_fusion), channel_id=1, source_target_pairs={{0,4},{1,5},{2,6},{3,7},{4,0},{5,1},{6,2},{7,3},{8,12},{9,13},{10,... | collective-permute-start | bytes 98312 | tf_op jit(solution)/shard_map/ppermute | solution.py:297
  135.0 4.9 %collective-permute-start.30 = (bf16[16,1024]{1,0:T(8,128)(2,1)S(1)}, bf16[16,1024]{1,0:T(8,128)(2,1)S(1)}, u32[]{:S(2)}, u32[]{:S(2)}) collective-permute-start(bf16[16,1024]{1,0:T(8,128)(2,1)S(1)} %slice_divide_fusion), channel_id=1, source_target_pairs={{0,2},{1,3},{2,4},{3,5},{4,6},{5,7},{6,0},{7,1},{8,10},{9,11},{10,... | collective-permute-start | bytes 98312 | tf_op jit(solution)/shard_map/ppermute | solution.py:297
  140.0 7.0 %copy-start.4 = (bf16[64,1024]{1,0:T(8,128)(2,1)}, bf16[64,1024]{1,0:T(8,128)(2,1)S(1)}, u32[]{:S(2)}) copy-start(bf16[64,1024]{1,0:T(8,128)(2,1)S(1)} %pad_maximum_fusion.1.mine_ref) | copy-start | bytes 393220
  140.0 7.0 %collective-permute-start.33 = (bf16[64,1024]{1,0:T(8,128)(2,1)S(1)}, bf16[64,1024]{1,0:T(8,128)(2,1)S(1)}, u32[]{:S(2)}, u32[]{:S(2)}) collective-permute-start(bf16[64,1024]{1,0:T(8,128)(2,1)S(1)} %pad_maximum_fusion.1.mine_ref), channel_id=1, source_target_pairs={{0,1},{1,0},{2,3},{3,2},{4,5},{5,4},{6,7},{7,6},{8,9},{9,8},{10,11... | collective-permute-start | bytes 393224 | tf_op jit(solution)/shard_map/ppermute | solution.py:301
  147.0 0.7 copy-start.5

commit v4 on v3

--- a/solution.py
+++ b/solution.py
@@ -22,7 +22,6 @@
 BLOCKS = 5
 BAND = BLOCKS * SLAB
 PER_STEP = 8
-SUMS = BLOCKS * SLAB + 4 * 3 * ROWS
 VMEM = pl.BlockSpec(memory_space=pltpu.VMEM)
 SMEM = pl.BlockSpec(memory_space=pltpu.SMEM)
 
@@ -58,8 +57,8 @@
     return 4 * ((place[1] + half) % 2) + (place[0] + e) % 4
 
 
-def rows_at(place, half, i):
-    return pl.ds(pl.multiple_of((4 * ((place[1] + half) % 2) + i) * ROWS, ROWS), ROWS)
+def rows_of(place, e, c):
+    return pl.ds(pl.multiple_of(((place[0] + e) % 4 * 2 + c) * ROWS, ROWS), ROWS)
 
 
 def project_kernel(half, place, field_ref, out_ref, held, sems):
@@ -97,17 +96,18 @@
 def spread_kernel(place, mine_ref, theirs_ref, field_ref, out_ref, held, sems):
     layers = field_ref.shape[1]
     copies = []
-    for half, ref in enumerate((mine_ref, theirs_ref)):
-        for i in range(4):
-            rows, slot = rows_at(place, half, i), half * 4 + i
-            base = to_left(tiles_of(ref[i * 2 * ROWS : (i + 1) * 2 * ROWS, :].astype(F32)), place[2])
-            for k in range(layers):
-                for t, x in enumerate(to_left(base, k) if k else base):
-                    columns = slice(t * LANES, (t + 1) * LANES)
-                    for part in range(2):
-                        held[slot, part, k, :, columns] = field_ref[part, k, rows, columns] + x[part * ROWS : (part + 1) * ROWS]
-            copies.append(pltpu.make_async_copy(held.at[slot], out_ref.at[:, :, rows, :], sems.at[slot]))
-            copies[-1].start()
+    for slot in range(VIEWS):
+        j, c = divmod(slot, 2)
+        rows, first = rows_of(place, 4 - j, c), slot * 2 * ROWS
+        update = jnp.where(place[1] == 0, mine_ref[first : first + 2 * ROWS, :].astype(F32), theirs_ref[first : first + 2 * ROWS, :].astype(F32))
+        base = to_left(tiles_of(update), place[2])
+        for k in range(layers):
+            for t, x in enumerate(to_left(base, k) if k else base):
+                columns = slice(t * LANES, (t + 1) * LANES)
+                for part in range(2):
+                    held[slot, part, k, :, columns] = field_ref[part, k, rows, columns] + x[part * ROWS : (part + 1) * ROWS]
+        copies.append(pltpu.make_async_copy(held.at[slot], out_ref.at[:, :, rows, :], sems.at[slot]))
+        copies[-1].start()
     for copy in copies:
         copy.wait()
 
@@ -126,14 +126,16 @@
 
 
 def join_kernel(place, mine_ref, theirs_ref, out_ref):
-    for half, ref in enumerate((mine_ref, theirs_ref)):
-        for j in range(4):
-            first = chunk_at(place, half, 4 - j) * (FRAME // VIEWS)
-            for part in range(2):
-                x = ref[j * 2 * ROWS : (j + 1) * 2 * ROWS, :][part * ROWS : (part + 1) * ROWS]
+    for j in range(4):
+        for part in range(2):
+            first = (j * 2 + part) * 2 * ROWS
+            own, other = mine_ref[first : first + 2 * ROWS, :].astype(F32), theirs_ref[first : first + 2 * ROWS, :].astype(F32)
+            x = jnp.where(place[1] == 1, own, other)
+            for c in range(2):
                 for g in range(4):
-                    rows = pl.ds(pl.multiple_of(first + g * ROWS, ROWS), ROWS)
-                    out_ref[part, rows, :] = x[:, g * FRAME : (g + 1) * FRAME].astype(F32)
+                    start = (place[3] + 4 - j) % 4 * SLAB + c * 4 * ROWS + g * ROWS
+                    piece = x[c * ROWS : (c + 1) * ROWS, g * FRAME : (g + 1) * FRAME]
+                    out_ref[part, pl.ds(pl.multiple_of(start, ROWS), ROWS), :] = piece
 
 
 def join(place, mine, theirs):
@@ -151,16 +153,16 @@
 
 
 def visit_kernel(place, off_ref, *refs):
-    bands, (theirs_band, probe_ref, fore_ref, back_ref, amp_ref, mine_ref, theirs_ref, band, upd, num) = refs[:BLOCKS], refs[BLOCKS:]
+    bands, (probe_ref, fore_ref, back_ref, amp_ref, update_ref, sums_ref, band, upd, num) = refs[: 2 * BLOCKS], refs[2 * BLOCKS :]
     step = pl.program_id(0)
 
     @pl.when(step == 0)
     def _():
-        for i in range(2 * BLOCKS):
-            half, block = i // BLOCKS, i % BLOCKS
+        for i, ref in enumerate(bands):
+            half, block = divmod(i, BLOCKS)
             for j in range(4):
-                first = (block * 4 * half + j) * 2 * ROWS
-                x = (theirs_band if half else bands[block])[first : first + 2 * ROWS, :].astype(F32)
+                x = ref[j * 2 * ROWS : (j + 1) * 2 * ROWS, :].astype(F32)
+                x = jnp.where(place[4] + block < place[5], x, 0.0)
                 first = pl.multiple_of(block * SLAB + chunk_at(place, half, 4 - j) * ROWS, ROWS)
                 for part in range(2):
                     for t in range(TILES):
@@ -238,32 +240,35 @@
     def _():
         peak = jnp.max(pr * pr + pi * pi) + 1e-06
         scale = 0.5 / jnp.full((2 * ROWS, COLUMNS), peak, F32)
-        for half, ref in enumerate((mine_ref, theirs_ref)):
-            for i in range(4):
-                for b in range(BLOCKS):
-                    rows = pl.ds(pl.multiple_of(b * SLAB + (4 * ((place[1] + half) % 2) + i) * ROWS, ROWS), ROWS)
+        for e in range(4):
+            for b in range(BLOCKS):
+                for c in range(2):
+                    rows = pl.ds(pl.multiple_of(b * SLAB + ((place[0] + e) % 4 * 2 + c) * ROWS, ROWS), ROWS)
                     x = [jnp.concatenate([upd[part, t, rows, :] for t in range(TILES)], 1) for part in range(2)]
-                    first = (b * 4 + i) * 2 * ROWS
-                    ref[first : first + 2 * ROWS, :] = (jnp.concatenate(x, 0) * scale).astype(BF16)
+                    first = ((e * BLOCKS + b) * 2 + c) * 2 * ROWS
+                    update_ref[first : first + 2 * ROWS, :] = (jnp.concatenate(x, 0) * scale).astype(BF16)
             planes = []
-            for e in range(4):
-                for k in range(3):
-                    first = chunk_at(place, half, e) * 4 * ROWS
+            for k in range(3):
+                for c in range(2):
+                    first = (place[3] + e) % 4 * SLAB + c * 4 * ROWS
                     rows = [pl.ds(pl.multiple_of(first + g * ROWS, ROWS), ROWS) for g in range(4)]
                     planes.append(jnp.concatenate([num[k, x, :] for x in rows], 1))
-            ref[BLOCKS * SLAB : SUMS, :] = jnp.concatenate(planes, 0).astype(BF16)
-
-
-def visit_all(place, corners, bands, others, probe, amplitude):
+            sums_ref[e * 6 * ROWS : (e + 1) * 6 * ROWS, :] = jnp.concatenate(planes, 0).astype(BF16)
+
+
+def visit_all(place, corners, bands, probe, amplitude):
     count = amplitude.shape[0]
     fore, back = dft_blocks(FRAME)
     amp_spec = pl.BlockSpec((PER_STEP, FRAME, FRAME), lambda i: (i, 0, 0))
     return pl.pallas_call(
         visit_kernel,
         grid=(count // PER_STEP,),
-        in_specs=[SMEM, SMEM] + [VMEM] * 9 + [amp_spec],
+        in_specs=[SMEM, SMEM] + [VMEM] * 13 + [amp_spec],
         out_specs=[VMEM] * 2,
-        out_shape=[jax.ShapeDtypeStruct((SUMS, COLUMNS), BF16)] * 2,
+        out_shape=[
+            jax.ShapeDtypeStruct((2 * BAND, COLUMNS), BF16),
+            jax.ShapeDtypeStruct((4 * 6 * ROWS, COLUMNS), BF16),
+        ],
         scratch_shapes=[
             pltpu.VMEM((2, TILES, BAND, LANES), F32),
             pltpu.VMEM((2, TILES, BAND, LANES), F32),
@@ -271,75 +276,87 @@
         ],
         compiler_params=pltpu.CompilerParams(vmem_limit_bytes=48 << 20),
         cost_estimate=pl.CostEstimate(flops=count * 16 * 2 * FRAME**3, bytes_accessed=16 << 20, transcendentals=0),
-    )(place, corners, *bands, others, probe, fore, back, amplitude)
-
-
-def slab_along(value, steps):
+    )(place, corners, *bands, probe, fore, back, amplitude)
+
+
+def moved(value, cores, target):
     count = lax.axis_size("slab")
-    first, last = (max(0, -steps), min(count, count - steps))
-    return lax.ppermute(value, "slab", [(source, source + steps) for source in range(first, last)])
-
-
-def slab_ring(value, axis, steps):
     moves = []
-    for i in range(lax.axis_size("slab")):
-        y, x = divmod(i, 4)
-        moves.append((i, 4 * y + (x + steps) % 4 if axis == 0 else 4 * ((y + steps) % 4) + x))
-    return lax.ppermute(value, "slab", moves)
-
-
-def ring_sum(value, axis):
-    one, two, three = (slab_ring(value, axis, k) for k in (1, 2, 3))
+    for slab in range(count):
+        for z in range(4):
+            for core in cores:
+                to_slab, to_z, to_core = target(slab, z, core)
+                moves.append((slab * VIEWS + z * 2 + core, to_slab % count * VIEWS + to_z % 4 * 2 + to_core))
+    return lax.ppermute(value, ("slab", "view"), moves)
+
+
+def core_swap(value, cores=(0, 1)):
+    return moved(value, cores, lambda slab, z, core: (slab, z, 1 - core))
+
+
+def slab_along(value, steps, cores=(0, 1)):
+    return moved(value, cores, lambda slab, z, core: (slab + steps, z, core))
+
+
+def z_along(value, steps, cores=(0, 1)):
+    return moved(value, cores, lambda slab, z, core: (slab, z + steps, core))
+
+
+def x_along(value, steps, cores=(0, 1)):
+    return moved(value, cores, lambda slab, z, core: (slab // 4 * 4 + (slab + steps) % 4, z, core))
+
+
+def y_along(value, steps, cores=(0, 1)):
+    return moved(value, cores, lambda slab, z, core: (slab + 4 * steps, z, core))
+
+
+def ring_parts(along, parts, cores):
+    return parts[0] + sum(along(parts[e].astype(BF16), e, cores).astype(F32) for e in (1, 2, 3))
+
+
+def ring_total(along, value, cores):
+    one, two, three = (along(value, e, cores) for e in (1, 2, 3))
     return (value + two) + (one + three)
 
 
-def z_along(value, steps):
-    return lax.ppermute(value, "view", [(i, (i + 2 * steps) % VIEWS) for i in range(VIEWS)])
-
-
-def core_swap(value):
-    return lax.ppermute(value, "view", [(i, i ^ 1) for i in range(VIEWS)])
-
-
-def z_sum(value):
-    return value[0] + z_along(value[1], 1) + z_along(value[2], 2) + z_along(value[3], 3)
-
-
-def z_gather(value):
-    return jnp.concatenate([value] + [z_along(value, d) for d in (1, 2, 3)], 0)
+def ring_gather(along, value, cores):
+    return jnp.concatenate([value] + [along(value, e, cores) for e in (1, 2, 3)], 0)
 
 
 def on_device(object_field, probe, amplitude, offsets):
     layers = object_field.shape[1]
-    view = lax.axis_index("view")
-    place = jnp.stack([view // 2, view % 2, view * layers]).astype(jnp.int32)
-    corners = offsets - jnp.stack([lax.axis_index("slab") * SLAB, 0]).astype(jnp.int32)
+    view, slab = lax.axis_index("view"), lax.axis_index("slab")
+    count = lax.axis_size("slab")
+    place = jnp.stack([view >> 1, view & 1, view * layers, slab & 3, slab, count]).astype(jnp.int32)
+    corners = offsets - jnp.stack([slab * SLAB, 0]).astype(jnp.int32)
 
     received = core_swap(project(place, object_field, 1))
-    piece = z_sum(project(place, object_field, 0) + received).astype(BF16)
-    mine = z_gather(piece)
+    shares = project(place, object_field, 0) + received
+    piece = shares[0] + sum(z_along(shares[e], e) for e in (1, 2, 3))
+    mine = ring_gather(z_along, piece.astype(BF16), (0, 1))
     bands = [mine] + [slab_along(mine, -k) for k in range(1, BLOCKS)]
-    others = core_swap(jnp.concatenate(bands, 0))
-
-    mine, theirs = visit_all(place, corners, bands, others, probe, amplitude)
-    both = mine.astype(F32) + core_swap(theirs).astype(F32)
-    update = both[:SLAB]
+    bands = bands + [core_swap(x) for x in bands]
+    update, sums = visit_all(place, corners, bands, probe, amplitude)
+
+    update = update.astype(F32) + core_swap(update, (1,)).astype(F32)
+    sums = sums.astype(F32) + core_swap(sums, (0,)).astype(F32)
+    update = ring_parts(z_along, update.reshape(4, 2 * BAND // 4, COLUMNS), (0,))
+    sums = ring_parts(x_along, sums.reshape(4, 6 * ROWS, COLUMNS), (1,))
+    blocks = update.reshape(BLOCKS, 4 * ROWS, COLUMNS)
+    update = blocks[0]
     for k in range(1, BLOCKS):
-        update = update + slab_along(both[k * SLAB : (k + 1) * SLAB].astype(BF16), k).astype(F32)
-    totals = z_sum(both[BLOCKS * SLAB :].reshape(4, 3 * ROWS, COLUMNS))
-    update, totals = lax.optimization_barrier((update, totals))
-    sent = update.astype(BF16)
-    update = update + sum(z_along(sent, d).astype(F32) for d in (1, 2, 3))
-    totals = ring_sum(totals, 0)
-    update, totals = lax.optimization_barrier((update, totals))
-    update_there = core_swap(update)
-    totals = ring_sum(totals, 1)
-    ratio = (totals[: 2 * ROWS].reshape(2, ROWS, COLUMNS) / totals[2 * ROWS :]).reshape(2 * ROWS, COLUMNS)
-    update_there, ratio = lax.optimization_barrier((update_there, ratio))
-    ratio = z_gather(ratio.astype(BF16))
+        term = slab_along(blocks[k].astype(BF16), k, (0,)).astype(F32)
+        update = update + jnp.where(slab >= k, term, 0.0)
+    sums = ring_total(z_along, sums, (1,))
+    update = ring_gather(z_along, update.astype(BF16), (0,))
+    sums = ring_total(y_along, sums, (1,))
+    planes = sums.reshape(3, 2 * ROWS, COLUMNS)
+    ratio = (planes[:2] / planes[2]).reshape(4 * ROWS, COLUMNS).astype(BF16)
+    update_there = core_swap(update, (0,))
+    ratio = ring_gather(x_along, ratio, (1,))
     object_new = spread(place, update, update_there, object_field)
     object_new, ratio = lax.optimization_barrier((object_new, ratio))
-    probe_step = join(place, ratio, core_swap(ratio))
+    probe_step = join(place, ratio, core_swap(ratio, (1,)))
     return object_new, probe_step
 
 

time: 150 us -> 154 us (1.027)
  starting transfers between devices: 66.6 us -> 76 us
  local copies, waits for them, and re-layouts: 5.38 us -> 2.64 us
    ppermute x34 -> x42, starting transfers between devices: 66.6 us -> 76 us  [moved(): return lax.ppermute(value, ('slab', 'view'), moves)]
    unnamed x25 -> x19, local copies, waits for them, and re-layouts: 4.64 us -> 1.88 us
    ppermute x34 -> x42, waiting for transfers between devices: 22.3 us -> 21.4 us  [moved(): return lax.ppermute(value, ('slab', 'view'), moves)]
  transfers between devices with their start and end apart: 34 -> 42, of which waited for: 14 -> 15; matrix products, arithmetic and copies ran while one was open for 3% -> 1% of each run, Pallas kernels for 6% -> 3%
where the time goes in v4:
time: 154 us
  starting transfers between devices  76 us (49%)
  Pallas kernels  50.3 us (33%)
  waiting for transfers between devices  21.4 us (14%)
  local copies, waits for them, and re-layouts  2.64 us (2%)
  other arithmetic  2.36 us (2%)
    ppermute x42, starting transfers between devices, moved(): return lax.ppermute(value, ('slab', 'view'), moves)  76 us
    pallas_call x1, Pallas kernels, visit_all(): pl.pallas_call(visit_kernel, grid=(count // PER_STEP,), in_specs=[SMEM, S...  35.3 us
    ppermute x42, waiting for transfers between devices, moved(): return lax.ppermute(value, ('slab', 'view'), moves)  21.4 us
    pallas_call x2, Pallas kernels, project(): pl.pallas_call(functools.partial(project_kernel, half), in_specs=[SMEM, p...  8.89 us
    pallas_call x1, Pallas kernels, spread(): pl.pallas_call(spread_kernel, in_specs=[SMEM, VMEM, VMEM, VMEM], out_spec...  4.19 us
  transfers between devices with their start and end apart: 42, of which 15 were waited for; matrix products, arithmetic and copies ran while one was open for 1% of the time, Pallas kernels for 3%

profile of v4, /device:TPU:1, one launch (start us, length us, event | category | flops | bytes accessed | tf_op | source)
XLA Modules:
  0.0 153.9 jit_solution(6208289079472647217)
XLA Ops:
  0.6 0.6 stack.29.place
  1.3 4.4 %shard_map.78 = f32[4,16,1024]{2,1,0:T(8,128)} custom-call(s32[6]{0:T(128)} %stack.29.place, f32[2,16,64,1024]{3,2,1,0:T(8,128)} %field_ref.5), custom_call_target="tpu_custom_call" | custom-call | flops 6291456 | bytes 12582912 | tf_op jit(solution)/shard_map/pallas_call | solution.py:85
  5.8 1.5 collective-permute-start
  7.3 4.4 %shard_map.77 = f32[4,16,1024]{2,1,0:T(8,128)} custom-call(s32[6]{0:T(128)} %stack.29.place, f32[2,16,64,1024]{3,2,1,0:T(8,128)} %field_ref.5), custom_call_target="tpu_custom_call" | custom-call | flops 6291456 | bytes 12582912 | tf_op jit(solution)/shard_map/pallas_call | solution.py:85
  11.7 1.0 add.66
  12.8 3.8 %collective-permute-start.2 = (f32[16,1024]{1,0:T(8,128)S(1)}, f32[16,1024]{1,0:T(8,128)S(1)}, u32[]{:S(2)}, u32[]{:S(2)}) collective-permute-start(f32[16,1024]{1,0:T(8,128)S(1)} %get-tuple-element.26), channel_id=1, source_target_pairs={{0,4},{1,5},{2,6},{3,7},{4,0},{5,1},{6,2},{7,3},{8,12},{9,13},{10,... | collective-permute-start | bytes 196616 | tf_op jit(solution)/shard_map/ppermute | solution.py:290
  16.5 0.4 collective-permute-start.3
  17.0 1.0 collective-permute-start.1
  18.0 0.9 collective-permute-done.2
  18.8 1.9 %collective-permute-done.3 = f32[16,1024]{1,0:T(8,128)S(1)} collective-permute-done((f32[16,1024]{1,0:T(8,128)S(1)}, f32[16,1024]{1,0:T(8,128)S(1)}, u32[]{:S(2)}, u32[]{:S(2)}) %collective-permute-start.3) | collective-permute-done | bytes 65568 | tf_op jit(solution)/shard_map/ppermute | solution.py:290
  20.7 0.5 collective-permute-done.1
  21.3 2.4 %collective-permute-start.6 = (bf16[16,1024]{1,0:T(8,128)(2,1)S(1)}, bf16[16,1024]{1,0:T(8,128)(2,1)S(1)}, u32[]{:S(2)}, u32[]{:S(2)}) collective-permute-start(bf16[16,1024]{1,0:T(8,128)(2,1)S(1)} %fusion.6), channel_id=1, source_target_pairs={{0,6},{1,7},{2,0},{3,1},{4,2},{5,3},{6,4},{7,5},{8,14},{9,15},{10,... | collective-permute-start | bytes 98312 | tf_op jit(solution)/shard_map/ppermute | solution.py:290
  23.7 0.7 collective-permute-start.4
  24.3 0.4 collective-permute-done.6
  24.7 3.3 %collective-permute-done.5 = bf16[16,1024]{1,0:T(8,128)(2,1)S(1)} collective-permute-done((bf16[16,1024]{1,0:T(8,128)(2,1)S(1)}, bf16[16,1024]{1,0:T(8,128)(2,1)S(1)}, u32[]{:S(2)}, u32[]{:S(2)}) %collective-permute-start.5) | collective-permute-done | bytes 32800 | tf_op jit(solution)/shard_map/ppermute | solution.py:290
  28.0 2.8 %collective-permute-start.10 = (bf16[64,1024]{1,0:T(8,128)(2,1)S(1)}, bf16[64,1024]{1,0:T(8,128)(2,1)S(1)}, u32[]{:S(2)}, u32[]{:S(2)}) collective-permute-start(bf16[64,1024]{1,0:T(8,128)(2,1)S(1)} %pad_maximum_fusion.2.refs_0_), channel_id=1, source_target_pairs={{0,96},{1,97},{2,98},{3,99},{4,100},{5,101},{6,102},{7,103},{8,104... | collective-permute-start | bytes 393224 | tf_op jit(solution)/shard_map/ppermute | solution.py:290
  30.8 1.4 collective-permute-start.9
  32.2 2.3 %collective-permute-start.8 = (bf16[64,1024]{1,0:T(8,128)(2,1)S(1)}, bf16[64,1024]{1,0:T(8,128)(2,1)S(1)}, u32[]{:S(2)}, u32[]{:S(2)}) collective-permute-start(bf16[64,1024]{1,0:T(8,128)(2,1)S(1)} %pad_maximum_fusion.2.refs_0_), channel_id=1, source_target_pairs={{0,112},{1,113},{2,114},{3,115},{4,116},{5,117},{6,118},{7,119},{8... | collective-permute-start | bytes 393224 | tf_op jit(solution)/shard_map/ppermute | solution.py:290
  34.5 1.2 collective-permute-start.7
  35.9 3.7 %collective-permute-start.11 = (bf16[64,1024]{1,0:T(8,128)(2,1)S(1)}, bf16[64,1024]{1,0:T(8,128)(2,1)S(1)}, u32[]{:S(2)}, u32[]{:S(2)}) collective-permute-start(bf16[64,1024]{1,0:T(8,128)(2,1)S(1)} %pad_maximum_fusion.2.refs_0_), channel_id=1, source_target_pairs={{0,1},{1,0},{2,3},{3,2},{4,5},{5,4},{6,7},{7,6},{8,9},{9,8},{10,11... | collective-permute-start | bytes 393224 | tf_op jit(solution)/shard_map/ppermute | solution.py:290
  39.6 0.9 collective-permute-start.14
  40.5 2.1 %collective-permute-start.13 = (bf16[64,1024]{1,0:T(8,128)(2,1)S(1)}, bf16[64,1024]{1,0:T(8,128)(2,1)S(1)}, u32[]{:S(2)}, u32[]{:S(2)}) collective-permute-start(bf16[64,1024]{1,0:T(8,128)(2,1)S(1)} %collective-permute-done.8.refs_2_), channel_id=1, source_target_pairs={{0,1},{1,0},{2,3},{3,2},{4,5},{5,4},{6,7},{7,6},{8,9},{9,8},{10,11... | collective-permute-start | bytes 393224 | tf_op jit(solution)/shard_map/ppermute | solution.py:290
  42.9 0.7 collective-permute-done.13.refs_7_
  43.6 0.4 collective-permute-done.12.refs_6_
  44.0 1.0 copy-done.3
  45.1 35.3 %shard_map.79 = (bf16[640,1024]{1,0:T(8,128)(2,1)S(1)}, bf16[192,1024]{1,0:T(8,128)(2,1)S(1)}) custom-call(s32[6]{0:T(128)S(1)} %copy-done, s32[32,2]{1,0:T(8,128)S(1)} %broadcast_subtract_fusion.off_ref, bf16[64,1024]{1,0:T(8,128)(2,1)S(1)} %pad_maximum_fusion.2.refs_0_, bf16[64,1024]{1,0:T(8,128)(2,1)S(1)} %collective-permute-done.7.refs_1_, ...), custom_call_target="tpu_custom_call" | custom-call | flops 17179869184 | bytes 16777216 | tf_op jit(solution)/shard_map/pallas_call | solution.py:263
  80.3 2.2 %collective-permute-start.16 = (bf16[640,1024]{1,0:T(8,128)(2,1)S(1)}, bf16[640,1024]{1,0:T(8,128)(2,1)S(1)}, u32[]{:S(2)}, u32[]{:S(2)}) collective-permute-start(bf16[640,1024]{1,0:T(8,128)(2,1)S(1)} %get-tuple-element.6), channel_id=1, source_target_pairs={{1,0},{3,2},{5,4},{7,6},{9,8},{11,10},{13,12},{15,14},{17,16},{19,... | collective-permute-start | bytes 3932168 | tf_op jit(solution)/shard_map/ppermute | solution.py:290
  82.5 1.3 collective-permute-start.28
  83.8 1.2 collective-permute-done.16
  85.1 0.6 convert_add_fusion
  85.8 0.8 collective-permute-start.17
  86.6 0.7 collective-permute-start.19
  87.3 0.8 collective-permute-start.18
  88.3 3.3 %collective-permute-start.29 = (bf16[48,1024]{1,0:T(8,128)(2,1)S(1)}, bf16[48,1024]{1,0:T(8,128)(2,1)S(1)}, u32[]{:S(2)}, u32[]{:S(2)}) collective-permute-start(bf16[48,1024]{1,0:T(8,128)(2,1)S(1)} %get-tuple-element.19), channel_id=1, source_target_pairs={{1,9},{3,11},{5,13},{7,15},{9,17},{11,19},{13,21},{15,23},{17,25},... | collective-permute-start | bytes 294920 | tf_op jit(solution)/shard_map/ppermute | solution.py:290
  91.7 5.2 %collective-permute-start.31 = (bf16[48,1024]{1,0:T(8,128)(2,1)S(1)}, bf16[48,1024]{1,0:T(8,128)(2,1)S(1)}, u32[]{:S(2)}, u32[]{:S(2)}) collective-permute-start(bf16[48,1024]{1,0:T(8,128)(2,1)S(1)} %get-tuple-element.20), channel_id=1, source_target_pairs={{1,25},{3,27},{5,29},{7,31},{9,1},{11,3},{13,5},{15,7},{17,9},{19,... | collective-permute-start | bytes 294920 | tf_op jit(solution)/shard_map/ppermute | solution.py:290
  96.9 3.1 %collective-permute-start.30 = (bf16[48,1024]{1,0:T(8,128)(2,1)S(1)}, bf16[48,1024]{1,0:T(8,128)(2,1)S(1)}, u32[]{:S(2)}, u32[]{:S(2)}) collective-permute-start(bf16[48,1024]{1,0:T(8,128)(2,1)S(1)} %get-tuple-element.21), channel_id=1, source_target_pairs={{1,17},{3,19},{5,21},{7,23},{9,25},{11,27},{13,29},{15,31},{17,1},... | collective-permute-start | bytes 294920 | tf_op jit(solution)/shard_map/ppermute | solution.py:290
  100.3 0.7 collective-permute-start.20
  100.9 0.7 collective-permute-start.23
  101.6 0.7 collective-permute-start.22
  102.3 0.7 collective-permute-start.21
  103.0 0.8 collective-permute-done.30
  103.8 2.8 %collective-permute-start.34 = (f32[48,1024]{1,0:T(8,128)S(1)}, f32[48,1024]{1,0:T(8,128)S(1)}, u32[]{:S(2)}, u32[]{:S(2)}) collective-permute-start(f32[48,1024]{1,0:T(8,128)S(1)} %slice_add_fusion.1), channel_id=1, source_target_pairs={{1,7},{3,1},{5,3},{7,5},{9,15},{11,9},{13,11},{15,13},{17,23},{19,... | collective-permute-start | bytes 589832 | tf_op jit(solution)/shard_map/ppermute | solution.py:290
  106.6 2.5 %collective-permute-start.33 = (f32[48,1024]{1,0:T(8,128)S(1)}, f32[48,1024]{1,0:T(8,128)S(1)}, u32[]{:S(2)}, u32[]{:S(2)}) collective-permute-start(f32[48,1024]{1,0:T(8,128)S(1)} %slice_add_fusion.1), channel_id=1, source_target_pairs={{1,3},{3,5},{5,7},{7,1},{9,11},{11,13},{13,15},{15,9},{17,19},{19,... | collective-permute-start | bytes 589832 | tf_op jit(solution)/shard_map/ppermute | solution.py:290
  109.1 3.0 %collective-permute-start.32 = (f32[48,1024]{1,0:T(8,128)S(1)}, f32[48,1024]{1,0:T(8,128)S(1)}, u32[]{:S(2)}, u32[]{:S(2)}) collective-permute-start(f32[48,1024]{1,0:T(8,128)S(1)} %slice_add_fusion.1), channel_id=1, source_target_pairs={{1,5},{3,7},{5,1},{7,3},{9,13},{11,15},{13,9},{15,11},{17,21},{19,... | collective-permute-start | bytes 589832 | tf_op jit(solution)/shard_map/ppermute | solution.py:290
  112.2 0.7 collective-permute-start.26
  112.9 1.6 %collective-permute-done.33 = f32[48,1024]{1,0:T(8,128)S(1)} collective-permute-done((f32[48,1024]{1,0:T(8,128)S(1)}, f32[48,1024]{1,0:T(8,128)S(1)}, u32[]{:S(2)}, u32[]{:S(2)}) %collective-permute-start.33) | collective-permute-done | bytes 196640 | tf_op jit(solution)/shard_map/ppermute | solution.py:290
  114.5 2.5 %collective-permute-done.32 = f32[48,1024]{1,0:T(8,128)S(1)} collective-permute-done((f32[48,1024]{1,0:T(8,128)S(1)}, f32[48,1024]{1,0:T(8,128)S(1)}, u32[]{:S(2)}, u32[]{:S(2)}) %collective-permute-start.32) | collective-permute-done | bytes 196640 | tf_op jit(solution)/shard_map/ppermute | solution.py:290
  117.1 4.2 %collective-permute-start.37 = (f32[48,1024]{1,0:T(8,128)S(1)}, f32[48,1024]{1,0:T(8,128)S(1)}, u32[]{:S(2)}, u32[]{:S(2)}) collective-permute-start(f32[48,1024]{1,0:T(8,128)S(1)} %add_add_fusion.1), channel_id=1, source_target_pairs={{1,97},{3,99},{5,101},{7,103},{9,105},{11,107},{13,109},{15,111},{... | collective-permute-start | bytes 589832 | tf_op jit(solution)/shard_map/ppermute | solution.py:290
  121.3 1.9 %collective-permute-start.36 = (f32[48,1024]{1,0:T(8,128)S(1)}, f32[48,1024]{1,0:T(8,128)S(1)}, u32[]{:S(2)}, u32[]{:S(2)}) collective-permute-start(f32[48,1024]{1,0:T(8,128)S(1)} %add_add_fusion.1), channel_id=1, source_target_pairs={{1,33},{3,35},{5,37},{7,39},{9,41},{11,43},{13,45},{15,47},{17,49}... | collective-permute-start | bytes 589832 | tf_op jit(solution)/shard_map/ppermute | solution.py:290
  123.2 3.1 %collective-permute-start.35 = (f32[48,1024]{1,0:T(8,128)S(1)}, f32[48,1024]{1,0:T(8,128)S(1)}, u32[]{:S(2)}, u32[]{:S(2)}) collective-permute-start(f32[48,1024]{1,0:T(8,128)S(1)} %add_add_fusion.1), channel_id=1, source_target_pairs={{1,65},{3,67},{5,69},{7,71},{9,73},{11,75},{13,77},{15,79},{17,81}... | collective-permute-start | bytes 589832 | tf_op jit(solution)/shard_map/ppermute | solution.py:290
  126.3 0.7 collective-permute-start.25
  127.0 0.7 collective-permute-start.24
  127.7 1.3 collective-permute-start.27
  129.1 2.1 %collective-permute-done.35 = f32[48,1024]{1,0:T(8,128)S(1)} collective-permute-done((f32[48,1024]{1,0:T(8,128)S(1)}, f32[48,1024]{1,0:T(8,128)S(1)}, u32[]{:S(2)}, u32[]{:S(2)}) %collective-permute-start.35) | collective-permute-done | bytes 196640 | tf_op jit(solution)/shard_map/ppermute | solution.py:290
  131.2 3.7 %collective-permute-start.40 = (bf16[32,1024]{1,0:T(8,128)(2,1)S(1)}, bf16[32,1024]{1,0:T(8,128)(2,1)S(1)}, u32[]{:S(2)}, u32[]{:S(2)}) collective-permute-start(bf16[32,1024]{1,0:T(8,128)(2,1)S(1)} %fusion), channel_id=1, source_target_pairs={{1,25},{3,27},{5,29},{7,31},{9,1},{11,3},{13,5},{15,7},{17,9},{19,... | collective-permute-start | bytes 196616 | tf_op jit(solution)/shard_map/ppermute | solution.py:290
  134.9 2.0 %collective-permute-start.39 = (bf16[32,1024]{1,0:T(8,128)(2,1)S(1)}, bf16[32,1024]{1,0:T(8,128)(2,1)S(1)}, u32[]{:S(2)}, u32[]{:S(2)}) collective-permute-start(bf16[32,1024]{1,0:T(8,128)(2,1)S(1)} %fusion), channel_id=1, source_target_pairs={{1,17},{3,19},{5,21},{7,23},{9,25},{11,27},{13,29},{15,31},{17,1},... | collective-permute-start | bytes 196616 | tf_op jit(solution)/shard_map/ppermute | solution.py:290
  136.9 2.4 %collective-permute-start.38 = (bf16[32,1024]{1,0:T(8,128)(2,1)S(1)}, bf16[32,1024]{1,0:T(8,128)(2,1)S(1)}, u32[]{:S(2)}, u32[]{:S(2)}) collective-permute-start(bf16[32,1024]{1,0:T(8,128)(2,1)S(1)} %fusion), channel_id=1, source_target_pairs={{1,9},{3,11},{5,13},{7,15},{9,17},{11,19},{13,21},{15,23},{17,25},... | collective-permute-start | bytes 196616 | tf_op jit(solution)/shard_map/ppermute | solution.py:290
  139.3 2.1 %collective-permute-done.39 = bf16[32,1024]{1,0:T(8,128)(2,1)S(1)} collective-permute-done((bf16[32,1024]{1,0:T(8,128)(2,1)S(1)}, bf16[32,1024]{1,0:T(8,128)(2,1)S(1)}, u32[]{:S(2)}, u32[]{:S(2)}) %collective-permute-start.39) | collective-permute-done | bytes 65568 | tf_op jit(solution)/shard_map/ppermute | solution.py:290
  141.4 1.7 %collective-permute-done.38 = bf16[32,1024]{1,0:T(8,128)(2,1)S(1)} collective-permute-done((bf16[32,1024]{1,0:T(8,128)(2,1)S(1)}, bf16[32,1024]{1,0:T(8,128)(2,1)S(1)}, u32[]{:S(2)}, u32[]{:S(2)}) %collective-permute-start.38) | collective-permute-done | bytes 65568 | tf_op jit(solution)/shard_map/ppermute | solution.py:290
  143.2 4.2 %shard_map.80 = f32[2,16,64,1024]{3,2,1,0:T(8,128)} custom-call(s32[6]{0:T(128)S(1)} %copy-done, bf16[128,1024]{1,0:T(8,128)(2,1)S(1)} %pad_maximum_fusion.mine_ref, bf16[128,1024]{1,0:T(8,128)(2,1)S(1)} %collective-permute-done.27.theirs_ref, f32[2,16,64,1024]{3,2,1,0:T(8,128)S(1)} %bitcast.21), custom_call_target="tpu_custom_call" | custom-call | flops 8388608 | bytes 16777216 | tf_op jit(solution)/shard_map/pallas_call | solution.py:117
  147.4 2.7 %collective-permute-start.41 = (bf16[128,1024]{1,0:T(8,128)(2,1)S(1)}, bf16[128,1024]{1,0:T(8,128)(2,1)S(1)}, u32[]{:S(2)}, u32[]{:S(2)}) collective-permute-start(bf16[128,1024]{1,0:T(8,128)(2,1)S(1)} %pad_maximum_fusion.1.mine_ref), channel_id=1, source_target_pairs={{1,0},{3,2},{5,4},{7,6},{9,8},{11,10},{13,12},{15,14},{17,16},{19,... | collective-permute-start | bytes 786440 | tf_op jit(solution)/shard_map/ppermute | solution.py:290
  150.1 1.1 collective-permute-done.41.theirs_ref
  151.2 0.7 copy-done.5
  152.0 1.9 %shard_map.81 = f32[2,256,256]{2,1,0:T(8,128)} custom-call(s32[6]{0:T(128)} %stack.29.place, bf16[128,1024]{1,0:T(8,128)(2,1)} %copy-done.4, bf16[128,1024]{1,0:T(8,128)(2,1)} %copy-done.5), custom_call_target="tpu_custom_call" | custom-call | flops 1000 | bytes 1048576 | tf_op jit(solution)/shard_map/pallas_call | solution.py:142
  (66 shorter events, 1.4 us)
Async XLA Ops:
  5.7 30.0 %copy-start.6 = (s32[32,2]{0,1:T(2,128)S(1)}, s32[32,2]{0,1:T(2,128)}, u32[]{:S(2)}) copy-start(s32[32,2]{0,1:T(2,128)} %param.9) | copy-start | bytes 772
  5.7 38.3 %copy-start = (s32[6]{0:T(128)S(1)}, s32[6]{0:T(128)}, u32[]{:S(2)}) copy-start(s32[6]{0:T(128)} %stack.29.place) | copy-start | bytes 76
  5.7 38.3 %copy-start.1 = (f32[2,256,256]{2,1,0:T(8,128)S(1)}, f32[2,256,256]{2,1,0:T(8,128)}, u32[]{:S(2)}) copy-start(f32[2,256,256]{2,1,0:T(8,128)} %refs_10_.1) | copy-start | bytes 1572868
  5.8 38.3 %copy-start.2 = (bf16[512,512]{1,0:T(8,128)(2,1)S(1)}, bf16[512,512]{1,0:T(8,128)(2,1)}, u32[]{:S(2)}) copy-start(bf16[512,512]{1,0:T(8,128)(2,1)} %constant.32.clone.refs_12_) | copy-start | bytes 1572868
  5.8 6.0 %collective-permute-start = (f32[4,16,1024]{2,1,0:T(8,128)}, f32[4,16,1024]{2,1,0:T(8,128)S(1)}, u32[]{:S(2)}, u32[]{:S(2)}) collective-permute-start(f32[4,16,1024]{2,1,0:T(8,128)} %shard_map.78), channel_id=1, source_target_pairs={{0,1},{1,0},{2,3},{3,2},{4,5},{5,4},{6,7},{7,6},{8,9},{9,8},{10,11... | collective-permute-start | bytes 786440 | tf_op jit(solution)/shard_map/ppermute | solution.py:290
  12.8 6.1 %collective-permute-start.2 = (f32[16,1024]{1,0:T(8,128)S(1)}, f32[16,1024]{1,0:T(8,128)S(1)}, u32[]{:S(2)}, u32[]{:S(2)}) collective-permute-start(f32[16,1024]{1,0:T(8,128)S(1)} %get-tuple-element.26), channel_id=1, source_target_pairs={{0,4},{1,5},{2,6},{3,7},{4,0},{5,1},{6,2},{7,3},{8,12},{9,13},{10,... | collective-permute-start | bytes 196616 | tf_op jit(solution)/shard_map/ppermute | solution.py:290
  16.5 4.2 %collective-permute-start.3 = (f32[16,1024]{1,0:T(8,128)S(1)}, f32[16,1024]{1,0:T(8,128)S(1)}, u32[]{:S(2)}, u32[]{:S(2)}) collective-permute-start(f32[16,1024]{1,0:T(8,128)S(1)} %get-tuple-element.27), channel_id=1, source_target_pairs={{0,6},{1,7},{2,0},{3,1},{4,2},{5,3},{6,4},{7,5},{8,14},{9,15},{10,... | collective-permute-start | bytes 196616 | tf_op jit(solution)/shard_map/ppermute | solution.py:290
  17.0 4.3 %collective-permute-start.1 = (f32[16,1024]{1,0:T(8,128)S(1)}, f32[16,1024]{1,0:T(8,128)S(1)}, u32[]{:S(2)}, u32[]{:S(2)}) collective-permute-start(f32[16,1024]{1,0:T(8,128)S(1)} %get-tuple-element.28), channel_id=1, source_target_pairs={{0,2},{1,3},{2,4},{3,5},{4,6},{5,7},{6,0},{7,1},{8,10},{9,11},{10,... | collective-permute-start | bytes 196616 | tf_op jit(solution)/shard_map/ppermute | solution.py:290
  21.3 3.4 %collective-permute-start.6 = (bf16[16,1024]{1,0:T(8,128)(2,1)S(1)}, bf16[16,1024]{1,0:T(8,128)(2,1)S(1)}, u32[]{:S(2)}, u32[]{:S(2)}) collective-permute-start(bf16[16,1024]{1,0:T(8,128)(2,1)S(1)} %fusion.6), channel_id=1, source_target_pairs={{0,6},{1,7},{2,0},{3,1},{4,2},{5,3},{6,4},{7,5},{8,14},{9,15},{10,... | collective-permute-start | bytes 98312 | tf_op jit(solution)/shard_map/ppermute | solution.py:290
  23.7 4.3 %collective-permute-start.5 = (bf16[16,1024]{1,0:T(8,128)(2,1)S(1)}, bf16[16,1024]{1,0:T(8,128)(2,1)S(1)}, u32[]{:S(2)}, u32[]{:S(2)}) collective-permute-start(bf16[16,1024]{1,0:T(8,128)(2,1)S(1)} %fusion.6), channel_id=1, source_target_pairs={{0,4},{1,5},{2,6},{3,7},{4,0},{5,1},{6,2},{7,3},{8,12},{9,13},{10,... | collective-permute-start | bytes 98312 | tf_op jit(solution)/shard_map/ppermute | solution.py:290
  23.7 4.3 %collective-permute-start.4 = (bf16[16,1024]{1,0:T(8,128)(2,1)S(1)}, bf16[16,1024]{1,0:T(8,128)(2,1)S(1)}, u32[]{:S(2)}, u32[]{:S(2)}) collective-permute-start(bf16[16,1024]{1,0:T(8,128)(2,1)S(1)} %fusion.6), channel_id=1, source_target_pairs={{0,2},{1,3},{2,4},{3,5},{4,6},{5,7},{6,0},{7,1},{8,10},{9,11},{10,... | collective-permute-start | bytes 98312 | tf_op jit(solution)/shard_map/ppermute | solution.py:290
  28.0 11.5 %collective-permute-start.10 = (bf16[64,1024]{1,0:T(8,128)(2,1)S(1)}, bf16[64,1024]{1,0:T(8,128)(2,1)S(1)}, u32[]{:S(2)}, u32[]{:S(2)}) collective-permute-start(bf16[64,1024]{1,0:T(8,128)(2,1)S(1)} %pad_maximum_fusion.2.refs_0_), channel_id=1, source_target_pairs={{0,96},{1,97},{2,98},{3,99},{4,100},{5,101},{6,102},{7,103},{8,104... | collective-permute-start | bytes 393224 | tf_op jit(solution)/shard_map/ppermute | solution.py:290
  30.8 8.8 %collective-permute-start.9 = (bf16[64,1024]{1,0:T(8,128)(2,1)S(1)}, bf16[64,1024]{1,0:T(8,128)(2,1)S(1)}, u32[]{:S(2)}, u32[]{:S(2)}) collective-permute-start(bf16[64,1024]{1,0:T(8,128)(2,1)S(1)} %pad_maximum_fusion.2.refs_0_), channel_id=1, source_target_pairs={{0,104},{1,105},{2,106},{3,107},{4,108},{5,109},{6,110},{7,111},{8... | collective-permute-start | bytes 393224 | tf_op jit(solution)/shard_map/ppermute | solution.py:290
  32.2 8.3 %collective-permute-start.8 = (bf16[64,1024]{1,0:T(8,128)(2,1)S(1)}, bf16[64,1024]{1,0:T(8,128)(2,1)S(1)}, u32[]{:S(2)}, u32[]{:S(2)}) collective-permute-start(bf16[64,1024]{1,0:T(8,128)(2,1)S(1)} %pad_maximum_fusion.2.refs_0_), channel_id=1, source_target_pairs={{0,112},{1,113},{2,114},{3,115},{4,116},{5,117},{6,118},{7,119},{8... | collective-permute-start | bytes 393224 | tf_op jit(solution)/shard_map/ppermute | solution.py:290
  34.5 8.1 %collective-permute-start.7 = (bf16[64,1024]{1,0:T(8,128)(2,1)S(1)}, bf16[64,1024]{1,0:T(8,128)(2,1)S(1)}, u32[]{:S(2)}, u32[]{:S(2)}) collective-permute-start(bf16[64,1024]{1,0:T(8,128)(2,1)S(1)} %pad_maximum_fusion.2.refs_0_), channel_id=1, source_target_pairs={{0,120},{1,121},{2,122},{3,123},{4,124},{5,125},{6,126},{7,127},{8... | collective-permute-start | bytes 393224 | tf_op jit(solution)/shard_map/ppermute | solution.py:290
  35.9 7.0 %collective-permute-start.11 = (bf16[64,1024]{1,0:T(8,128)(2,1)S(1)}, bf16[64,1024]{1,0:T(8,128)(2,1)S(1)}, u32[]{:S(2)}, u32[]{:S(2)}) collective-permute-start(bf16[64,1024]{1,0:T(8,128)(2,1)S(1)} %pad_maximum_fusion.2.refs_0_), channel_id=1, source_target_pairs={{0,1},{1,0},{2,3},{3,2},{4,5},{5,4},{6,7},{7,6},{8,9},{9,8},{10,11... | collective-permute-start | bytes 393224 | tf_op jit(solution)/shard_map/ppermute | solution.py:290
  39.5 3.4 %collective-permute-start.15 = (bf16[64,1024]{1,0:T(8,128)(2,1)S(1)}, bf16[64,1024]{1,0:T(8,128)(2,1)S(1)}, u32[]{:S(2)}, u32[]{:S(2)}) collective-permute-start(bf16[64,1024]{1,0:T(8,128)(2,1)S(1)} %collective-permute-done.10.refs_4_), channel_id=1, source_target_pairs={{0,1},{1,0},{2,3},{3,2},{4,5},{5,4},{6,7},{7,6},{8,9},{9,8},{10,11... | collective-permute-start | bytes 393224 | tf_op jit(solution)/shard_map/ppermute | solution.py:290
  39.6 3.3 %collective-permute-start.14 = (bf16[64,1024]{1,0:T(8,128)(2,1)S(1)}, bf16[64,1024]{1,0:T(8,128)(2,1)S(1)}, u32[]{:S(2)}, u32[]{:S(2)}) collective-permute-start(bf16[64,1024]{1,0:T(8,128)(2,1)S(1)} %collective-permute-done.9.refs_3_), channel_id=1, source_target_pairs={{0,1},{1,0},{2,3},{3,2},{4,5},{5,4},{6,7},{7,6},{8,9},{9,8},{10,11... | collective-permute-start | bytes 393224 | tf_op jit(solution)/shard_map/ppermute | solution.py:290
  40.5 3.1 %collective-permute-start.13 = (bf16[64,1024]{1,0:T(8,128)(2,1)S(1)}, bf16[64,1024]{1,0:T(8,128)(2,1)S(1)}, u32[]{:S(2)}, u32[]{:S(2)}) collective-permute-start(bf16[64,1024]{1,0:T(8,128)(2,1)S(1)} %collective-permute-done.8.refs_2_), channel_id=1, source_target_pairs={{0,1},{1,0},{2,3},{3,2},{4,5},{5,4},{6,7},{7,6},{8,9},{9,8},{10,11... | collective-permute-start | bytes 393224 | tf_op jit(solution)/shard_map/ppermute | solution.py:290
  42.6 1.3 collective-permute-start.12
  44.0 1.0 copy-start.3
  80.3 4.7 %collective-permute-start.16 = (bf16[640,1024]{1,0:T(8,128)(2,1)S(1)}, bf16[640,1024]{1,0:T(8,128)(2,1)S(1)}, u32[]{:S(2)}, u32[]{:S(2)}) collective-permute-start(bf16[640,1024]{1,0:T(8,128)(2,1)S(1)} %get-tuple-element.6), channel_id=1, source_target_pairs={{1,0},{3,2},{5,4},{7,6},{9,8},{11,10},{13,12},{15,14},{17,16},{19,... | collective-permute-start | bytes 3932168 | tf_op jit(solution)/shard_map/ppermute | solution.py:290
  82.5 5.6 %collective-permute-start.28 = (bf16[192,1024]{1,0:T(8,128)(2,1)S(1)}, bf16[192,1024]{1,0:T(8,128)(2,1)S(1)}, u32[]{:S(2)}, u32[]{:S(2)}) collective-permute-start(bf16[192,1024]{1,0:T(8,128)(2,1)S(1)} %get-tuple-element.7), channel_id=1, source_target_pairs={{0,1},{2,3},{4,5},{6,7},{8,9},{10,11},{12,13},{14,15},{16,17},{18,... | collective-permute-start | bytes 1179656 | tf_op jit(solution)/shard_map/ppermute | solution.py:290
  85.1 58.1 %slice-start = ((s8[8388608]{0:T(1024)(128)(4,1)}), s8[4194304]{0:T(1024)(128)(4,1)S(1)}, s32[]{:S(2)}) async-start(s8[8388608]{0:T(1024)(128)(4,1)} %bitcast.20), calls=%async_computation | async-start | bytes 8388608
  85.8 11.1 %collective-permute-start.17 = (bf16[160,1024]{1,0:T(8,128)(2,1)S(1)}, bf16[160,1024]{1,0:T(8,128)(2,1)S(1)}, u32[]{:S(2)}, u32[]{:S(2)}) collective-permute-start(bf16[160,1024]{1,0:T(8,128)(2,1)S(1)} %get-tuple-element.14), channel_id=1, source_target_pairs={{0,2},{2,4},{4,6},{6,0},{8,10},{10,12},{12,14},{14,8},{16,18},{18,... | collective-permute-start | bytes 983048 | tf_op jit(solution)/shard_map/ppermute | solution.py:290
  86.6 13.4 %collective-permute-start.19 = (bf16[160,1024]{1,0:T(8,128)(2,1)S(1)}, bf16[160,1024]{1,0:T(8,128)(2,1)S(1)}, u32[]{:S(2)}, u32[]{:S(2)}) collective-permute-start(bf16[160,1024]{1,0:T(8,128)(2,1)S(1)} %get-tuple-element.15), channel_id=1, source_target_pairs={{0,6},{2,0},{4,2},{6,4},{8,14},{10,8},{12,10},{14,12},{16,22},{18,... | collective-permute-start | bytes 983048 | tf_op jit(solution)/shard_map/ppermute | solution.py:290
  87.3 55.9 %slice-start.1 = ((s8[8388608]{0:T(1024)(128)(4,1)}), s8[4194304]{0:T(1024)(128)(4,1)S(1)}, s32[]{:S(2)}) async-start(s8[8388608]{0:T(1024)(128)(4,1)} %bitcast.20), calls=%async_computation.1 | async-start | bytes 8388608
  87.3 12.7 %collective-permute-start.18 = (bf16[160,1024]{1,0:T(8,128)(2,1)S(1)}, bf16[160,1024]{1,0:T(8,128)(2,1)S(1)}, u32[]{:S(2)}, u32[]{:S(2)}) collective-permute-start(bf16[160,1024]{1,0:T(8,128)(2,1)S(1)} %get-tuple-element.16), channel_id=1, source_target_pairs={{0,4},{2,6},{4,0},{6,2},{8,12},{10,14},{12,8},{14,10},{16,20},{18,... | collective-permute-start | bytes 983048 | tf_op jit(solution)/shard_map/ppermute | solution.py:290
  88.3 13.3 %collective-permute-start.29 = (bf16[48,1024]{1,0:T(8,128)(2,1)S(1)}, bf16[48,1024]{1,0:T(8,128)(2,1)S(1)}, u32[]{:S(2)}, u32[]{:S(2)}) collective-permute-start(bf16[48,1024]{1,0:T(8,128)(2,1)S(1)} %get-tuple-element.19), channel_id=1, source_target_pairs={{1,9},{3,11},{5,13},{7,15},{9,17},{11,19},{13,21},{15,23},{17,25},... | collective-permute-start | bytes 294920 | tf_op jit(solution)/shard_map/ppermute | solution.py:290
  91.7 10.6 %collective-permute-start.31 = (bf16[48,1024]{1,0:T(8,128)(2,1)S(1)}, bf16[48,1024]{1,0:T(8,128)(2,1)S(1)}, u32[]{:S(2)}, u32[]{:S(2)}) collective-permute-start(bf16[48,1024]{1,0:T(8,128)(2,1)S(1)} %get-tuple-element.20), channel_id=1, source_target_pairs={{1,25},{3,27},{5,29},{7,31},{9,1},{11,3},{13,5},{15,7},{17,9},{19,... | collective-permute-start | bytes 294920 | tf_op jit(solution)/shard_map/ppermute | solution.py:290
  96.9 6.9 %collective-permute-start.30 = (bf16[48,1024]{1,0:T(8,128)(2,1)S(1)}, bf16[48,1024]{1,0:T(8,128)(2,1)S(1)}, u32[]{:S(2)}, u32[]{:S(2)}) collective-permute-start(bf16[48,1024]{1,0:T(8,128)(2,1)S(1)} %get-tuple-element.21), channel_id=1, source_target_pairs={{1,17},{3,19},{5,21},{7,23},{9,25},{11,27},{13,29},{15,31},{17,1},... | collective-permute-start | bytes 294920 | tf_op jit(solution)/shard_map/ppermute | solution.py:290
  100.3 6.3 %collective-permute-start.20 = (bf16[32,1024]{1,0:T(8,128)(2,1)S(1)}, bf16[32,1024]{1,0:T(8,128)(2,1)S(1)}, u32[]{:S(2)}, u32[]{:S(2)}) collective-permute-start(bf16[32,1024]{1,0:T(8,128)(2,1)S(1)} %get-tuple-element.22), channel_id=1, source_target_pairs={{0,8},{2,10},{4,12},{6,14},{8,16},{10,18},{12,20},{14,22},{16,24},... | collective-permute-start | bytes 196616 | tf_op jit(solution)/shard_map/ppermute | solution.py:290
  100.9 8.2 %collective-permute-start.23 = (bf16[32,1024]{1,0:T(8,128)(2,1)S(1)}, bf16[32,1024]{1,0:T(8,128)(2,1)S(1)}, u32[]{:S(2)}, u32[]{:S(2)}) collective-permute-start(bf16[32,1024]{1,0:T(8,128)(2,1)S(1)} %get-tuple-element.23), channel_id=1, source_target_pairs={{0,32},{2,34},{4,36},{6,38},{8,40},{10,42},{12,44},{14,46},{16,48}... | collective-permute-start | bytes 196616 | tf_op jit(solution)/shard_map/ppermute | solution.py:290
  101.6 10.5 %collective-permute-start.22 = (bf16[32,1024]{1,0:T(8,128)(2,1)S(1)}, bf16[32,1024]{1,0:T(8,128)(2,1)S(1)}, u32[]{:S(2)}, u32[]{:S(2)}) collective-permute-start(bf16[32,1024]{1,0:T(8,128)(2,1)S(1)} %get-tuple-element.24), channel_id=1, source_target_pairs={{0,24},{2,26},{4,28},{6,30},{8,32},{10,34},{12,36},{14,38},{16,40}... | collective-permute-start | bytes 196616 | tf_op jit(solution)/shard_map/ppermute | solution.py:290
  102.3 9.8 %collective-permute-start.21 = (bf16[32,1024]{1,0:T(8,128)(2,1)S(1)}, bf16[32,1024]{1,0:T(8,128)(2,1)S(1)}, u32[]{:S(2)}, u32[]{:S(2)}) collective-permute-start(bf16[32,1024]{1,0:T(8,128)(2,1)S(1)} %get-tuple-element.25), channel_id=1, source_target_pairs={{0,16},{2,18},{4,20},{6,22},{8,24},{10,26},{12,28},{14,30},{16,32}... | collective-permute-start | bytes 196616 | tf_op jit(solution)/shard_map/ppermute | solution.py:290
  103.8 9.0 %collective-permute-start.34 = (f32[48,1024]{1,0:T(8,128)S(1)}, f32[48,1024]{1,0:T(8,128)S(1)}, u32[]{:S(2)}, u32[]{:S(2)}) collective-permute-start(f32[48,1024]{1,0:T(8,128)S(1)} %slice_add_fusion.1), channel_id=1, source_target_pairs={{1,7},{3,1},{5,3},{7,5},{9,15},{11,9},{13,11},{15,13},{17,23},{19,... | collective-permute-start | bytes 589832 | tf_op jit(solution)/shard_map/ppermute | solution.py:290
  106.6 7.9 %collective-permute-start.33 = (f32[48,1024]{1,0:T(8,128)S(1)}, f32[48,1024]{1,0:T(8,128)S(1)}, u32[]{:S(2)}, u32[]{:S(2)}) collective-permute-start(f32[48,1024]{1,0:T(8,128)S(1)} %slice_add_fusion.1), channel_id=1, source_target_pairs={{1,3},{3,5},{5,7},{7,1},{9,11},{11,13},{13,15},{15,9},{17,19},{19,... | collective-permute-start | bytes 589832 | tf_op jit(solution)/shard_map/ppermute | solution.py:290
  109.1 7.9 %collective-permute-start.32 = (f32[48,1024]{1,0:T(8,128)S(1)}, f32[48,1024]{1,0:T(8,128)S(1)}, u32[]{:S(2)}, u32[]{:S(2)}) collective-permute-start(f32[48,1024]{1,0:T(8,128)S(1)} %slice_add_fusion.1), channel_id=1, source_target_pairs={{1,5},{3,7},{5,1},{7,3},{9,13},{11,15},{13,9},{15,11},{17,21},{19,... | collective-permute-start | bytes 589832 | tf_op jit(solution)/shard_map/ppermute | solution.py:290
  112.2 14.8 %collective-permute-start.26 = (bf16[32,1024]{1,0:T(8,128)(2,1)S(1)}, bf16[32,1024]{1,0:T(8,128)(2,1)S(1)}, u32[]{:S(2)}, u32[]{:S(2)}) collective-permute-start(bf16[32,1024]{1,0:T(8,128)(2,1)S(1)} %fusion.4), channel_id=1, source_target_pairs={{0,6},{2,0},{4,2},{6,4},{8,14},{10,8},{12,10},{14,12},{16,22},{18,... | collective-permute-start | bytes 196616 | tf_op jit(solution)/shard_map/ppermute | solution.py:290
  117.1 11.9 %collective-permute-start.37 = (f32[48,1024]{1,0:T(8,128)S(1)}, f32[48,1024]{1,0:T(8,128)S(1)}, u32[]{:S(2)}, u32[]{:S(2)}) collective-permute-start(f32[48,1024]{1,0:T(8,128)S(1)} %add_add_fusion.1), channel_id=1, source_target_pairs={{1,97},{3,99},{5,101},{7,103},{9,105},{11,107},{13,109},{15,111},{... | collective-permute-start | bytes 589832 | tf_op jit(solution)/shard_map/ppermute | solution.py:290
  121.3 7.7 %collective-permute-start.36 = (f32[48,1024]{1,0:T(8,128)S(1)}, f32[48,1024]{1,0:T(8,128)S(1)}, u32[]{:S(2)}, u32[]{:S(2)}) collective-permute-start(f32[48,1024]{1,0:T(8,128)S(1)} %add_add_fusion.1), channel_id=1, source_target_pairs={{1,33},{3,35},{5,37},{7,39},{9,41},{11,43},{13,45},{15,47},{17,49}... | collective-permute-start | bytes 589832 | tf_op jit(solution)/shard_map/ppermute | solution.py:290
  123.2 7.9 %collective-permute-start.35 = (f32[48,1024]{1,0:T(8,128)S(1)}, f32[48,1024]{1,0:T(8,128)S(1)}, u32[]{:S(2)}, u32[]{:S(2)}) collective-permute-start(f32[48,1024]{1,0:T(8,128)S(1)} %add_add_fusion.1), channel_id=1, source_target_pairs={{1,65},{3,67},{5,69},{7,71},{9,73},{11,75},{13,77},{15,79},{17,81}... | collective-permute-start | bytes 589832 | tf_op jit(solution)/shard_map/ppermute | solution.py:290
  126.3 1.4 collective-permute-start.25
  127.0 0.7 collective-permute-start.24
  127.7 15.5 %collective-permute-start.27 = (bf16[128,1024]{1,0:T(8,128)(2,1)S(1)}, bf16[128,1024]{1,0:T(8,128)(2,1)S(1)}, u32[]{:S(2)}, u32[]{:S(2)}) collective-permute-start(bf16[128,1024]{1,0:T(8,128)(2,1)S(1)} %pad_maximum_fusion.mine_ref), channel_id=1, source_target_pairs={{0,1},{2,3},{4,5},{6,7},{8,9},{10,11},{12,13},{14,15},{16,17},{18,... | collective-permute-start | bytes 786440 | tf_op jit(solution)/shard_map/ppermute | solution.py:290
  131.2 8.1 %collective-permute-start.40 = (bf16[32,1024]{1,0:T(8,128)(2,1)S(1)}, bf16[32,1024]{1,0:T(8,128)(2,1)S(1)}, u32[]{:S(2)}, u32[]{:S(2)}) collective-permute-start(bf16[32,1024]{1,0:T(8,128)(2,1)S(1)} %fusion), channel_id=1, source_target_pairs={{1,25},{3,27},{5,29},{7,31},{9,1},{11,3},{13,5},{15,7},{17,9},{19,... | collective-permute-start | bytes 196616 | tf_op jit(solution)/shard_map/ppermute | solution.py:290
  134.9 6.5 %collective-permute-start.39 = (bf16[32,1024]{1,0:T(8,128)(2,1)S(1)}, bf16[32,1024]{1,0:T(8,128)(2,1)S(1)}, u32[]{:S(2)}, u32[]{:S(2)}) collective-permute-start(bf16[32,1024]{1,0:T(8,128)(2,1)S(1)} %fusion), channel_id=1, source_target_pairs={{1,17},{3,19},{5,21},{7,23},{9,25},{11,27},{13,29},{15,31},{17,1},... | collective-permute-start | bytes 196616 | tf_op jit(solution)/shard_map/ppermute | solution.py:290
  136.9 6.2 %collective-permute-start.38 = (bf16[32,1024]{1,0:T(8,128)(2,1)S(1)}, bf16[32,1024]{1,0:T(8,128)(2,1)S(1)}, u32[]{:S(2)}, u32[]{:S(2)}) collective-permute-start(bf16[32,1024]{1,0:T(8,128)(2,1)S(1)} %fusion), channel_id=1, source_target_pairs={{1,9},{3,11},{5,13},{7,15},{9,17},{11,19},{13,21},{15,23},{17,25},... | collective-permute-start | bytes 196616 | tf_op jit(solution)/shard_map/ppermute | solution.py:290
  143.2 4.2 %copy-start.4 = (bf16[128,1024]{1,0:T(8,128)(2,1)}, bf16[128,1024]{1,0:T(8,128)(2,1)S(1)}, u32[]{:S(2)}) copy-start(bf16[128,1024]{1,0:T(8,128)(2,1)S(1)} %pad_maximum_fusion.1.mine_ref) | copy-start | bytes 786436
  147.4 3.8 %collective-permute-start.41 = (bf16[128,1024]{1,0:T(8,128)(2,1)S(1)}, bf16[128,1024]{1,0:T(8,128)(2,1)S(1)}, u32[]{:S(2)}, u32[]{:S(2)}) collective-permute-start(bf16[128,1024]{1,0:T(8,128)(2,1)S(1)} %pad_maximum_fusion.1.mine_ref), channel_id=1, source_target_pairs={{1,0},{3,2},{5,4},{7,6},{9,8},{11,10},{13,12},{15,14},{17,16},{19,... | collective-permute-start | bytes 786440 | tf_op jit(solution)/shard_map/ppermute | solution.py:290
  151.2 0.7 copy-start.5

commit v5 on v3

--- a/solution.py
+++ b/solution.py
@@ -127,13 +127,12 @@
 
 def join_kernel(place, mine_ref, theirs_ref, out_ref):
     for half, ref in enumerate((mine_ref, theirs_ref)):
-        for j in range(4):
-            first = chunk_at(place, half, 4 - j) * (FRAME // VIEWS)
-            for part in range(2):
-                x = ref[j * 2 * ROWS : (j + 1) * 2 * ROWS, :][part * ROWS : (part + 1) * ROWS]
+        for part in range(2):
+            for i in range(4):
+                x = ref[(part * 4 + i) * ROWS : (part * 4 + i + 1) * ROWS, :]
                 for g in range(4):
-                    rows = pl.ds(pl.multiple_of(first + g * ROWS, ROWS), ROWS)
-                    out_ref[part, rows, :] = x[:, g * FRAME : (g + 1) * FRAME].astype(F32)
+                    start = ((4 * ((place[1] + half) % 2) + i) * 4 + g) * ROWS
+                    out_ref[part, pl.ds(pl.multiple_of(start, ROWS), ROWS), :] = x[:, g * FRAME : (g + 1) * FRAME]
 
 
 def join(place, mine, theirs):
@@ -151,16 +150,16 @@
 
 
 def visit_kernel(place, off_ref, *refs):
-    bands, (theirs_band, probe_ref, fore_ref, back_ref, amp_ref, mine_ref, theirs_ref, band, upd, num) = refs[:BLOCKS], refs[BLOCKS:]
+    bands, (probe_ref, fore_ref, back_ref, amp_ref, mine_ref, theirs_ref, band, upd, num) = refs[: 2 * BLOCKS], refs[2 * BLOCKS :]
     step = pl.program_id(0)
 
     @pl.when(step == 0)
     def _():
-        for i in range(2 * BLOCKS):
-            half, block = i // BLOCKS, i % BLOCKS
+        for i, ref in enumerate(bands):
+            half, block = divmod(i, BLOCKS)
             for j in range(4):
-                first = (block * 4 * half + j) * 2 * ROWS
-                x = (theirs_band if half else bands[block])[first : first + 2 * ROWS, :].astype(F32)
+                x = ref[j * 2 * ROWS : (j + 1) * 2 * ROWS, :].astype(F32)
+                x = jnp.where(place[3] + block < place[4], x, 0.0)
                 first = pl.multiple_of(block * SLAB + chunk_at(place, half, 4 - j) * ROWS, ROWS)
                 for part in range(2):
                     for t in range(TILES):
@@ -246,22 +245,22 @@
                     first = (b * 4 + i) * 2 * ROWS
                     ref[first : first + 2 * ROWS, :] = (jnp.concatenate(x, 0) * scale).astype(BF16)
             planes = []
-            for e in range(4):
-                for k in range(3):
-                    first = chunk_at(place, half, e) * 4 * ROWS
+            for k in range(3):
+                for i in range(4):
+                    first = (4 * ((place[1] + half) % 2) + i) * 4 * ROWS
                     rows = [pl.ds(pl.multiple_of(first + g * ROWS, ROWS), ROWS) for g in range(4)]
                     planes.append(jnp.concatenate([num[k, x, :] for x in rows], 1))
             ref[BLOCKS * SLAB : SUMS, :] = jnp.concatenate(planes, 0).astype(BF16)
 
 
-def visit_all(place, corners, bands, others, probe, amplitude):
+def visit_all(place, corners, bands, probe, amplitude):
     count = amplitude.shape[0]
     fore, back = dft_blocks(FRAME)
     amp_spec = pl.BlockSpec((PER_STEP, FRAME, FRAME), lambda i: (i, 0, 0))
     return pl.pallas_call(
         visit_kernel,
         grid=(count // PER_STEP,),
-        in_specs=[SMEM, SMEM] + [VMEM] * 9 + [amp_spec],
+        in_specs=[SMEM, SMEM] + [VMEM] * 13 + [amp_spec],
         out_specs=[VMEM] * 2,
         out_shape=[jax.ShapeDtypeStruct((SUMS, COLUMNS), BF16)] * 2,
         scratch_shapes=[
@@ -271,26 +270,20 @@
         ],
         compiler_params=pltpu.CompilerParams(vmem_limit_bytes=48 << 20),
         cost_estimate=pl.CostEstimate(flops=count * 16 * 2 * FRAME**3, bytes_accessed=16 << 20, transcendentals=0),
-    )(place, corners, *bands, others, probe, fore, back, amplitude)
+    )(place, corners, *bands, probe, fore, back, amplitude)
 
 
 def slab_along(value, steps):
     count = lax.axis_size("slab")
-    first, last = (max(0, -steps), min(count, count - steps))
-    return lax.ppermute(value, "slab", [(source, source + steps) for source in range(first, last)])
-
-
-def slab_ring(value, axis, steps):
-    moves = []
-    for i in range(lax.axis_size("slab")):
-        y, x = divmod(i, 4)
-        moves.append((i, 4 * y + (x + steps) % 4 if axis == 0 else 4 * ((y + steps) % 4) + x))
-    return lax.ppermute(value, "slab", moves)
-
-
-def ring_sum(value, axis):
-    one, two, three = (slab_ring(value, axis, k) for k in (1, 2, 3))
-    return (value + two) + (one + three)
+    return lax.ppermute(value, "slab", [(i, (i + steps) % count) for i in range(count)])
+
+
+def x_along(value, steps):
+    return lax.ppermute(value, "slab", [(i, i // 4 * 4 + (i + steps) % 4) for i in range(lax.axis_size("slab"))])
+
+
+def y_along(value, steps):
+    return slab_along(value, 4 * steps)
 
 
 def z_along(value, steps):
@@ -301,44 +294,47 @@
     return lax.ppermute(value, "view", [(i, i ^ 1) for i in range(VIEWS)])
 
 
-def z_sum(value):
-    return value[0] + z_along(value[1], 1) + z_along(value[2], 2) + z_along(value[3], 3)
-
-
-def z_gather(value):
-    return jnp.concatenate([value] + [z_along(value, d) for d in (1, 2, 3)], 0)
+def ring_parts(along, value):
+    value = lax.reduce_precision(value, exponent_bits=8, mantissa_bits=7)
+    sent = value.astype(BF16)
+    return [value] + [along(sent, e) for e in (1, 2, 3)]
+
+
+def paired(parts):
+    own, one, two, three = (x.astype(F32) for x in parts)
+    return (own + two) + (one + three)
 
 
 def on_device(object_field, probe, amplitude, offsets):
     layers = object_field.shape[1]
-    view = lax.axis_index("view")
-    place = jnp.stack([view // 2, view % 2, view * layers]).astype(jnp.int32)
-    corners = offsets - jnp.stack([lax.axis_index("slab") * SLAB, 0]).astype(jnp.int32)
+    view, slab = lax.axis_index("view"), lax.axis_index("slab")
+    place = jnp.stack([view >> 1, view & 1, view * layers, slab, lax.axis_size("slab")]).astype(jnp.int32)
+    corners = offsets - jnp.stack([slab * SLAB, 0]).astype(jnp.int32)
 
     received = core_swap(project(place, object_field, 1))
-    piece = z_sum(project(place, object_field, 0) + received).astype(BF16)
-    mine = z_gather(piece)
+    shares = project(place, object_field, 0) + received
+    piece = (shares[0] + sum(z_along(shares[e], e) for e in (1, 2, 3))).astype(BF16)
+    mine = jnp.concatenate([piece] + [z_along(piece, e) for e in (1, 2, 3)], 0)
     bands = [mine] + [slab_along(mine, -k) for k in range(1, BLOCKS)]
-    others = core_swap(jnp.concatenate(bands, 0))
-
-    mine, theirs = visit_all(place, corners, bands, others, probe, amplitude)
+    bands = bands + [core_swap(x) for x in bands]
+
+    mine, theirs = visit_all(place, corners, bands, probe, amplitude)
     both = mine.astype(F32) + core_swap(theirs).astype(F32)
     update = both[:SLAB]
     for k in range(1, BLOCKS):
-        update = update + slab_along(both[k * SLAB : (k + 1) * SLAB].astype(BF16), k).astype(F32)
-    totals = z_sum(both[BLOCKS * SLAB :].reshape(4, 3 * ROWS, COLUMNS))
-    update, totals = lax.optimization_barrier((update, totals))
+        term = slab_along(both[k * SLAB : (k + 1) * SLAB].astype(BF16), k).astype(F32)
+        update = update + jnp.where(slab >= k, term, 0.0)
+    sums = paired(ring_parts(z_along, both[BLOCKS * SLAB :]))
+    update, sums = lax.optimization_barrier((update, sums))
     sent = update.astype(BF16)
     update = update + sum(z_along(sent, d).astype(F32) for d in (1, 2, 3))
-    totals = ring_sum(totals, 0)
-    update, totals = lax.optimization_barrier((update, totals))
-    update_there = core_swap(update)
-    totals = ring_sum(totals, 1)
-    ratio = (totals[: 2 * ROWS].reshape(2, ROWS, COLUMNS) / totals[2 * ROWS :]).reshape(2 * ROWS, COLUMNS)
-    update_there, ratio = lax.optimization_barrier((update_there, ratio))
-    ratio = z_gather(ratio.astype(BF16))
-    object_new = spread(place, update, update_there, object_field)
-    object_new, ratio = lax.optimization_barrier((object_new, ratio))
+    sums = paired(ring_parts(x_along, sums))
+    update, sums = lax.optimization_barrier((update, sums))
+    parts = ring_parts(y_along, sums)
+    object_new = spread(place, update, core_swap(update), object_field)
+    object_new, parts = lax.optimization_barrier((object_new, parts))
+    planes = paired(parts).reshape(3, 4 * ROWS, COLUMNS)
+    ratio = (planes[:2] / planes[2]).reshape(8 * ROWS, COLUMNS)
     probe_step = join(place, ratio, core_swap(ratio))
     return object_new, probe_step
 

time: 150 us -> 140 us (0.933)
  starting transfers between devices: 66.6 us -> 48 us
  waiting for transfers between devices: 22.3 us -> 32.2 us
    ppermute x14, starting transfers between devices: 34.7 us -> 19.6 us  [the longest x11 16.4 us: slab_along(): lax.ppermute(value, 'slab', [(i, (i + steps) % count) for i in range(coun...]
    ppermute x14, waiting for transfers between devices: 6.32 us -> 13.9 us  [the longest x11 7.78 us: slab_along(): lax.ppermute(value, 'slab', [(i, (i + steps) % count) for i in range(coun...]
    ppermute x15 -> x12, waiting for transfers between devices: 9.78 us -> 13.8 us  [z_along(): lax.ppermute(value, 'view', [(i, (i + 2 * steps) % VIEWS) for i in range(...]
    ppermute x15 -> x12, starting transfers between devices: 15.5 us -> 12.1 us  [z_along(): lax.ppermute(value, 'view', [(i, (i + 2 * steps) % VIEWS) for i in range(...]
    ppermute x5 -> x9, waiting for transfers between devices: 6.2 us -> 4.6 us  [core_swap(): return lax.ppermute(value, 'view', [(i, i ^ 1) for i in range(VIEWS)])]
    unnamed x25 -> x17, local copies, waits for them, and re-layouts: 4.64 us -> 5.25 us
    ppermute x5 -> x9, starting transfers between devices: 16.4 us -> 16.3 us  [core_swap(): return lax.ppermute(value, 'view', [(i, i ^ 1) for i in range(VIEWS)])]
  transfers between devices with their start and end apart: 34 -> 35, of which waited for: 14 -> 18; matrix products, arithmetic and copies ran while one was open for 3% -> 0% of each run, Pallas kernels for 6% -> 6%
where the time goes in v5:
time: 140 us
  Pallas kernels  50.4 us (36%)
  starting transfers between devices  48 us (34%)
  waiting for transfers between devices  32.2 us (23%)
  local copies, waits for them, and re-layouts  5.95 us (4%)
  other arithmetic  2.16 us (2%)
    pallas_call x1, Pallas kernels, visit_all(): pl.pallas_call(visit_kernel, grid=(count // PER_STEP,), in_specs=[SMEM, S...  35.4 us
    ppermute x11, starting transfers between devices, slab_along(): lax.ppermute(value, 'slab', [(i, (i + steps) % count) for i in range(coun...  16.4 us
    ppermute x9, starting transfers between devices, core_swap(): return lax.ppermute(value, 'view', [(i, i ^ 1) for i in range(VIEWS)])  16.3 us
    ppermute x12, waiting for transfers between devices, z_along(): lax.ppermute(value, 'view', [(i, (i + 2 * steps) % VIEWS) for i in range(...  13.8 us
    ppermute x12, starting transfers between devices, z_along(): lax.ppermute(value, 'view', [(i, (i + 2 * steps) % VIEWS) for i in range(...  12.1 us
    pallas_call x2, Pallas kernels, project(): pl.pallas_call(functools.partial(project_kernel, half), in_specs=[SMEM, p...  8.89 us
    ppermute x11, waiting for transfers between devices, slab_along(): lax.ppermute(value, 'slab', [(i, (i + steps) % count) for i in range(coun...  7.78 us
    ppermute x3, waiting for transfers between devices, x_along(): lax.ppermute(value, 'slab', [(i, i // 4 * 4 + (i + steps) % 4) for i in r...  6.11 us
  transfers between devices with their start and end apart: 35, of which 18 were waited for; matrix products, arithmetic and copies ran while one was open for 0% of the time, Pallas kernels for 6%

profile of v5, /device:TPU:1, one launch (start us, length us, event | category | flops | bytes accessed | tf_op | source)
XLA Modules:
  0.0 139.8 jit_solution(16793715077078834980)
XLA Ops:
  0.6 0.6 stack.25.place
  1.3 4.4 %shard_map.78 = f32[4,16,1024]{2,1,0:T(8,128)} custom-call(s32[5]{0:T(128)} %stack.25.place, f32[2,16,64,1024]{3,2,1,0:T(8,128)} %field_ref.5), custom_call_target="tpu_custom_call" | custom-call | flops 6291456 | bytes 12582912 | tf_op jit(solution)/shard_map/pallas_call | solution.py:86
  5.7 1.5 %collective-permute-start = (f32[4,16,1024]{2,1,0:T(8,128)}, f32[4,16,1024]{2,1,0:T(8,128)S(1)}, u32[]{:S(2)}, u32[]{:S(2)}) collective-permute-start(f32[4,16,1024]{2,1,0:T(8,128)} %shard_map.78), channel_id=1, source_target_pairs={{0,1},{1,0},{2,3},{3,2},{4,5},{5,4},{6,7},{7,6},{8,9},{9,8},{10,11... | collective-permute-start | bytes 786440 | tf_op jit(solution)/shard_map/ppermute | solution.py:294
  7.2 4.4 %shard_map.77 = f32[4,16,1024]{2,1,0:T(8,128)} custom-call(s32[5]{0:T(128)} %stack.25.place, f32[2,16,64,1024]{3,2,1,0:T(8,128)} %field_ref.5), custom_call_target="tpu_custom_call" | custom-call | flops 6291456 | bytes 12582912 | tf_op jit(solution)/shard_map/pallas_call | solution.py:86
  11.7 1.1 add.63
  12.8 3.9 %collective-permute-start.3 = (f32[16,1024]{1,0:T(8,128)S(1)}, f32[16,1024]{1,0:T(8,128)S(1)}, u32[]{:S(2)}, u32[]{:S(2)}) collective-permute-start(f32[16,1024]{1,0:T(8,128)S(1)} %get-tuple-element.33), channel_id=1, source_target_pairs={{0,6},{1,7},{2,0},{3,1},{4,2},{5,3},{6,4},{7,5},{8,14},{9,15},{10,... | collective-permute-start | bytes 196616 | tf_op jit(solution)/shard_map/ppermute | solution.py:290
  16.8 1.3 collective-permute-start.2
  18.1 0.2 collective-permute-done.3
  18.3 4.9 %collective-permute-done.1 = f32[16,1024]{1,0:T(8,128)S(1)} collective-permute-done((f32[16,1024]{1,0:T(8,128)S(1)}, f32[16,1024]{1,0:T(8,128)S(1)}, u32[]{:S(2)}, u32[]{:S(2)}) %collective-permute-start.1) | collective-permute-done | bytes 65568 | tf_op jit(solution)/shard_map/ppermute | solution.py:290
  23.1 1.0 collective-permute-start.6
  24.1 0.7 collective-permute-start.4
  24.8 1.2 collective-permute-done.6
  26.0 2.5 %collective-permute-done.5 = bf16[16,1024]{1,0:T(8,128)(2,1)S(1)} collective-permute-done((bf16[16,1024]{1,0:T(8,128)(2,1)S(1)}, bf16[16,1024]{1,0:T(8,128)(2,1)S(1)}, u32[]{:S(2)}, u32[]{:S(2)}) %collective-permute-start.5) | collective-permute-done | bytes 32800 | tf_op jit(solution)/shard_map/ppermute | solution.py:290
  28.5 0.2 collective-permute-done.4
  28.7 5.0 %collective-permute-start.7 = (bf16[64,1024]{1,0:T(8,128)(2,1)S(1)}, bf16[64,1024]{1,0:T(8,128)(2,1)S(1)}, u32[]{:S(2)}, u32[]{:S(2)}) collective-permute-start(bf16[64,1024]{1,0:T(8,128)(2,1)S(1)} %pad_maximum_fusion.refs_0_), channel_id=1, source_target_pairs={{0,120},{8,0},{16,8},{24,16},{32,24},{40,32},{48,40},{56,48},{64,5... | collective-permute-start | bytes 393224 | tf_op jit(solution)/shard_map/ppermute | solution.py:278
  33.7 0.5 collective-permute-start.8
  34.3 0.8 collective-permute-start.9
  35.0 0.2 collective-permute-start.10
  35.2 0.1 copy.9
  35.3 0.1 pad_add_fusion
  35.4 4.0 %collective-permute-start.11 = (bf16[64,1024]{1,0:T(8,128)(2,1)S(1)}, bf16[64,1024]{1,0:T(8,128)(2,1)S(1)}, u32[]{:S(2)}, u32[]{:S(2)}) collective-permute-start(bf16[64,1024]{1,0:T(8,128)(2,1)S(1)} %pad_maximum_fusion.refs_0_), channel_id=1, source_target_pairs={{0,1},{1,0},{2,3},{3,2},{4,5},{5,4},{6,7},{7,6},{8,9},{9,8},{10,11... | collective-permute-start | bytes 393224 | tf_op jit(solution)/shard_map/ppermute | solution.py:294
  39.4 2.3 %collective-permute-start.12 = (bf16[64,1024]{1,0:T(8,128)(2,1)S(1)}, bf16[64,1024]{1,0:T(8,128)(2,1)S(1)}, u32[]{:S(2)}, u32[]{:S(2)}) collective-permute-start(bf16[64,1024]{1,0:T(8,128)(2,1)S(1)} %collective-permute-done.7.refs_1_), channel_id=1, source_target_pairs={{0,1},{1,0},{2,3},{3,2},{4,5},{5,4},{6,7},{7,6},{8,9},{9,8},{10,11... | collective-permute-start | bytes 393224 | tf_op jit(solution)/shard_map/ppermute | solution.py:294
  41.7 1.8 %collective-permute-start.13 = (bf16[64,1024]{1,0:T(8,128)(2,1)S(1)}, bf16[64,1024]{1,0:T(8,128)(2,1)S(1)}, u32[]{:S(2)}, u32[]{:S(2)}) collective-permute-start(bf16[64,1024]{1,0:T(8,128)(2,1)S(1)} %collective-permute-done.8.refs_2_), channel_id=1, source_target_pairs={{0,1},{1,0},{2,3},{3,2},{4,5},{5,4},{6,7},{7,6},{8,9},{9,8},{10,11... | collective-permute-start | bytes 393224 | tf_op jit(solution)/shard_map/ppermute | solution.py:294
  43.5 1.3 collective-permute-start.14
  44.8 0.9 collective-permute-done.14.refs_8_
  45.8 0.4 collective-permute-done.15.refs_9_
  46.2 1.0 copy-done.4
  47.2 35.4 %shard_map.79 = (bf16[416,1024]{1,0:T(8,128)(2,1)S(1)}, bf16[416,1024]{1,0:T(8,128)(2,1)S(1)}) custom-call(s32[5]{0:T(128)S(1)} %copy-done.1, s32[32,2]{1,0:T(8,128)S(1)} %broadcast_subtract_fusion.off_ref, bf16[64,1024]{1,0:T(8,128)(2,1)S(1)} %pad_maximum_fusion.refs_0_, bf16[64,1024]{1,0:T(8,128)(2,1)S(1)} %collective-permute-done.7.refs_1_, ...), custom_call_target="tpu_custom_call" | custom-call | flops 17179869184 | bytes 16777216 | tf_op jit(solution)/shard_map/pallas_call | solution.py:260
  82.6 0.3 collective-permute-start.16
  82.9 2.1 %collective-permute-done.16 = bf16[416,1024]{1,0:T(8,128)(2,1)S(1)} collective-permute-done((bf16[416,1024]{1,0:T(8,128)(2,1)S(1)}, bf16[416,1024]{1,0:T(8,128)(2,1)S(1)}, u32[]{:S(2)}, u32[]{:S(2)}) %collective-permute-start.16) | collective-permute-done | bytes 852000 | tf_op jit(solution)/shard_map/ppermute | solution.py:294
  85.0 0.4 fusion.6
  85.4 0.1 collective-permute-start.20
  85.5 3.8 %collective-permute-start.19 = (bf16[64,1024]{1,0:T(8,128)(2,1)S(1)}, bf16[64,1024]{1,0:T(8,128)(2,1)S(1)}, u32[]{:S(2)}, u32[]{:S(2)}) collective-permute-start(bf16[64,1024]{1,0:T(8,128)(2,1)S(1)} %get-tuple-element.28), channel_id=1, source_target_pairs={{0,24},{8,32},{16,40},{24,48},{32,56},{40,64},{48,72},{56,80},{64,... | collective-permute-start | bytes 393224 | tf_op jit(solution)/shard_map/ppermute | solution.py:278
  89.3 0.6 collective-permute-start.17
  89.9 1.5 %collective-permute-start.23 = (bf16[96,1024]{1,0:T(8,128)(2,1)S(1)}, bf16[96,1024]{1,0:T(8,128)(2,1)S(1)}, u32[]{:S(2)}, u32[]{:S(2)}) collective-permute-start(bf16[96,1024]{1,0:T(8,128)(2,1)S(1)} %fusion), channel_id=1, source_target_pairs={{0,6},{1,7},{2,0},{3,1},{4,2},{5,3},{6,4},{7,5},{8,14},{9,15},{10,... | collective-permute-start | bytes 589832 | tf_op jit(solution)/shard_map/ppermute | solution.py:290
  91.4 2.9 %collective-permute-done.20 = bf16[64,1024]{1,0:T(8,128)(2,1)S(1)} collective-permute-done((bf16[64,1024]{1,0:T(8,128)(2,1)S(1)}, bf16[64,1024]{1,0:T(8,128)(2,1)S(1)}, u32[]{:S(2)}, u32[]{:S(2)}) %collective-permute-start.20) | collective-permute-done | bytes 131104 | tf_op jit(solution)/shard_map/ppermute | solution.py:278
  94.4 0.7 collective-permute-done.19
  95.0 1.3 collective-permute-start.21
  96.4 0.5 collective-permute-done.18
  96.9 3.7 %collective-permute-done.17 = bf16[64,1024]{1,0:T(8,128)(2,1)S(1)} collective-permute-done((bf16[64,1024]{1,0:T(8,128)(2,1)S(1)}, bf16[64,1024]{1,0:T(8,128)(2,1)S(1)}, u32[]{:S(2)}, u32[]{:S(2)}) %collective-permute-start.17) | collective-permute-done | bytes 131104 | tf_op jit(solution)/shard_map/ppermute | solution.py:278
  100.5 0.1 fusion.3
  100.7 1.1 collective-permute-done.22
  101.8 2.4 %collective-permute-done.21 = bf16[96,1024]{1,0:T(8,128)(2,1)S(1)} collective-permute-done((bf16[96,1024]{1,0:T(8,128)(2,1)S(1)}, bf16[96,1024]{1,0:T(8,128)(2,1)S(1)}, u32[]{:S(2)}, u32[]{:S(2)}) %collective-permute-start.21) | collective-permute-done | bytes 196640 | tf_op jit(solution)/shard_map/ppermute | solution.py:290
  104.2 0.1 add_add_fusion.2
  104.4 0.1 collective-permute-start.26
  104.4 1.6 %collective-permute-start.25 = (bf16[64,1024]{1,0:T(8,128)(2,1)S(1)}, bf16[64,1024]{1,0:T(8,128)(2,1)S(1)}, u32[]{:S(2)}, u32[]{:S(2)}) collective-permute-start(bf16[64,1024]{1,0:T(8,128)(2,1)S(1)} %convert_element_type.84), channel_id=1, source_target_pairs={{0,4},{1,5},{2,6},{3,7},{4,0},{5,1},{6,2},{7,3},{8,12},{9,13},{10,... | collective-permute-start | bytes 393224 | tf_op jit(solution)/shard_map/ppermute | solution.py:290
  106.0 0.8 collective-permute-start.24
  106.8 1.9 %collective-permute-start.29 = (bf16[96,1024]{1,0:T(8,128)(2,1)S(1)}, bf16[96,1024]{1,0:T(8,128)(2,1)S(1)}, u32[]{:S(2)}, u32[]{:S(2)}) collective-permute-start(bf16[96,1024]{1,0:T(8,128)(2,1)S(1)} %reduce-precision_convert_fusion), channel_id=1, source_target_pairs={{0,24},{8,0},{16,8},{24,16},{32,56},{40,32},{48,40},{56,48},{64,88... | collective-permute-start | bytes 589832 | tf_op jit(solution)/shard_map/ppermute | solution.py:282
  108.8 1.3 collective-permute-start.27
  110.0 1.2 collective-permute-done.24
  111.3 0.4 collective-permute-done.29
  111.7 5.7 %collective-permute-done.28 = bf16[96,1024]{1,0:T(8,128)(2,1)S(1)} collective-permute-done((bf16[96,1024]{1,0:T(8,128)(2,1)S(1)}, bf16[96,1024]{1,0:T(8,128)(2,1)S(1)}, u32[]{:S(2)}, u32[]{:S(2)}) %collective-permute-start.28) | collective-permute-done | bytes 196640 | tf_op jit(solution)/shard_map/ppermute | solution.py:282
  117.4 0.1 add_add_fusion.1
  117.5 4.2 %collective-permute-start.30 = (f32[64,1024]{1,0:T(8,128)S(1)}, f32[64,1024]{1,0:T(8,128)S(1)}, u32[]{:S(2)}, u32[]{:S(2)}) collective-permute-start(f32[64,1024]{1,0:T(8,128)S(1)} %add_add_fusion.3.mine_ref), channel_id=1, source_target_pairs={{0,1},{1,0},{2,3},{3,2},{4,5},{5,4},{6,7},{7,6},{8,9},{9,8},{10,11... | collective-permute-start | bytes 786440 | tf_op jit(solution)/shard_map/ppermute | solution.py:294
  121.7 1.0 collective-permute-start.31
  122.7 2.5 %collective-permute-start.32 = (bf16[96,1024]{1,0:T(8,128)(2,1)S(1)}, bf16[96,1024]{1,0:T(8,128)(2,1)S(1)}, u32[]{:S(2)}, u32[]{:S(2)}) collective-permute-start(bf16[96,1024]{1,0:T(8,128)(2,1)S(1)} %get-tuple-element.30), channel_id=1, source_target_pairs={{0,64},{8,72},{16,80},{24,88},{32,96},{40,104},{48,112},{56,120},{... | collective-permute-start | bytes 589832 | tf_op jit(solution)/shard_map/ppermute | solution.py:278
  125.2 2.0 %collective-permute-start.33 = (bf16[96,1024]{1,0:T(8,128)(2,1)S(1)}, bf16[96,1024]{1,0:T(8,128)(2,1)S(1)}, u32[]{:S(2)}, u32[]{:S(2)}) collective-permute-start(bf16[96,1024]{1,0:T(8,128)(2,1)S(1)} %get-tuple-element.30), channel_id=1, source_target_pairs={{0,96},{8,104},{16,112},{24,120},{32,0},{40,8},{48,16},{56,24},{64... | collective-permute-start | bytes 589832 | tf_op jit(solution)/shard_map/ppermute | solution.py:278
  127.2 3.4 %copy-done = f32[2,16,64,1024]{3,2,1,0:T(8,128)S(1)} copy-done((f32[2,16,64,1024]{3,2,1,0:T(8,128)S(1)}, f32[2,16,64,1024]{3,2,1,0:T(8,128)}, u32[]{:S(2)}) %copy-start) | copy-done | bytes 8388632
  130.6 4.3 %shard_map.80 = f32[2,16,64,1024]{3,2,1,0:T(8,128)} custom-call(s32[5]{0:T(128)S(1)} %copy-done.1, f32[64,1024]{1,0:T(8,128)S(1)} %add_add_fusion.3.mine_ref, f32[64,1024]{1,0:T(8,128)S(1)} %collective-permute-done.30.theirs_ref, f32[2,16,64,1024]{3,2,1,0:T(8,128)S(1)} %copy-done), custom_call_target="tpu_custom_call" | custom-call | flops 8388608 | bytes 16777216 | tf_op jit(solution)/shard_map/pallas_call | solution.py:117
  134.9 0.1 add_add_fusion
  135.1 0.9 collective-permute-start.34
  136.0 1.2 collective-permute-done.34.theirs_ref
  137.2 0.7 copy-done.6
  137.9 1.9 %shard_map.81 = f32[2,256,256]{2,1,0:T(8,128)} custom-call(s32[5]{0:T(128)} %stack.25.place, f32[64,1024]{1,0:T(8,128)} %copy-done.5, f32[64,1024]{1,0:T(8,128)} %copy-done.6), custom_call_target="tpu_custom_call" | custom-call | flops 1000 | bytes 1048576 | tf_op jit(solution)/shard_map/pallas_call | solution.py:139
  (48 shorter events, 0.4 us)
Async XLA Ops:
  5.7 6.0 %collective-permute-start = (f32[4,16,1024]{2,1,0:T(8,128)}, f32[4,16,1024]{2,1,0:T(8,128)S(1)}, u32[]{:S(2)}, u32[]{:S(2)}) collective-permute-start(f32[4,16,1024]{2,1,0:T(8,128)} %shard_map.78), channel_id=1, source_target_pairs={{0,1},{1,0},{2,3},{3,2},{4,5},{5,4},{6,7},{7,6},{8,9},{9,8},{10,11... | collective-permute-start | bytes 786440 | tf_op jit(solution)/shard_map/ppermute | solution.py:294
  11.7 23.5 %copy-start.7 = (s32[32,2]{0,1:T(2,128)S(1)}, s32[32,2]{0,1:T(2,128)}, u32[]{:S(2)}) copy-start(s32[32,2]{0,1:T(2,128)} %param.9) | copy-start | bytes 772
  11.7 34.5 %copy-start.1 = (s32[5]{0:T(128)S(1)}, s32[5]{0:T(128)}, u32[]{:S(2)}) copy-start(s32[5]{0:T(128)} %stack.25.place) | copy-start | bytes 64
  11.7 34.5 %copy-start.2 = (f32[2,256,256]{2,1,0:T(8,128)S(1)}, f32[2,256,256]{2,1,0:T(8,128)}, u32[]{:S(2)}) copy-start(f32[2,256,256]{2,1,0:T(8,128)} %refs_10_.1) | copy-start | bytes 1572868
  11.7 34.4 %copy-start.3 = (bf16[512,512]{1,0:T(8,128)(2,1)S(1)}, bf16[512,512]{1,0:T(8,128)(2,1)}, u32[]{:S(2)}) copy-start(bf16[512,512]{1,0:T(8,128)(2,1)} %constant.31.clone.refs_11_) | copy-start | bytes 1572868
  12.8 5.4 %collective-permute-start.3 = (f32[16,1024]{1,0:T(8,128)S(1)}, f32[16,1024]{1,0:T(8,128)S(1)}, u32[]{:S(2)}, u32[]{:S(2)}) collective-permute-start(f32[16,1024]{1,0:T(8,128)S(1)} %get-tuple-element.33), channel_id=1, source_target_pairs={{0,6},{1,7},{2,0},{3,1},{4,2},{5,3},{6,4},{7,5},{8,14},{9,15},{10,... | collective-permute-start | bytes 196616 | tf_op jit(solution)/shard_map/ppermute | solution.py:290
  16.8 6.4 %collective-permute-start.1 = (f32[16,1024]{1,0:T(8,128)S(1)}, f32[16,1024]{1,0:T(8,128)S(1)}, u32[]{:S(2)}, u32[]{:S(2)}) collective-permute-start(f32[16,1024]{1,0:T(8,128)S(1)} %get-tuple-element.34), channel_id=1, source_target_pairs={{0,2},{1,3},{2,4},{3,5},{4,6},{5,7},{6,0},{7,1},{8,10},{9,11},{10,... | collective-permute-start | bytes 196616 | tf_op jit(solution)/shard_map/ppermute | solution.py:290
  16.8 6.4 %collective-permute-start.2 = (f32[16,1024]{1,0:T(8,128)S(1)}, f32[16,1024]{1,0:T(8,128)S(1)}, u32[]{:S(2)}, u32[]{:S(2)}) collective-permute-start(f32[16,1024]{1,0:T(8,128)S(1)} %get-tuple-element.32), channel_id=1, source_target_pairs={{0,4},{1,5},{2,6},{3,7},{4,0},{5,1},{6,2},{7,3},{8,12},{9,13},{10,... | collective-permute-start | bytes 196616 | tf_op jit(solution)/shard_map/ppermute | solution.py:290
  23.1 2.8 %collective-permute-start.6 = (bf16[16,1024]{1,0:T(8,128)(2,1)S(1)}, bf16[16,1024]{1,0:T(8,128)(2,1)S(1)}, u32[]{:S(2)}, u32[]{:S(2)}) collective-permute-start(bf16[16,1024]{1,0:T(8,128)(2,1)S(1)} %fusion.5), channel_id=1, source_target_pairs={{0,6},{1,7},{2,0},{3,1},{4,2},{5,3},{6,4},{7,5},{8,14},{9,15},{10,... | collective-permute-start | bytes 98312 | tf_op jit(solution)/shard_map/ppermute | solution.py:290
  24.1 4.4 %collective-permute-start.5 = (bf16[16,1024]{1,0:T(8,128)(2,1)S(1)}, bf16[16,1024]{1,0:T(8,128)(2,1)S(1)}, u32[]{:S(2)}, u32[]{:S(2)}) collective-permute-start(bf16[16,1024]{1,0:T(8,128)(2,1)S(1)} %fusion.5), channel_id=1, source_target_pairs={{0,4},{1,5},{2,6},{3,7},{4,0},{5,1},{6,2},{7,3},{8,12},{9,13},{10,... | collective-permute-start | bytes 98312 | tf_op jit(solution)/shard_map/ppermute | solution.py:290
  24.1 4.6 %collective-permute-start.4 = (bf16[16,1024]{1,0:T(8,128)(2,1)S(1)}, bf16[16,1024]{1,0:T(8,128)(2,1)S(1)}, u32[]{:S(2)}, u32[]{:S(2)}) collective-permute-start(bf16[16,1024]{1,0:T(8,128)(2,1)S(1)} %fusion.5), channel_id=1, source_target_pairs={{0,2},{1,3},{2,4},{3,5},{4,6},{5,7},{6,0},{7,1},{8,10},{9,11},{10,... | collective-permute-start | bytes 98312 | tf_op jit(solution)/shard_map/ppermute | solution.py:290
  28.7 10.7 %collective-permute-start.7 = (bf16[64,1024]{1,0:T(8,128)(2,1)S(1)}, bf16[64,1024]{1,0:T(8,128)(2,1)S(1)}, u32[]{:S(2)}, u32[]{:S(2)}) collective-permute-start(bf16[64,1024]{1,0:T(8,128)(2,1)S(1)} %pad_maximum_fusion.refs_0_), channel_id=1, source_target_pairs={{0,120},{8,0},{16,8},{24,16},{32,24},{40,32},{48,40},{56,48},{64,5... | collective-permute-start | bytes 393224 | tf_op jit(solution)/shard_map/ppermute | solution.py:278
  33.7 8.0 %collective-permute-start.8 = (bf16[64,1024]{1,0:T(8,128)(2,1)S(1)}, bf16[64,1024]{1,0:T(8,128)(2,1)S(1)}, u32[]{:S(2)}, u32[]{:S(2)}) collective-permute-start(bf16[64,1024]{1,0:T(8,128)(2,1)S(1)} %pad_maximum_fusion.refs_0_), channel_id=1, source_target_pairs={{0,112},{8,120},{16,0},{24,8},{32,16},{40,24},{48,32},{56,40},{64,... | collective-permute-start | bytes 393224 | tf_op jit(solution)/shard_map/ppermute | solution.py:278
  34.3 9.2 %collective-permute-start.9 = (bf16[64,1024]{1,0:T(8,128)(2,1)S(1)}, bf16[64,1024]{1,0:T(8,128)(2,1)S(1)}, u32[]{:S(2)}, u32[]{:S(2)}) collective-permute-start(bf16[64,1024]{1,0:T(8,128)(2,1)S(1)} %pad_maximum_fusion.refs_0_), channel_id=1, source_target_pairs={{0,104},{8,112},{16,120},{24,0},{32,8},{40,16},{48,24},{56,32},{64... | collective-permute-start | bytes 393224 | tf_op jit(solution)/shard_map/ppermute | solution.py:278
  35.0 9.8 %collective-permute-start.10 = (bf16[64,1024]{1,0:T(8,128)(2,1)S(1)}, bf16[64,1024]{1,0:T(8,128)(2,1)S(1)}, u32[]{:S(2)}, u32[]{:S(2)}) collective-permute-start(bf16[64,1024]{1,0:T(8,128)(2,1)S(1)} %pad_maximum_fusion.refs_0_), channel_id=1, source_target_pairs={{0,96},{8,104},{16,112},{24,120},{32,0},{40,8},{48,16},{56,24},{64... | collective-permute-start | bytes 393224 | tf_op jit(solution)/shard_map/ppermute | solution.py:278
  35.4 9.4 %collective-permute-start.11 = (bf16[64,1024]{1,0:T(8,128)(2,1)S(1)}, bf16[64,1024]{1,0:T(8,128)(2,1)S(1)}, u32[]{:S(2)}, u32[]{:S(2)}) collective-permute-start(bf16[64,1024]{1,0:T(8,128)(2,1)S(1)} %pad_maximum_fusion.refs_0_), channel_id=1, source_target_pairs={{0,1},{1,0},{2,3},{3,2},{4,5},{5,4},{6,7},{7,6},{8,9},{9,8},{10,11... | collective-permute-start | bytes 393224 | tf_op jit(solution)/shard_map/ppermute | solution.py:294
  39.4 5.4 %collective-permute-start.12 = (bf16[64,1024]{1,0:T(8,128)(2,1)S(1)}, bf16[64,1024]{1,0:T(8,128)(2,1)S(1)}, u32[]{:S(2)}, u32[]{:S(2)}) collective-permute-start(bf16[64,1024]{1,0:T(8,128)(2,1)S(1)} %collective-permute-done.7.refs_1_), channel_id=1, source_target_pairs={{0,1},{1,0},{2,3},{3,2},{4,5},{5,4},{6,7},{7,6},{8,9},{9,8},{10,11... | collective-permute-start | bytes 393224 | tf_op jit(solution)/shard_map/ppermute | solution.py:294
  41.7 3.1 %collective-permute-start.13 = (bf16[64,1024]{1,0:T(8,128)(2,1)S(1)}, bf16[64,1024]{1,0:T(8,128)(2,1)S(1)}, u32[]{:S(2)}, u32[]{:S(2)}) collective-permute-start(bf16[64,1024]{1,0:T(8,128)(2,1)S(1)} %collective-permute-done.8.refs_2_), channel_id=1, source_target_pairs={{0,1},{1,0},{2,3},{3,2},{4,5},{5,4},{6,7},{7,6},{8,9},{9,8},{10,11... | collective-permute-start | bytes 393224 | tf_op jit(solution)/shard_map/ppermute | solution.py:294
  43.5 2.3 %collective-permute-start.14 = (bf16[64,1024]{1,0:T(8,128)(2,1)S(1)}, bf16[64,1024]{1,0:T(8,128)(2,1)S(1)}, u32[]{:S(2)}, u32[]{:S(2)}) collective-permute-start(bf16[64,1024]{1,0:T(8,128)(2,1)S(1)} %collective-permute-done.9.refs_3_), channel_id=1, source_target_pairs={{0,1},{1,0},{2,3},{3,2},{4,5},{5,4},{6,7},{7,6},{8,9},{9,8},{10,11... | collective-permute-start | bytes 393224 | tf_op jit(solution)/shard_map/ppermute | solution.py:294
  44.8 1.3 collective-permute-start.15
  46.2 1.0 copy-start.4
  82.6 2.5 %collective-permute-start.16 = (bf16[416,1024]{1,0:T(8,128)(2,1)S(1)}, bf16[416,1024]{1,0:T(8,128)(2,1)S(1)}, u32[]{:S(2)}, u32[]{:S(2)}) collective-permute-start(bf16[416,1024]{1,0:T(8,128)(2,1)S(1)} %get-tuple-element.14), channel_id=1, source_target_pairs={{0,1},{1,0},{2,3},{3,2},{4,5},{5,4},{6,7},{7,6},{8,9},{9,8},{10,11... | collective-permute-start | bytes 2555912 | tf_op jit(solution)/shard_map/ppermute | solution.py:294
  85.4 8.9 %collective-permute-start.20 = (bf16[64,1024]{1,0:T(8,128)(2,1)S(1)}, bf16[64,1024]{1,0:T(8,128)(2,1)S(1)}, u32[]{:S(2)}, u32[]{:S(2)}) collective-permute-start(bf16[64,1024]{1,0:T(8,128)(2,1)S(1)} %get-tuple-element.27), channel_id=1, source_target_pairs={{0,32},{8,40},{16,48},{24,56},{32,64},{40,72},{48,80},{56,88},{64,... | collective-permute-start | bytes 393224 | tf_op jit(solution)/shard_map/ppermute | solution.py:278
  85.5 9.5 %collective-permute-start.19 = (bf16[64,1024]{1,0:T(8,128)(2,1)S(1)}, bf16[64,1024]{1,0:T(8,128)(2,1)S(1)}, u32[]{:S(2)}, u32[]{:S(2)}) collective-permute-start(bf16[64,1024]{1,0:T(8,128)(2,1)S(1)} %get-tuple-element.28), channel_id=1, source_target_pairs={{0,24},{8,32},{16,40},{24,48},{32,56},{40,64},{48,72},{56,80},{64,... | collective-permute-start | bytes 393224 | tf_op jit(solution)/shard_map/ppermute | solution.py:278
  89.3 7.5 %collective-permute-start.18 = (bf16[64,1024]{1,0:T(8,128)(2,1)S(1)}, bf16[64,1024]{1,0:T(8,128)(2,1)S(1)}, u32[]{:S(2)}, u32[]{:S(2)}) collective-permute-start(bf16[64,1024]{1,0:T(8,128)(2,1)S(1)} %get-tuple-element.29), channel_id=1, source_target_pairs={{0,16},{8,24},{16,32},{24,40},{32,48},{40,56},{48,64},{56,72},{64,... | collective-permute-start | bytes 393224 | tf_op jit(solution)/shard_map/ppermute | solution.py:278
  89.3 11.2 %collective-permute-start.17 = (bf16[64,1024]{1,0:T(8,128)(2,1)S(1)}, bf16[64,1024]{1,0:T(8,128)(2,1)S(1)}, u32[]{:S(2)}, u32[]{:S(2)}) collective-permute-start(bf16[64,1024]{1,0:T(8,128)(2,1)S(1)} %get-tuple-element.26), channel_id=1, source_target_pairs={{0,8},{8,16},{16,24},{24,32},{32,40},{40,48},{48,56},{56,64},{64,7... | collective-permute-start | bytes 393224 | tf_op jit(solution)/shard_map/ppermute | solution.py:278
  89.9 10.7 %collective-permute-start.23 = (bf16[96,1024]{1,0:T(8,128)(2,1)S(1)}, bf16[96,1024]{1,0:T(8,128)(2,1)S(1)}, u32[]{:S(2)}, u32[]{:S(2)}) collective-permute-start(bf16[96,1024]{1,0:T(8,128)(2,1)S(1)} %fusion), channel_id=1, source_target_pairs={{0,6},{1,7},{2,0},{3,1},{4,2},{5,3},{6,4},{7,5},{8,14},{9,15},{10,... | collective-permute-start | bytes 589832 | tf_op jit(solution)/shard_map/ppermute | solution.py:290
  94.4 7.4 %collective-permute-start.22 = (bf16[96,1024]{1,0:T(8,128)(2,1)S(1)}, bf16[96,1024]{1,0:T(8,128)(2,1)S(1)}, u32[]{:S(2)}, u32[]{:S(2)}) collective-permute-start(bf16[96,1024]{1,0:T(8,128)(2,1)S(1)} %fusion), channel_id=1, source_target_pairs={{0,2},{1,3},{2,4},{3,5},{4,6},{5,7},{6,0},{7,1},{8,10},{9,11},{10,... | collective-permute-start | bytes 589832 | tf_op jit(solution)/shard_map/ppermute | solution.py:290
  95.0 9.2 %collective-permute-start.21 = (bf16[96,1024]{1,0:T(8,128)(2,1)S(1)}, bf16[96,1024]{1,0:T(8,128)(2,1)S(1)}, u32[]{:S(2)}, u32[]{:S(2)}) collective-permute-start(bf16[96,1024]{1,0:T(8,128)(2,1)S(1)} %fusion), channel_id=1, source_target_pairs={{0,4},{1,5},{2,6},{3,7},{4,0},{5,1},{6,2},{7,3},{8,12},{9,13},{10,... | collective-permute-start | bytes 589832 | tf_op jit(solution)/shard_map/ppermute | solution.py:290
  104.4 4.4 %collective-permute-start.26 = (bf16[64,1024]{1,0:T(8,128)(2,1)S(1)}, bf16[64,1024]{1,0:T(8,128)(2,1)S(1)}, u32[]{:S(2)}, u32[]{:S(2)}) collective-permute-start(bf16[64,1024]{1,0:T(8,128)(2,1)S(1)} %convert_element_type.84), channel_id=1, source_target_pairs={{0,6},{1,7},{2,0},{3,1},{4,2},{5,3},{6,4},{7,5},{8,14},{9,15},{10,... | collective-permute-start | bytes 393224 | tf_op jit(solution)/shard_map/ppermute | solution.py:290
  104.4 5.6 %collective-permute-start.25 = (bf16[64,1024]{1,0:T(8,128)(2,1)S(1)}, bf16[64,1024]{1,0:T(8,128)(2,1)S(1)}, u32[]{:S(2)}, u32[]{:S(2)}) collective-permute-start(bf16[64,1024]{1,0:T(8,128)(2,1)S(1)} %convert_element_type.84), channel_id=1, source_target_pairs={{0,4},{1,5},{2,6},{3,7},{4,0},{5,1},{6,2},{7,3},{8,12},{9,13},{10,... | collective-permute-start | bytes 393224 | tf_op jit(solution)/shard_map/ppermute | solution.py:290
  106.0 5.2 %collective-permute-start.24 = (bf16[64,1024]{1,0:T(8,128)(2,1)S(1)}, bf16[64,1024]{1,0:T(8,128)(2,1)S(1)}, u32[]{:S(2)}, u32[]{:S(2)}) collective-permute-start(bf16[64,1024]{1,0:T(8,128)(2,1)S(1)} %convert_element_type.84), channel_id=1, source_target_pairs={{0,2},{1,3},{2,4},{3,5},{4,6},{5,7},{6,0},{7,1},{8,10},{9,11},{10,... | collective-permute-start | bytes 393224 | tf_op jit(solution)/shard_map/ppermute | solution.py:290
  106.8 4.9 %collective-permute-start.29 = (bf16[96,1024]{1,0:T(8,128)(2,1)S(1)}, bf16[96,1024]{1,0:T(8,128)(2,1)S(1)}, u32[]{:S(2)}, u32[]{:S(2)}) collective-permute-start(bf16[96,1024]{1,0:T(8,128)(2,1)S(1)} %reduce-precision_convert_fusion), channel_id=1, source_target_pairs={{0,24},{8,0},{16,8},{24,16},{32,56},{40,32},{48,40},{56,48},{64,88... | collective-permute-start | bytes 589832 | tf_op jit(solution)/shard_map/ppermute | solution.py:282
  108.7 8.7 %collective-permute-start.28 = (bf16[96,1024]{1,0:T(8,128)(2,1)S(1)}, bf16[96,1024]{1,0:T(8,128)(2,1)S(1)}, u32[]{:S(2)}, u32[]{:S(2)}) collective-permute-start(bf16[96,1024]{1,0:T(8,128)(2,1)S(1)} %reduce-precision_convert_fusion), channel_id=1, source_target_pairs={{0,8},{8,16},{16,24},{24,0},{32,40},{40,48},{48,56},{56,32},{64,72... | collective-permute-start | bytes 589832 | tf_op jit(solution)/shard_map/ppermute | solution.py:282
  108.8 8.7 %collective-permute-start.27 = (bf16[96,1024]{1,0:T(8,128)(2,1)S(1)}, bf16[96,1024]{1,0:T(8,128)(2,1)S(1)}, u32[]{:S(2)}, u32[]{:S(2)}) collective-permute-start(bf16[96,1024]{1,0:T(8,128)(2,1)S(1)} %reduce-precision_convert_fusion), channel_id=1, source_target_pairs={{0,16},{8,24},{16,0},{24,8},{32,48},{40,56},{48,32},{56,40},{64,80... | collective-permute-start | bytes 589832 | tf_op jit(solution)/shard_map/ppermute | solution.py:282
  117.5 9.7 %collective-permute-start.30 = (f32[64,1024]{1,0:T(8,128)S(1)}, f32[64,1024]{1,0:T(8,128)S(1)}, u32[]{:S(2)}, u32[]{:S(2)}) collective-permute-start(f32[64,1024]{1,0:T(8,128)S(1)} %add_add_fusion.3.mine_ref), channel_id=1, source_target_pairs={{0,1},{1,0},{2,3},{3,2},{4,5},{5,4},{6,7},{7,6},{8,9},{9,8},{10,11... | collective-permute-start | bytes 786440 | tf_op jit(solution)/shard_map/ppermute | solution.py:294
  121.7 13.1 %collective-permute-start.31 = (bf16[96,1024]{1,0:T(8,128)(2,1)S(1)}, bf16[96,1024]{1,0:T(8,128)(2,1)S(1)}, u32[]{:S(2)}, u32[]{:S(2)}) collective-permute-start(bf16[96,1024]{1,0:T(8,128)(2,1)S(1)} %get-tuple-element.30), channel_id=1, source_target_pairs={{0,32},{8,40},{16,48},{24,56},{32,64},{40,72},{48,80},{56,88},{64,... | collective-permute-start | bytes 589832 | tf_op jit(solution)/shard_map/ppermute | solution.py:278
  122.7 12.2 %collective-permute-start.32 = (bf16[96,1024]{1,0:T(8,128)(2,1)S(1)}, bf16[96,1024]{1,0:T(8,128)(2,1)S(1)}, u32[]{:S(2)}, u32[]{:S(2)}) collective-permute-start(bf16[96,1024]{1,0:T(8,128)(2,1)S(1)} %get-tuple-element.30), channel_id=1, source_target_pairs={{0,64},{8,72},{16,80},{24,88},{32,96},{40,104},{48,112},{56,120},{... | collective-permute-start | bytes 589832 | tf_op jit(solution)/shard_map/ppermute | solution.py:278
  125.2 9.7 %collective-permute-start.33 = (bf16[96,1024]{1,0:T(8,128)(2,1)S(1)}, bf16[96,1024]{1,0:T(8,128)(2,1)S(1)}, u32[]{:S(2)}, u32[]{:S(2)}) collective-permute-start(bf16[96,1024]{1,0:T(8,128)(2,1)S(1)} %get-tuple-element.30), channel_id=1, source_target_pairs={{0,96},{8,104},{16,112},{24,120},{32,0},{40,8},{48,16},{56,24},{64... | collective-permute-start | bytes 589832 | tf_op jit(solution)/shard_map/ppermute | solution.py:278
  127.2 3.4 %copy-start = (f32[2,16,64,1024]{3,2,1,0:T(8,128)S(1)}, f32[2,16,64,1024]{3,2,1,0:T(8,128)}, u32[]{:S(2)}) copy-start(f32[2,16,64,1024]{3,2,1,0:T(8,128)} %field_ref.5) | copy-start | bytes 25165828
  135.0 2.1 %copy-start.5 = (f32[64,1024]{1,0:T(8,128)}, f32[64,1024]{1,0:T(8,128)S(1)}, u32[]{:S(2)}) copy-start(f32[64,1024]{1,0:T(8,128)S(1)} %slice_divide_fusion.mine_ref) | copy-start | bytes 786436
  135.1 2.1 %collective-permute-start.34 = (f32[64,1024]{1,0:T(8,128)S(1)}, f32[64,1024]{1,0:T(8,128)S(1)}, u32[]{:S(2)}, u32[]{:S(2)}) collective-permute-start(f32[64,1024]{1,0:T(8,128)S(1)} %slice_divide_fusion.mine_ref), channel_id=1, source_target_pairs={{0,1},{1,0},{2,3},{3,2},{4,5},{5,4},{6,7},{7,6},{8,9},{9,8},{10,11... | collective-permute-start | bytes 786440 | tf_op jit(solution)/shard_map/ppermute | solution.py:294
  137.2 0.7 copy-start.6

commit v6 on v5

--- a/solution.py
+++ b/solution.py
@@ -120,7 +120,7 @@
         out_specs=pl.BlockSpec(memory_space=pl.ANY),
         out_shape=jax.ShapeDtypeStruct(field.shape, F32),
         scratch_shapes=[pltpu.VMEM((VIEWS, 2, layers, ROWS, COLUMNS), F32), pltpu.SemaphoreType.DMA((VIEWS,))],
-        compiler_params=pltpu.CompilerParams(vmem_limit_bytes=40 << 20),
+        compiler_params=pltpu.CompilerParams(vmem_limit_bytes=20 << 20),
         cost_estimate=pl.CostEstimate(flops=layers * 8 * 16 * 1024 * 4, bytes_accessed=16 << 20, transcendentals=0),
     )(place, mine, theirs, field)
 
@@ -141,6 +141,7 @@
         in_specs=[SMEM, VMEM, VMEM],
         out_specs=VMEM,
         out_shape=jax.ShapeDtypeStruct((2, FRAME, FRAME), F32),
+        compiler_params=pltpu.CompilerParams(vmem_limit_bytes=8 << 20),
         cost_estimate=pl.CostEstimate(flops=1000, bytes_accessed=1 << 20, transcendentals=0),
     )(place, mine, theirs)
 
@@ -268,7 +269,7 @@
             pltpu.VMEM((2, TILES, BAND, LANES), F32),
             pltpu.VMEM((3, FRAME, FRAME), F32),
         ],
-        compiler_params=pltpu.CompilerParams(vmem_limit_bytes=48 << 20),
+        compiler_params=pltpu.CompilerParams(vmem_limit_bytes=46 << 20),
         cost_estimate=pl.CostEstimate(flops=count * 16 * 2 * FRAME**3, bytes_accessed=16 << 20, transcendentals=0),
     )(place, corners, *bands, probe, fore, back, amplitude)
 
@@ -320,11 +321,12 @@
 
     mine, theirs = visit_all(place, corners, bands, probe, amplitude)
     both = mine.astype(F32) + core_swap(theirs).astype(F32)
+    parts = ring_parts(z_along, both[BLOCKS * SLAB :])
     update = both[:SLAB]
     for k in range(1, BLOCKS):
         term = slab_along(both[k * SLAB : (k + 1) * SLAB].astype(BF16), k).astype(F32)
         update = update + jnp.where(slab >= k, term, 0.0)
-    sums = paired(ring_parts(z_along, both[BLOCKS * SLAB :]))
+    sums = paired(parts)
     update, sums = lax.optimization_barrier((update, sums))
     sent = update.astype(BF16)
     update = update + sum(z_along(sent, d).astype(F32) for d in (1, 2, 3))

time: 140 us -> 140 us (level); the launches traced: 140 us -> 138 us
    unnamed x17 -> x13, local copies, waits for them, and re-layouts: 5.25 us -> 4.53 us
  transfers between devices with their start and end apart: 35 -> 35, of which waited for: 18 -> 19; matrix products, arithmetic and copies ran while one was open for 0% -> 0% of each run, Pallas kernels for 6% -> 6%
where the time goes in v6:
time: 140 us; the launch traced here: 138 us
  Pallas kernels  50 us (36%)
  starting transfers between devices  47.2 us (34%)
  waiting for transfers between devices  32.8 us (23%)
  local copies, waits for them, and re-layouts  5.26 us (4%)
  other arithmetic  2.16 us (2%)
    pallas_call x1, Pallas kernels, visit_all(): pl.pallas_call(visit_kernel, grid=(count // PER_STEP,), in_specs=[SMEM, S...  35.4 us
    ppermute x9, starting transfers between devices, core_swap(): return lax.ppermute(value, 'view', [(i, i ^ 1) for i in range(VIEWS)])  16.2 us
    ppermute x11, starting transfers between devices, slab_along(): lax.ppermute(value, 'slab', [(i, (i + steps) % count) for i in range(coun...  16.1 us
    ppermute x12, waiting for transfers between devices, z_along(): lax.ppermute(value, 'view', [(i, (i + 2 * steps) % VIEWS) for i in range(...  14.8 us
    ppermute x12, starting transfers between devices, z_along(): lax.ppermute(value, 'view', [(i, (i + 2 * steps) % VIEWS) for i in range(...  11.9 us
    pallas_call x2, Pallas kernels, project(): pl.pallas_call(functools.partial(project_kernel, half), in_specs=[SMEM, p...  8.89 us
    ppermute x11, waiting for transfers between devices, slab_along(): lax.ppermute(value, 'slab', [(i, (i + steps) % count) for i in range(coun...  7.64 us
    ppermute x3, waiting for transfers between devices, x_along(): lax.ppermute(value, 'slab', [(i, i // 4 * 4 + (i + steps) % 4) for i in r...  5.58 us
  transfers between devices with their start and end apart: 35, of which 19 were waited for; matrix products, arithmetic and copies ran while one was open for 0% of the time, Pallas kernels for 6%

profile of v6, /device:TPU:1, one launch (start us, length us, event | category | flops | bytes accessed | tf_op | source)
XLA Modules:
  0.0 138.4 jit_solution(6718627100610564201)
XLA Ops:
  0.6 0.7 stack.25.place
  1.3 4.4 %shard_map.78 = f32[4,16,1024]{2,1,0:T(8,128)} custom-call(s32[5]{0:T(128)} %stack.25.place, f32[2,16,64,1024]{3,2,1,0:T(8,128)} %field_ref.5), custom_call_target="tpu_custom_call" | custom-call | flops 6291456 | bytes 12582912 | tf_op jit(solution)/shard_map/pallas_call | solution.py:86
  5.8 1.5 %collective-permute-start = (f32[4,16,1024]{2,1,0:T(8,128)}, f32[4,16,1024]{2,1,0:T(8,128)S(1)}, u32[]{:S(2)}, u32[]{:S(2)}) collective-permute-start(f32[4,16,1024]{2,1,0:T(8,128)} %shard_map.78), channel_id=1, source_target_pairs={{0,1},{1,0},{2,3},{3,2},{4,5},{5,4},{6,7},{7,6},{8,9},{9,8},{10,11... | collective-permute-start | bytes 786440 | tf_op jit(solution)/shard_map/ppermute | solution.py:295
  7.3 4.4 %shard_map.77 = f32[4,16,1024]{2,1,0:T(8,128)} custom-call(s32[5]{0:T(128)} %stack.25.place, f32[2,16,64,1024]{3,2,1,0:T(8,128)} %field_ref.5), custom_call_target="tpu_custom_call" | custom-call | flops 6291456 | bytes 12582912 | tf_op jit(solution)/shard_map/pallas_call | solution.py:86
  11.8 1.1 add.63
  12.9 3.9 %collective-permute-start.3 = (f32[16,1024]{1,0:T(8,128)S(1)}, f32[16,1024]{1,0:T(8,128)S(1)}, u32[]{:S(2)}, u32[]{:S(2)}) collective-permute-start(f32[16,1024]{1,0:T(8,128)S(1)} %get-tuple-element.33), channel_id=1, source_target_pairs={{0,6},{1,7},{2,0},{3,1},{4,2},{5,3},{6,4},{7,5},{8,14},{9,15},{10,... | collective-permute-start | bytes 196616 | tf_op jit(solution)/shard_map/ppermute | solution.py:291
  16.8 1.3 collective-permute-start.2
  18.1 0.2 collective-permute-done.3
  18.3 4.9 %collective-permute-done.1 = f32[16,1024]{1,0:T(8,128)S(1)} collective-permute-done((f32[16,1024]{1,0:T(8,128)S(1)}, f32[16,1024]{1,0:T(8,128)S(1)}, u32[]{:S(2)}, u32[]{:S(2)}) %collective-permute-start.1) | collective-permute-done | bytes 65568 | tf_op jit(solution)/shard_map/ppermute | solution.py:291
  23.2 1.0 collective-permute-start.6
  24.2 0.7 collective-permute-start.4
  24.8 1.2 collective-permute-done.6
  26.0 2.5 %collective-permute-done.5 = bf16[16,1024]{1,0:T(8,128)(2,1)S(1)} collective-permute-done((bf16[16,1024]{1,0:T(8,128)(2,1)S(1)}, bf16[16,1024]{1,0:T(8,128)(2,1)S(1)}, u32[]{:S(2)}, u32[]{:S(2)}) %collective-permute-start.5) | collective-permute-done | bytes 32800 | tf_op jit(solution)/shard_map/ppermute | solution.py:291
  28.5 0.2 collective-permute-done.4
  28.8 5.0 %collective-permute-start.7 = (bf16[64,1024]{1,0:T(8,128)(2,1)S(1)}, bf16[64,1024]{1,0:T(8,128)(2,1)S(1)}, u32[]{:S(2)}, u32[]{:S(2)}) collective-permute-start(bf16[64,1024]{1,0:T(8,128)(2,1)S(1)} %pad_maximum_fusion.refs_0_), channel_id=1, source_target_pairs={{0,120},{8,0},{16,8},{24,16},{32,24},{40,32},{48,40},{56,48},{64,5... | collective-permute-start | bytes 393224 | tf_op jit(solution)/shard_map/ppermute | solution.py:279
  33.8 0.5 collective-permute-start.8
  34.3 0.8 collective-permute-start.9
  35.1 0.2 collective-permute-start.10
  35.2 0.1 copy.9
  35.3 0.1 pad_add_fusion
  35.4 4.0 %collective-permute-start.11 = (bf16[64,1024]{1,0:T(8,128)(2,1)S(1)}, bf16[64,1024]{1,0:T(8,128)(2,1)S(1)}, u32[]{:S(2)}, u32[]{:S(2)}) collective-permute-start(bf16[64,1024]{1,0:T(8,128)(2,1)S(1)} %pad_maximum_fusion.refs_0_), channel_id=1, source_target_pairs={{0,1},{1,0},{2,3},{3,2},{4,5},{5,4},{6,7},{7,6},{8,9},{9,8},{10,11... | collective-permute-start | bytes 393224 | tf_op jit(solution)/shard_map/ppermute | solution.py:295
  39.5 2.3 %collective-permute-start.12 = (bf16[64,1024]{1,0:T(8,128)(2,1)S(1)}, bf16[64,1024]{1,0:T(8,128)(2,1)S(1)}, u32[]{:S(2)}, u32[]{:S(2)}) collective-permute-start(bf16[64,1024]{1,0:T(8,128)(2,1)S(1)} %collective-permute-done.7.refs_1_), channel_id=1, source_target_pairs={{0,1},{1,0},{2,3},{3,2},{4,5},{5,4},{6,7},{7,6},{8,9},{9,8},{10,11... | collective-permute-start | bytes 393224 | tf_op jit(solution)/shard_map/ppermute | solution.py:295
  41.7 1.8 %collective-permute-start.13 = (bf16[64,1024]{1,0:T(8,128)(2,1)S(1)}, bf16[64,1024]{1,0:T(8,128)(2,1)S(1)}, u32[]{:S(2)}, u32[]{:S(2)}) collective-permute-start(bf16[64,1024]{1,0:T(8,128)(2,1)S(1)} %collective-permute-done.8.refs_2_), channel_id=1, source_target_pairs={{0,1},{1,0},{2,3},{3,2},{4,5},{5,4},{6,7},{7,6},{8,9},{9,8},{10,11... | collective-permute-start | bytes 393224 | tf_op jit(solution)/shard_map/ppermute | solution.py:295
  43.5 1.3 collective-permute-start.14
  44.9 0.9 collective-permute-done.14.refs_8_
  45.8 0.4 collective-permute-done.15.refs_9_
  46.2 1.0 copy-done.4
  47.2 35.4 %shard_map.79 = (bf16[416,1024]{1,0:T(8,128)(2,1)S(1)}, bf16[416,1024]{1,0:T(8,128)(2,1)S(1)}) custom-call(s32[5]{0:T(128)S(1)} %copy-done.1, s32[32,2]{1,0:T(8,128)S(1)} %broadcast_subtract_fusion.off_ref, bf16[64,1024]{1,0:T(8,128)(2,1)S(1)} %pad_maximum_fusion.refs_0_, bf16[64,1024]{1,0:T(8,128)(2,1)S(1)} %collective-permute-done.7.refs_1_, ...), custom_call_target="tpu_custom_call" | custom-call | flops 17179869184 | bytes 16777216 | tf_op jit(solution)/shard_map/pallas_call | solution.py:261
  82.6 0.2 collective-permute-start.16
  82.8 2.3 %collective-permute-done.16 = bf16[416,1024]{1,0:T(8,128)(2,1)S(1)} collective-permute-done((bf16[416,1024]{1,0:T(8,128)(2,1)S(1)}, bf16[416,1024]{1,0:T(8,128)(2,1)S(1)}, u32[]{:S(2)}, u32[]{:S(2)}) %collective-permute-start.16) | collective-permute-done | bytes 852000 | tf_op jit(solution)/shard_map/ppermute | solution.py:295
  85.1 0.4 fusion.6
  85.5 0.1 collective-permute-start.20
  85.6 3.9 %collective-permute-start.19 = (bf16[64,1024]{1,0:T(8,128)(2,1)S(1)}, bf16[64,1024]{1,0:T(8,128)(2,1)S(1)}, u32[]{:S(2)}, u32[]{:S(2)}) collective-permute-start(bf16[64,1024]{1,0:T(8,128)(2,1)S(1)} %get-tuple-element.28), channel_id=1, source_target_pairs={{0,24},{8,32},{16,40},{24,48},{32,56},{40,64},{48,72},{56,80},{64,... | collective-permute-start | bytes 393224 | tf_op jit(solution)/shard_map/ppermute | solution.py:279
  89.5 0.6 collective-permute-start.17
  90.1 1.5 %collective-permute-start.23 = (bf16[96,1024]{1,0:T(8,128)(2,1)S(1)}, bf16[96,1024]{1,0:T(8,128)(2,1)S(1)}, u32[]{:S(2)}, u32[]{:S(2)}) collective-permute-start(bf16[96,1024]{1,0:T(8,128)(2,1)S(1)} %fusion), channel_id=1, source_target_pairs={{0,6},{1,7},{2,0},{3,1},{4,2},{5,3},{6,4},{7,5},{8,14},{9,15},{10,... | collective-permute-start | bytes 589832 | tf_op jit(solution)/shard_map/ppermute | solution.py:291
  91.6 3.0 %collective-permute-done.20 = bf16[64,1024]{1,0:T(8,128)(2,1)S(1)} collective-permute-done((bf16[64,1024]{1,0:T(8,128)(2,1)S(1)}, bf16[64,1024]{1,0:T(8,128)(2,1)S(1)}, u32[]{:S(2)}, u32[]{:S(2)}) %collective-permute-start.20) | collective-permute-done | bytes 131104 | tf_op jit(solution)/shard_map/ppermute | solution.py:279
  94.6 0.6 collective-permute-done.19
  95.2 1.5 %collective-permute-start.21 = (bf16[96,1024]{1,0:T(8,128)(2,1)S(1)}, bf16[96,1024]{1,0:T(8,128)(2,1)S(1)}, u32[]{:S(2)}, u32[]{:S(2)}) collective-permute-start(bf16[96,1024]{1,0:T(8,128)(2,1)S(1)} %fusion), channel_id=1, source_target_pairs={{0,4},{1,5},{2,6},{3,7},{4,0},{5,1},{6,2},{7,3},{8,12},{9,13},{10,... | collective-permute-start | bytes 589832 | tf_op jit(solution)/shard_map/ppermute | solution.py:291
  96.6 0.4 collective-permute-done.18
  97.0 3.7 %collective-permute-done.17 = bf16[64,1024]{1,0:T(8,128)(2,1)S(1)} collective-permute-done((bf16[64,1024]{1,0:T(8,128)(2,1)S(1)}, bf16[64,1024]{1,0:T(8,128)(2,1)S(1)}, u32[]{:S(2)}, u32[]{:S(2)}) %collective-permute-start.17) | collective-permute-done | bytes 131104 | tf_op jit(solution)/shard_map/ppermute | solution.py:279
  100.7 0.1 fusion.3
  100.8 1.0 collective-permute-done.22
  101.8 3.1 %collective-permute-done.21 = bf16[96,1024]{1,0:T(8,128)(2,1)S(1)} collective-permute-done((bf16[96,1024]{1,0:T(8,128)(2,1)S(1)}, bf16[96,1024]{1,0:T(8,128)(2,1)S(1)}, u32[]{:S(2)}, u32[]{:S(2)}) %collective-permute-start.21) | collective-permute-done | bytes 196640 | tf_op jit(solution)/shard_map/ppermute | solution.py:291
  104.9 0.1 add_add_fusion.2
  105.0 0.1 collective-permute-start.26
  105.1 1.2 collective-permute-start.25
  106.3 0.8 collective-permute-start.24
  107.1 1.7 %collective-permute-start.29 = (bf16[96,1024]{1,0:T(8,128)(2,1)S(1)}, bf16[96,1024]{1,0:T(8,128)(2,1)S(1)}, u32[]{:S(2)}, u32[]{:S(2)}) collective-permute-start(bf16[96,1024]{1,0:T(8,128)(2,1)S(1)} %reduce-precision_convert_fusion), channel_id=1, source_target_pairs={{0,24},{8,0},{16,8},{24,16},{32,56},{40,32},{48,40},{56,48},{64,88... | collective-permute-start | bytes 589832 | tf_op jit(solution)/shard_map/ppermute | solution.py:283
  108.9 1.2 collective-permute-start.27
  110.2 0.4 collective-permute-done.25
  110.6 1.3 collective-permute-done.24
  112.0 0.1 collective-permute-done.29
  112.0 5.5 %collective-permute-done.28 = bf16[96,1024]{1,0:T(8,128)(2,1)S(1)} collective-permute-done((bf16[96,1024]{1,0:T(8,128)(2,1)S(1)}, bf16[96,1024]{1,0:T(8,128)(2,1)S(1)}, u32[]{:S(2)}, u32[]{:S(2)}) %collective-permute-start.28) | collective-permute-done | bytes 196640 | tf_op jit(solution)/shard_map/ppermute | solution.py:283
  117.5 0.1 add_add_fusion.1
  117.7 4.2 %collective-permute-start.30 = (f32[64,1024]{1,0:T(8,128)S(1)}, f32[64,1024]{1,0:T(8,128)S(1)}, u32[]{:S(2)}, u32[]{:S(2)}) collective-permute-start(f32[64,1024]{1,0:T(8,128)S(1)} %add_add_fusion.3.mine_ref), channel_id=1, source_target_pairs={{0,1},{1,0},{2,3},{3,2},{4,5},{5,4},{6,7},{7,6},{8,9},{9,8},{10,11... | collective-permute-start | bytes 786440 | tf_op jit(solution)/shard_map/ppermute | solution.py:295
  121.9 0.6 collective-permute-start.31
  122.5 2.5 %collective-permute-start.32 = (bf16[96,1024]{1,0:T(8,128)(2,1)S(1)}, bf16[96,1024]{1,0:T(8,128)(2,1)S(1)}, u32[]{:S(2)}, u32[]{:S(2)}) collective-permute-start(bf16[96,1024]{1,0:T(8,128)(2,1)S(1)} %get-tuple-element.30), channel_id=1, source_target_pairs={{0,64},{8,72},{16,80},{24,88},{32,96},{40,104},{48,112},{56,120},{... | collective-permute-start | bytes 589832 | tf_op jit(solution)/shard_map/ppermute | solution.py:279
  125.0 2.0 %collective-permute-start.33 = (bf16[96,1024]{1,0:T(8,128)(2,1)S(1)}, bf16[96,1024]{1,0:T(8,128)(2,1)S(1)}, u32[]{:S(2)}, u32[]{:S(2)}) collective-permute-start(bf16[96,1024]{1,0:T(8,128)(2,1)S(1)} %get-tuple-element.30), channel_id=1, source_target_pairs={{0,96},{8,104},{16,112},{24,120},{32,0},{40,8},{48,16},{56,24},{64... | collective-permute-start | bytes 589832 | tf_op jit(solution)/shard_map/ppermute | solution.py:279
  127.0 3.4 %copy-done = f32[2,16,64,1024]{3,2,1,0:T(8,128)S(1)} copy-done((f32[2,16,64,1024]{3,2,1,0:T(8,128)S(1)}, f32[2,16,64,1024]{3,2,1,0:T(8,128)}, u32[]{:S(2)}) %copy-start) | copy-done | bytes 8388632
  130.4 4.3 %shard_map.80 = f32[2,16,64,1024]{3,2,1,0:T(8,128)} custom-call(s32[5]{0:T(128)S(1)} %copy-done.1, f32[64,1024]{1,0:T(8,128)S(1)} %add_add_fusion.3.mine_ref, f32[64,1024]{1,0:T(8,128)S(1)} %collective-permute-done.30.theirs_ref, f32[2,16,64,1024]{3,2,1,0:T(8,128)S(1)} %copy-done), custom_call_target="tpu_custom_call" | custom-call | flops 8388608 | bytes 16777216 | tf_op jit(solution)/shard_map/pallas_call | solution.py:117
  134.7 0.1 add_add_fusion
  134.9 0.9 collective-permute-start.34
  135.8 1.2 collective-permute-done.34.theirs_ref
  137.0 1.4 %shard_map.81 = f32[2,256,256]{2,1,0:T(8,128)} custom-call(s32[5]{0:T(128)S(1)} %copy-done.1, f32[64,1024]{1,0:T(8,128)S(1)} %slice_divide_fusion.mine_ref, f32[64,1024]{1,0:T(8,128)S(1)} %collective-permute-done.34.theirs_ref), custom_call_target="tpu_custom_call" | custom-call | flops 1000 | bytes 1048576 | tf_op jit(solution)/shard_map/pallas_call | solution.py:139
  (44 shorter events, 0.4 us)
Async XLA Ops:
  5.8 6.0 %collective-permute-start = (f32[4,16,1024]{2,1,0:T(8,128)}, f32[4,16,1024]{2,1,0:T(8,128)S(1)}, u32[]{:S(2)}, u32[]{:S(2)}) collective-permute-start(f32[4,16,1024]{2,1,0:T(8,128)} %shard_map.78), channel_id=1, source_target_pairs={{0,1},{1,0},{2,3},{3,2},{4,5},{5,4},{6,7},{7,6},{8,9},{9,8},{10,11... | collective-permute-start | bytes 786440 | tf_op jit(solution)/shard_map/ppermute | solution.py:295
  11.7 23.5 %copy-start.5 = (s32[32,2]{0,1:T(2,128)S(1)}, s32[32,2]{0,1:T(2,128)}, u32[]{:S(2)}) copy-start(s32[32,2]{0,1:T(2,128)} %param.9) | copy-start | bytes 772
  11.7 34.5 %copy-start.1 = (s32[5]{0:T(128)S(1)}, s32[5]{0:T(128)}, u32[]{:S(2)}) copy-start(s32[5]{0:T(128)} %stack.25.place) | copy-start | bytes 64
  11.7 34.5 %copy-start.2 = (f32[2,256,256]{2,1,0:T(8,128)S(1)}, f32[2,256,256]{2,1,0:T(8,128)}, u32[]{:S(2)}) copy-start(f32[2,256,256]{2,1,0:T(8,128)} %refs_10_.1) | copy-start | bytes 1572868
  11.7 34.4 %copy-start.3 = (bf16[512,512]{1,0:T(8,128)(2,1)S(1)}, bf16[512,512]{1,0:T(8,128)(2,1)}, u32[]{:S(2)}) copy-start(bf16[512,512]{1,0:T(8,128)(2,1)} %constant.31.clone.refs_11_) | copy-start | bytes 1572868
  12.9 5.4 %collective-permute-start.3 = (f32[16,1024]{1,0:T(8,128)S(1)}, f32[16,1024]{1,0:T(8,128)S(1)}, u32[]{:S(2)}, u32[]{:S(2)}) collective-permute-start(f32[16,1024]{1,0:T(8,128)S(1)} %get-tuple-element.33), channel_id=1, source_target_pairs={{0,6},{1,7},{2,0},{3,1},{4,2},{5,3},{6,4},{7,5},{8,14},{9,15},{10,... | collective-permute-start | bytes 196616 | tf_op jit(solution)/shard_map/ppermute | solution.py:291
  16.8 6.4 %collective-permute-start.1 = (f32[16,1024]{1,0:T(8,128)S(1)}, f32[16,1024]{1,0:T(8,128)S(1)}, u32[]{:S(2)}, u32[]{:S(2)}) collective-permute-start(f32[16,1024]{1,0:T(8,128)S(1)} %get-tuple-element.34), channel_id=1, source_target_pairs={{0,2},{1,3},{2,4},{3,5},{4,6},{5,7},{6,0},{7,1},{8,10},{9,11},{10,... | collective-permute-start | bytes 196616 | tf_op jit(solution)/shard_map/ppermute | solution.py:291
  16.8 6.4 %collective-permute-start.2 = (f32[16,1024]{1,0:T(8,128)S(1)}, f32[16,1024]{1,0:T(8,128)S(1)}, u32[]{:S(2)}, u32[]{:S(2)}) collective-permute-start(f32[16,1024]{1,0:T(8,128)S(1)} %get-tuple-element.32), channel_id=1, source_target_pairs={{0,4},{1,5},{2,6},{3,7},{4,0},{5,1},{6,2},{7,3},{8,12},{9,13},{10,... | collective-permute-start | bytes 196616 | tf_op jit(solution)/shard_map/ppermute | solution.py:291
  23.2 2.8 %collective-permute-start.6 = (bf16[16,1024]{1,0:T(8,128)(2,1)S(1)}, bf16[16,1024]{1,0:T(8,128)(2,1)S(1)}, u32[]{:S(2)}, u32[]{:S(2)}) collective-permute-start(bf16[16,1024]{1,0:T(8,128)(2,1)S(1)} %fusion.5), channel_id=1, source_target_pairs={{0,6},{1,7},{2,0},{3,1},{4,2},{5,3},{6,4},{7,5},{8,14},{9,15},{10,... | collective-permute-start | bytes 98312 | tf_op jit(solution)/shard_map/ppermute | solution.py:291
  24.2 4.4 %collective-permute-start.5 = (bf16[16,1024]{1,0:T(8,128)(2,1)S(1)}, bf16[16,1024]{1,0:T(8,128)(2,1)S(1)}, u32[]{:S(2)}, u32[]{:S(2)}) collective-permute-start(bf16[16,1024]{1,0:T(8,128)(2,1)S(1)} %fusion.5), channel_id=1, source_target_pairs={{0,4},{1,5},{2,6},{3,7},{4,0},{5,1},{6,2},{7,3},{8,12},{9,13},{10,... | collective-permute-start | bytes 98312 | tf_op jit(solution)/shard_map/ppermute | solution.py:291
  24.2 4.6 %collective-permute-start.4 = (bf16[16,1024]{1,0:T(8,128)(2,1)S(1)}, bf16[16,1024]{1,0:T(8,128)(2,1)S(1)}, u32[]{:S(2)}, u32[]{:S(2)}) collective-permute-start(bf16[16,1024]{1,0:T(8,128)(2,1)S(1)} %fusion.5), channel_id=1, source_target_pairs={{0,2},{1,3},{2,4},{3,5},{4,6},{5,7},{6,0},{7,1},{8,10},{9,11},{10,... | collective-permute-start | bytes 98312 | tf_op jit(solution)/shard_map/ppermute | solution.py:291
  28.8 10.7 %collective-permute-start.7 = (bf16[64,1024]{1,0:T(8,128)(2,1)S(1)}, bf16[64,1024]{1,0:T(8,128)(2,1)S(1)}, u32[]{:S(2)}, u32[]{:S(2)}) collective-permute-start(bf16[64,1024]{1,0:T(8,128)(2,1)S(1)} %pad_maximum_fusion.refs_0_), channel_id=1, source_target_pairs={{0,120},{8,0},{16,8},{24,16},{32,24},{40,32},{48,40},{56,48},{64,5... | collective-permute-start | bytes 393224 | tf_op jit(solution)/shard_map/ppermute | solution.py:279
  33.8 8.0 %collective-permute-start.8 = (bf16[64,1024]{1,0:T(8,128)(2,1)S(1)}, bf16[64,1024]{1,0:T(8,128)(2,1)S(1)}, u32[]{:S(2)}, u32[]{:S(2)}) collective-permute-start(bf16[64,1024]{1,0:T(8,128)(2,1)S(1)} %pad_maximum_fusion.refs_0_), channel_id=1, source_target_pairs={{0,112},{8,120},{16,0},{24,8},{32,16},{40,24},{48,32},{56,40},{64,... | collective-permute-start | bytes 393224 | tf_op jit(solution)/shard_map/ppermute | solution.py:279
  34.3 9.2 %collective-permute-start.9 = (bf16[64,1024]{1,0:T(8,128)(2,1)S(1)}, bf16[64,1024]{1,0:T(8,128)(2,1)S(1)}, u32[]{:S(2)}, u32[]{:S(2)}) collective-permute-start(bf16[64,1024]{1,0:T(8,128)(2,1)S(1)} %pad_maximum_fusion.refs_0_), channel_id=1, source_target_pairs={{0,104},{8,112},{16,120},{24,0},{32,8},{40,16},{48,24},{56,32},{64... | collective-permute-start | bytes 393224 | tf_op jit(solution)/shard_map/ppermute | solution.py:279
  35.1 9.8 %collective-permute-start.10 = (bf16[64,1024]{1,0:T(8,128)(2,1)S(1)}, bf16[64,1024]{1,0:T(8,128)(2,1)S(1)}, u32[]{:S(2)}, u32[]{:S(2)}) collective-permute-start(bf16[64,1024]{1,0:T(8,128)(2,1)S(1)} %pad_maximum_fusion.refs_0_), channel_id=1, source_target_pairs={{0,96},{8,104},{16,112},{24,120},{32,0},{40,8},{48,16},{56,24},{64... | collective-permute-start | bytes 393224 | tf_op jit(solution)/shard_map/ppermute | solution.py:279
  35.4 9.4 %collective-permute-start.11 = (bf16[64,1024]{1,0:T(8,128)(2,1)S(1)}, bf16[64,1024]{1,0:T(8,128)(2,1)S(1)}, u32[]{:S(2)}, u32[]{:S(2)}) collective-permute-start(bf16[64,1024]{1,0:T(8,128)(2,1)S(1)} %pad_maximum_fusion.refs_0_), channel_id=1, source_target_pairs={{0,1},{1,0},{2,3},{3,2},{4,5},{5,4},{6,7},{7,6},{8,9},{9,8},{10,11... | collective-permute-start | bytes 393224 | tf_op jit(solution)/shard_map/ppermute | solution.py:295
  39.5 5.4 %collective-permute-start.12 = (bf16[64,1024]{1,0:T(8,128)(2,1)S(1)}, bf16[64,1024]{1,0:T(8,128)(2,1)S(1)}, u32[]{:S(2)}, u32[]{:S(2)}) collective-permute-start(bf16[64,1024]{1,0:T(8,128)(2,1)S(1)} %collective-permute-done.7.refs_1_), channel_id=1, source_target_pairs={{0,1},{1,0},{2,3},{3,2},{4,5},{5,4},{6,7},{7,6},{8,9},{9,8},{10,11... | collective-permute-start | bytes 393224 | tf_op jit(solution)/shard_map/ppermute | solution.py:295
  41.7 3.1 %collective-permute-start.13 = (bf16[64,1024]{1,0:T(8,128)(2,1)S(1)}, bf16[64,1024]{1,0:T(8,128)(2,1)S(1)}, u32[]{:S(2)}, u32[]{:S(2)}) collective-permute-start(bf16[64,1024]{1,0:T(8,128)(2,1)S(1)} %collective-permute-done.8.refs_2_), channel_id=1, source_target_pairs={{0,1},{1,0},{2,3},{3,2},{4,5},{5,4},{6,7},{7,6},{8,9},{9,8},{10,11... | collective-permute-start | bytes 393224 | tf_op jit(solution)/shard_map/ppermute | solution.py:295
  43.5 2.3 %collective-permute-start.14 = (bf16[64,1024]{1,0:T(8,128)(2,1)S(1)}, bf16[64,1024]{1,0:T(8,128)(2,1)S(1)}, u32[]{:S(2)}, u32[]{:S(2)}) collective-permute-start(bf16[64,1024]{1,0:T(8,128)(2,1)S(1)} %collective-permute-done.9.refs_3_), channel_id=1, source_target_pairs={{0,1},{1,0},{2,3},{3,2},{4,5},{5,4},{6,7},{7,6},{8,9},{9,8},{10,11... | collective-permute-start | bytes 393224 | tf_op jit(solution)/shard_map/ppermute | solution.py:295
  44.8 1.3 collective-permute-start.15
  46.2 1.0 copy-start.4
  82.6 2.5 %collective-permute-start.16 = (bf16[416,1024]{1,0:T(8,128)(2,1)S(1)}, bf16[416,1024]{1,0:T(8,128)(2,1)S(1)}, u32[]{:S(2)}, u32[]{:S(2)}) collective-permute-start(bf16[416,1024]{1,0:T(8,128)(2,1)S(1)} %get-tuple-element.14), channel_id=1, source_target_pairs={{0,1},{1,0},{2,3},{3,2},{4,5},{5,4},{6,7},{7,6},{8,9},{9,8},{10,11... | collective-permute-start | bytes 2555912 | tf_op jit(solution)/shard_map/ppermute | solution.py:295
  85.5 9.0 %collective-permute-start.20 = (bf16[64,1024]{1,0:T(8,128)(2,1)S(1)}, bf16[64,1024]{1,0:T(8,128)(2,1)S(1)}, u32[]{:S(2)}, u32[]{:S(2)}) collective-permute-start(bf16[64,1024]{1,0:T(8,128)(2,1)S(1)} %get-tuple-element.27), channel_id=1, source_target_pairs={{0,32},{8,40},{16,48},{24,56},{32,64},{40,72},{48,80},{56,88},{64,... | collective-permute-start | bytes 393224 | tf_op jit(solution)/shard_map/ppermute | solution.py:279
  85.6 9.6 %collective-permute-start.19 = (bf16[64,1024]{1,0:T(8,128)(2,1)S(1)}, bf16[64,1024]{1,0:T(8,128)(2,1)S(1)}, u32[]{:S(2)}, u32[]{:S(2)}) collective-permute-start(bf16[64,1024]{1,0:T(8,128)(2,1)S(1)} %get-tuple-element.28), channel_id=1, source_target_pairs={{0,24},{8,32},{16,40},{24,48},{32,56},{40,64},{48,72},{56,80},{64,... | collective-permute-start | bytes 393224 | tf_op jit(solution)/shard_map/ppermute | solution.py:279
  89.5 7.5 %collective-permute-start.18 = (bf16[64,1024]{1,0:T(8,128)(2,1)S(1)}, bf16[64,1024]{1,0:T(8,128)(2,1)S(1)}, u32[]{:S(2)}, u32[]{:S(2)}) collective-permute-start(bf16[64,1024]{1,0:T(8,128)(2,1)S(1)} %get-tuple-element.29), channel_id=1, source_target_pairs={{0,16},{8,24},{16,32},{24,40},{32,48},{40,56},{48,64},{56,72},{64,... | collective-permute-start | bytes 393224 | tf_op jit(solution)/shard_map/ppermute | solution.py:279
  89.5 11.2 %collective-permute-start.17 = (bf16[64,1024]{1,0:T(8,128)(2,1)S(1)}, bf16[64,1024]{1,0:T(8,128)(2,1)S(1)}, u32[]{:S(2)}, u32[]{:S(2)}) collective-permute-start(bf16[64,1024]{1,0:T(8,128)(2,1)S(1)} %get-tuple-element.26), channel_id=1, source_target_pairs={{0,8},{8,16},{16,24},{24,32},{32,40},{40,48},{48,56},{56,64},{64,7... | collective-permute-start | bytes 393224 | tf_op jit(solution)/shard_map/ppermute | solution.py:279
  90.1 10.7 %collective-permute-start.23 = (bf16[96,1024]{1,0:T(8,128)(2,1)S(1)}, bf16[96,1024]{1,0:T(8,128)(2,1)S(1)}, u32[]{:S(2)}, u32[]{:S(2)}) collective-permute-start(bf16[96,1024]{1,0:T(8,128)(2,1)S(1)} %fusion), channel_id=1, source_target_pairs={{0,6},{1,7},{2,0},{3,1},{4,2},{5,3},{6,4},{7,5},{8,14},{9,15},{10,... | collective-permute-start | bytes 589832 | tf_op jit(solution)/shard_map/ppermute | solution.py:291
  94.6 7.3 %collective-permute-start.22 = (bf16[96,1024]{1,0:T(8,128)(2,1)S(1)}, bf16[96,1024]{1,0:T(8,128)(2,1)S(1)}, u32[]{:S(2)}, u32[]{:S(2)}) collective-permute-start(bf16[96,1024]{1,0:T(8,128)(2,1)S(1)} %fusion), channel_id=1, source_target_pairs={{0,2},{1,3},{2,4},{3,5},{4,6},{5,7},{6,0},{7,1},{8,10},{9,11},{10,... | collective-permute-start | bytes 589832 | tf_op jit(solution)/shard_map/ppermute | solution.py:291
  95.2 9.7 %collective-permute-start.21 = (bf16[96,1024]{1,0:T(8,128)(2,1)S(1)}, bf16[96,1024]{1,0:T(8,128)(2,1)S(1)}, u32[]{:S(2)}, u32[]{:S(2)}) collective-permute-start(bf16[96,1024]{1,0:T(8,128)(2,1)S(1)} %fusion), channel_id=1, source_target_pairs={{0,4},{1,5},{2,6},{3,7},{4,0},{5,1},{6,2},{7,3},{8,12},{9,13},{10,... | collective-permute-start | bytes 589832 | tf_op jit(solution)/shard_map/ppermute | solution.py:291
  105.0 3.9 %collective-permute-start.26 = (bf16[64,1024]{1,0:T(8,128)(2,1)S(1)}, bf16[64,1024]{1,0:T(8,128)(2,1)S(1)}, u32[]{:S(2)}, u32[]{:S(2)}) collective-permute-start(bf16[64,1024]{1,0:T(8,128)(2,1)S(1)} %convert_element_type.84), channel_id=1, source_target_pairs={{0,6},{1,7},{2,0},{3,1},{4,2},{5,3},{6,4},{7,5},{8,14},{9,15},{10,... | collective-permute-start | bytes 393224 | tf_op jit(solution)/shard_map/ppermute | solution.py:291
  105.1 5.5 %collective-permute-start.25 = (bf16[64,1024]{1,0:T(8,128)(2,1)S(1)}, bf16[64,1024]{1,0:T(8,128)(2,1)S(1)}, u32[]{:S(2)}, u32[]{:S(2)}) collective-permute-start(bf16[64,1024]{1,0:T(8,128)(2,1)S(1)} %convert_element_type.84), channel_id=1, source_target_pairs={{0,4},{1,5},{2,6},{3,7},{4,0},{5,1},{6,2},{7,3},{8,12},{9,13},{10,... | collective-permute-start | bytes 393224 | tf_op jit(solution)/shard_map/ppermute | solution.py:291
  106.3 5.6 %collective-permute-start.24 = (bf16[64,1024]{1,0:T(8,128)(2,1)S(1)}, bf16[64,1024]{1,0:T(8,128)(2,1)S(1)}, u32[]{:S(2)}, u32[]{:S(2)}) collective-permute-start(bf16[64,1024]{1,0:T(8,128)(2,1)S(1)} %convert_element_type.84), channel_id=1, source_target_pairs={{0,2},{1,3},{2,4},{3,5},{4,6},{5,7},{6,0},{7,1},{8,10},{9,11},{10,... | collective-permute-start | bytes 393224 | tf_op jit(solution)/shard_map/ppermute | solution.py:291
  107.1 4.9 %collective-permute-start.29 = (bf16[96,1024]{1,0:T(8,128)(2,1)S(1)}, bf16[96,1024]{1,0:T(8,128)(2,1)S(1)}, u32[]{:S(2)}, u32[]{:S(2)}) collective-permute-start(bf16[96,1024]{1,0:T(8,128)(2,1)S(1)} %reduce-precision_convert_fusion), channel_id=1, source_target_pairs={{0,24},{8,0},{16,8},{24,16},{32,56},{40,32},{48,40},{56,48},{64,88... | collective-permute-start | bytes 589832 | tf_op jit(solution)/shard_map/ppermute | solution.py:283
  108.9 8.7 %collective-permute-start.28 = (bf16[96,1024]{1,0:T(8,128)(2,1)S(1)}, bf16[96,1024]{1,0:T(8,128)(2,1)S(1)}, u32[]{:S(2)}, u32[]{:S(2)}) collective-permute-start(bf16[96,1024]{1,0:T(8,128)(2,1)S(1)} %reduce-precision_convert_fusion), channel_id=1, source_target_pairs={{0,8},{8,16},{16,24},{24,0},{32,40},{40,48},{48,56},{56,32},{64,72... | collective-permute-start | bytes 589832 | tf_op jit(solution)/shard_map/ppermute | solution.py:283
  108.9 8.6 %collective-permute-start.27 = (bf16[96,1024]{1,0:T(8,128)(2,1)S(1)}, bf16[96,1024]{1,0:T(8,128)(2,1)S(1)}, u32[]{:S(2)}, u32[]{:S(2)}) collective-permute-start(bf16[96,1024]{1,0:T(8,128)(2,1)S(1)} %reduce-precision_convert_fusion), channel_id=1, source_target_pairs={{0,16},{8,24},{16,0},{24,8},{32,48},{40,56},{48,32},{56,40},{64,80... | collective-permute-start | bytes 589832 | tf_op jit(solution)/shard_map/ppermute | solution.py:283
  117.7 9.3 %collective-permute-start.30 = (f32[64,1024]{1,0:T(8,128)S(1)}, f32[64,1024]{1,0:T(8,128)S(1)}, u32[]{:S(2)}, u32[]{:S(2)}) collective-permute-start(f32[64,1024]{1,0:T(8,128)S(1)} %add_add_fusion.3.mine_ref), channel_id=1, source_target_pairs={{0,1},{1,0},{2,3},{3,2},{4,5},{5,4},{6,7},{7,6},{8,9},{9,8},{10,11... | collective-permute-start | bytes 786440 | tf_op jit(solution)/shard_map/ppermute | solution.py:295
  121.9 12.8 %collective-permute-start.31 = (bf16[96,1024]{1,0:T(8,128)(2,1)S(1)}, bf16[96,1024]{1,0:T(8,128)(2,1)S(1)}, u32[]{:S(2)}, u32[]{:S(2)}) collective-permute-start(bf16[96,1024]{1,0:T(8,128)(2,1)S(1)} %get-tuple-element.30), channel_id=1, source_target_pairs={{0,32},{8,40},{16,48},{24,56},{32,64},{40,72},{48,80},{56,88},{64,... | collective-permute-start | bytes 589832 | tf_op jit(solution)/shard_map/ppermute | solution.py:279
  122.5 12.2 %collective-permute-start.32 = (bf16[96,1024]{1,0:T(8,128)(2,1)S(1)}, bf16[96,1024]{1,0:T(8,128)(2,1)S(1)}, u32[]{:S(2)}, u32[]{:S(2)}) collective-permute-start(bf16[96,1024]{1,0:T(8,128)(2,1)S(1)} %get-tuple-element.30), channel_id=1, source_target_pairs={{0,64},{8,72},{16,80},{24,88},{32,96},{40,104},{48,112},{56,120},{... | collective-permute-start | bytes 589832 | tf_op jit(solution)/shard_map/ppermute | solution.py:279
  125.0 9.7 %collective-permute-start.33 = (bf16[96,1024]{1,0:T(8,128)(2,1)S(1)}, bf16[96,1024]{1,0:T(8,128)(2,1)S(1)}, u32[]{:S(2)}, u32[]{:S(2)}) collective-permute-start(bf16[96,1024]{1,0:T(8,128)(2,1)S(1)} %get-tuple-element.30), channel_id=1, source_target_pairs={{0,96},{8,104},{16,112},{24,120},{32,0},{40,8},{48,16},{56,24},{64... | collective-permute-start | bytes 589832 | tf_op jit(solution)/shard_map/ppermute | solution.py:279
  127.0 3.4 %copy-start = (f32[2,16,64,1024]{3,2,1,0:T(8,128)S(1)}, f32[2,16,64,1024]{3,2,1,0:T(8,128)}, u32[]{:S(2)}) copy-start(f32[2,16,64,1024]{3,2,1,0:T(8,128)} %field_ref.5) | copy-start | bytes 25165828
  134.9 2.1 %collective-permute-start.34 = (f32[64,1024]{1,0:T(8,128)S(1)}, f32[64,1024]{1,0:T(8,128)S(1)}, u32[]{:S(2)}, u32[]{:S(2)}) collective-permute-start(f32[64,1024]{1,0:T(8,128)S(1)} %slice_divide_fusion.mine_ref), channel_id=1, source_target_pairs={{0,1},{1,0},{2,3},{3,2},{4,5},{5,4},{6,7},{7,6},{8,9},{9,8},{10,11... | collective-permute-start | bytes 786440 | tf_op jit(solution)/shard_map/ppermute | solution.py:295

commit v7 on v6

--- a/solution.py
+++ b/solution.py
@@ -269,7 +269,7 @@
             pltpu.VMEM((2, TILES, BAND, LANES), F32),
             pltpu.VMEM((3, FRAME, FRAME), F32),
         ],
-        compiler_params=pltpu.CompilerParams(vmem_limit_bytes=46 << 20),
+        compiler_params=pltpu.CompilerParams(vmem_limit_bytes=44 << 20),
         cost_estimate=pl.CostEstimate(flops=count * 16 * 2 * FRAME**3, bytes_accessed=16 << 20, transcendentals=0),
     )(place, corners, *bands, probe, fore, back, amplitude)
 

time: 140 us -> 141 us (level)
  starting transfers between devices: 47.2 us -> 49.7 us
    ppermute x12, waiting for transfers between devices: 14.8 us -> 12 us  [z_along(): lax.ppermute(value, 'view', [(i, (i + 2 * steps) % VIEWS) for i in range(...]
    ppermute x9, starting transfers between devices: 16.2 us -> 19 us  [core_swap(): return lax.ppermute(value, 'view', [(i, i ^ 1) for i in range(VIEWS)])]
    ppermute x11, starting transfers between devices: 16.1 us -> 14.1 us  [slab_along(): lax.ppermute(value, 'slab', [(i, (i + steps) % count) for i in range(coun...]
    ppermute x11, waiting for transfers between devices: 7.64 us -> 9.42 us  [slab_along(): lax.ppermute(value, 'slab', [(i, (i + steps) % count) for i in range(coun...]
    ppermute x3, starting transfers between devices: 2.99 us -> 4.43 us  [x_along(): lax.ppermute(value, 'slab', [(i, i // 4 * 4 + (i + steps) % 4) for i in r...]
  transfers between devices with their start and end apart: 35 -> 35, of which waited for: 19 -> 20; matrix products, arithmetic and copies ran while one was open for 0% -> 0% of each run, Pallas kernels for 6% -> 6%
where the time goes in v7:
time: 141 us; the launch traced here: 140 us
  Pallas kernels  49.9 us (35%)
  starting transfers between devices  49.7 us (35%)
  waiting for transfers between devices  32.3 us (23%)
  local copies, waits for them, and re-layouts  5.26 us (4%)
  other arithmetic  2.16 us (2%)
    pallas_call x1, Pallas kernels, visit_all(): pl.pallas_call(visit_kernel, grid=(count // PER_STEP,), in_specs=[SMEM, S...  35.3 us
    ppermute x9, starting transfers between devices, core_swap(): return lax.ppermute(value, 'view', [(i, i ^ 1) for i in range(VIEWS)])  19 us
    ppermute x11, starting transfers between devices, slab_along(): lax.ppermute(value, 'slab', [(i, (i + steps) % count) for i in range(coun...  14.1 us
    ppermute x12, starting transfers between devices, z_along(): lax.ppermute(value, 'view', [(i, (i + 2 * steps) % VIEWS) for i in range(...  12.2 us
    ppermute x12, waiting for transfers between devices, z_along(): lax.ppermute(value, 'view', [(i, (i + 2 * steps) % VIEWS) for i in range(...  12 us
    ppermute x11, waiting for transfers between devices, slab_along(): lax.ppermute(value, 'slab', [(i, (i + steps) % count) for i in range(coun...  9.42 us
    pallas_call x2, Pallas kernels, project(): pl.pallas_call(functools.partial(project_kernel, half), in_specs=[SMEM, p...  8.89 us
    ppermute x3, waiting for transfers between devices, x_along(): lax.ppermute(value, 'slab', [(i, i // 4 * 4 + (i + steps) % 4) for i in r...  6.22 us
  transfers between devices with their start and end apart: 35, of which 20 were waited for; matrix products, arithmetic and copies ran while one was open for 0% of the time, Pallas kernels for 6%

profile of v7, /device:TPU:1, one launch (start us, length us, event | category | flops | bytes accessed | tf_op | source)
XLA Modules:
  0.0 140.2 jit_solution(13472175640740721464)
XLA Ops:
  0.6 0.7 stack.25.place
  1.3 4.4 %shard_map.78 = f32[4,16,1024]{2,1,0:T(8,128)} custom-call(s32[5]{0:T(128)} %stack.25.place, f32[2,16,64,1024]{3,2,1,0:T(8,128)} %field_ref.5), custom_call_target="tpu_custom_call" | custom-call | flops 6291456 | bytes 12582912 | tf_op jit(solution)/shard_map/pallas_call | solution.py:86
  5.8 1.5 %collective-permute-start = (f32[4,16,1024]{2,1,0:T(8,128)}, f32[4,16,1024]{2,1,0:T(8,128)S(1)}, u32[]{:S(2)}, u32[]{:S(2)}) collective-permute-start(f32[4,16,1024]{2,1,0:T(8,128)} %shard_map.78), channel_id=1, source_target_pairs={{0,1},{1,0},{2,3},{3,2},{4,5},{5,4},{6,7},{7,6},{8,9},{9,8},{10,11... | collective-permute-start | bytes 786440 | tf_op jit(solution)/shard_map/ppermute | solution.py:295
  7.3 4.4 %shard_map.77 = f32[4,16,1024]{2,1,0:T(8,128)} custom-call(s32[5]{0:T(128)} %stack.25.place, f32[2,16,64,1024]{3,2,1,0:T(8,128)} %field_ref.5), custom_call_target="tpu_custom_call" | custom-call | flops 6291456 | bytes 12582912 | tf_op jit(solution)/shard_map/pallas_call | solution.py:86
  11.8 1.1 add.63
  12.9 3.9 %collective-permute-start.3 = (f32[16,1024]{1,0:T(8,128)S(1)}, f32[16,1024]{1,0:T(8,128)S(1)}, u32[]{:S(2)}, u32[]{:S(2)}) collective-permute-start(f32[16,1024]{1,0:T(8,128)S(1)} %get-tuple-element.33), channel_id=1, source_target_pairs={{0,6},{1,7},{2,0},{3,1},{4,2},{5,3},{6,4},{7,5},{8,14},{9,15},{10,... | collective-permute-start | bytes 196616 | tf_op jit(solution)/shard_map/ppermute | solution.py:291
  16.8 1.3 collective-permute-start.2
  18.1 0.2 collective-permute-done.3
  18.3 4.9 %collective-permute-done.1 = f32[16,1024]{1,0:T(8,128)S(1)} collective-permute-done((f32[16,1024]{1,0:T(8,128)S(1)}, f32[16,1024]{1,0:T(8,128)S(1)}, u32[]{:S(2)}, u32[]{:S(2)}) %collective-permute-start.1) | collective-permute-done | bytes 65568 | tf_op jit(solution)/shard_map/ppermute | solution.py:291
  23.2 1.0 collective-permute-start.6
  24.2 0.7 collective-permute-start.4
  24.8 1.2 collective-permute-done.6
  26.0 2.5 %collective-permute-done.5 = bf16[16,1024]{1,0:T(8,128)(2,1)S(1)} collective-permute-done((bf16[16,1024]{1,0:T(8,128)(2,1)S(1)}, bf16[16,1024]{1,0:T(8,128)(2,1)S(1)}, u32[]{:S(2)}, u32[]{:S(2)}) %collective-permute-start.5) | collective-permute-done | bytes 32800 | tf_op jit(solution)/shard_map/ppermute | solution.py:291
  28.5 0.2 collective-permute-done.4
  28.8 5.0 %collective-permute-start.7 = (bf16[64,1024]{1,0:T(8,128)(2,1)S(1)}, bf16[64,1024]{1,0:T(8,128)(2,1)S(1)}, u32[]{:S(2)}, u32[]{:S(2)}) collective-permute-start(bf16[64,1024]{1,0:T(8,128)(2,1)S(1)} %pad_maximum_fusion.refs_0_), channel_id=1, source_target_pairs={{0,120},{8,0},{16,8},{24,16},{32,24},{40,32},{48,40},{56,48},{64,5... | collective-permute-start | bytes 393224 | tf_op jit(solution)/shard_map/ppermute | solution.py:279
  33.8 0.5 collective-permute-start.8
  34.3 0.8 collective-permute-start.9
  35.1 0.2 collective-permute-start.10
  35.2 0.1 copy.9
  35.3 0.1 pad_add_fusion
  35.4 4.0 %collective-permute-start.11 = (bf16[64,1024]{1,0:T(8,128)(2,1)S(1)}, bf16[64,1024]{1,0:T(8,128)(2,1)S(1)}, u32[]{:S(2)}, u32[]{:S(2)}) collective-permute-start(bf16[64,1024]{1,0:T(8,128)(2,1)S(1)} %pad_maximum_fusion.refs_0_), channel_id=1, source_target_pairs={{0,1},{1,0},{2,3},{3,2},{4,5},{5,4},{6,7},{7,6},{8,9},{9,8},{10,11... | collective-permute-start | bytes 393224 | tf_op jit(solution)/shard_map/ppermute | solution.py:295
  39.5 2.3 %collective-permute-start.12 = (bf16[64,1024]{1,0:T(8,128)(2,1)S(1)}, bf16[64,1024]{1,0:T(8,128)(2,1)S(1)}, u32[]{:S(2)}, u32[]{:S(2)}) collective-permute-start(bf16[64,1024]{1,0:T(8,128)(2,1)S(1)} %collective-permute-done.7.refs_1_), channel_id=1, source_target_pairs={{0,1},{1,0},{2,3},{3,2},{4,5},{5,4},{6,7},{7,6},{8,9},{9,8},{10,11... | collective-permute-start | bytes 393224 | tf_op jit(solution)/shard_map/ppermute | solution.py:295
  41.7 1.8 %collective-permute-start.13 = (bf16[64,1024]{1,0:T(8,128)(2,1)S(1)}, bf16[64,1024]{1,0:T(8,128)(2,1)S(1)}, u32[]{:S(2)}, u32[]{:S(2)}) collective-permute-start(bf16[64,1024]{1,0:T(8,128)(2,1)S(1)} %collective-permute-done.8.refs_2_), channel_id=1, source_target_pairs={{0,1},{1,0},{2,3},{3,2},{4,5},{5,4},{6,7},{7,6},{8,9},{9,8},{10,11... | collective-permute-start | bytes 393224 | tf_op jit(solution)/shard_map/ppermute | solution.py:295
  43.5 1.3 collective-permute-start.14
  44.9 0.9 collective-permute-done.14.refs_8_
  45.8 0.4 collective-permute-done.15.refs_9_
  46.2 1.0 copy-done.4
  47.2 35.3 %shard_map.79 = (bf16[416,1024]{1,0:T(8,128)(2,1)S(1)}, bf16[416,1024]{1,0:T(8,128)(2,1)S(1)}) custom-call(s32[5]{0:T(128)S(1)} %copy-done.1, s32[32,2]{1,0:T(8,128)S(1)} %broadcast_subtract_fusion.off_ref, bf16[64,1024]{1,0:T(8,128)(2,1)S(1)} %pad_maximum_fusion.refs_0_, bf16[64,1024]{1,0:T(8,128)(2,1)S(1)} %collective-permute-done.7.refs_1_, ...), custom_call_target="tpu_custom_call" | custom-call | flops 17179869184 | bytes 16777216 | tf_op jit(solution)/shard_map/pallas_call | solution.py:261
  82.6 0.3 collective-permute-start.16
  82.8 2.2 %collective-permute-done.16 = bf16[416,1024]{1,0:T(8,128)(2,1)S(1)} collective-permute-done((bf16[416,1024]{1,0:T(8,128)(2,1)S(1)}, bf16[416,1024]{1,0:T(8,128)(2,1)S(1)}, u32[]{:S(2)}, u32[]{:S(2)}) %collective-permute-start.16) | collective-permute-done | bytes 852000 | tf_op jit(solution)/shard_map/ppermute | solution.py:295
  85.0 0.4 fusion.6
  85.4 0.1 collective-permute-start.20
  85.5 4.0 %collective-permute-start.19 = (bf16[64,1024]{1,0:T(8,128)(2,1)S(1)}, bf16[64,1024]{1,0:T(8,128)(2,1)S(1)}, u32[]{:S(2)}, u32[]{:S(2)}) collective-permute-start(bf16[64,1024]{1,0:T(8,128)(2,1)S(1)} %get-tuple-element.28), channel_id=1, source_target_pairs={{0,24},{8,32},{16,40},{24,48},{32,56},{40,64},{48,72},{56,80},{64,... | collective-permute-start | bytes 393224 | tf_op jit(solution)/shard_map/ppermute | solution.py:279
  89.5 0.6 collective-permute-start.17
  90.1 1.5 %collective-permute-start.23 = (bf16[96,1024]{1,0:T(8,128)(2,1)S(1)}, bf16[96,1024]{1,0:T(8,128)(2,1)S(1)}, u32[]{:S(2)}, u32[]{:S(2)}) collective-permute-start(bf16[96,1024]{1,0:T(8,128)(2,1)S(1)} %fusion), channel_id=1, source_target_pairs={{0,6},{1,7},{2,0},{3,1},{4,2},{5,3},{6,4},{7,5},{8,14},{9,15},{10,... | collective-permute-start | bytes 589832 | tf_op jit(solution)/shard_map/ppermute | solution.py:291
  91.6 2.9 %collective-permute-done.20 = bf16[64,1024]{1,0:T(8,128)(2,1)S(1)} collective-permute-done((bf16[64,1024]{1,0:T(8,128)(2,1)S(1)}, bf16[64,1024]{1,0:T(8,128)(2,1)S(1)}, u32[]{:S(2)}, u32[]{:S(2)}) %collective-permute-start.20) | collective-permute-done | bytes 131104 | tf_op jit(solution)/shard_map/ppermute | solution.py:279
  94.4 0.8 collective-permute-done.19
  95.2 1.4 collective-permute-start.21
  96.6 0.4 collective-permute-done.18
  97.0 3.7 %collective-permute-done.17 = bf16[64,1024]{1,0:T(8,128)(2,1)S(1)} collective-permute-done((bf16[64,1024]{1,0:T(8,128)(2,1)S(1)}, bf16[64,1024]{1,0:T(8,128)(2,1)S(1)}, u32[]{:S(2)}, u32[]{:S(2)}) %collective-permute-start.17) | collective-permute-done | bytes 131104 | tf_op jit(solution)/shard_map/ppermute | solution.py:279
  100.7 0.1 fusion.3
  100.8 2.3 %collective-permute-done.22 = bf16[96,1024]{1,0:T(8,128)(2,1)S(1)} collective-permute-done((bf16[96,1024]{1,0:T(8,128)(2,1)S(1)}, bf16[96,1024]{1,0:T(8,128)(2,1)S(1)}, u32[]{:S(2)}, u32[]{:S(2)}) %collective-permute-start.22) | collective-permute-done | bytes 196640 | tf_op jit(solution)/shard_map/ppermute | solution.py:291
  103.2 0.1 add_add_fusion.2
  103.3 0.1 collective-permute-start.26
  103.4 1.6 %collective-permute-start.25 = (bf16[64,1024]{1,0:T(8,128)(2,1)S(1)}, bf16[64,1024]{1,0:T(8,128)(2,1)S(1)}, u32[]{:S(2)}, u32[]{:S(2)}) collective-permute-start(bf16[64,1024]{1,0:T(8,128)(2,1)S(1)} %convert_element_type.84), channel_id=1, source_target_pairs={{0,4},{1,5},{2,6},{3,7},{4,0},{5,1},{6,2},{7,3},{8,12},{9,13},{10,... | collective-permute-start | bytes 393224 | tf_op jit(solution)/shard_map/ppermute | solution.py:291
  105.0 0.8 collective-permute-start.24
  105.8 3.2 %collective-permute-start.29 = (bf16[96,1024]{1,0:T(8,128)(2,1)S(1)}, bf16[96,1024]{1,0:T(8,128)(2,1)S(1)}, u32[]{:S(2)}, u32[]{:S(2)}) collective-permute-start(bf16[96,1024]{1,0:T(8,128)(2,1)S(1)} %reduce-precision_convert_fusion), channel_id=1, source_target_pairs={{0,24},{8,0},{16,8},{24,16},{32,56},{40,32},{48,40},{56,48},{64,88... | collective-permute-start | bytes 589832 | tf_op jit(solution)/shard_map/ppermute | solution.py:283
  109.0 1.3 collective-permute-start.27
  110.2 0.7 collective-permute-done.24
  110.9 0.6 collective-permute-done.29
  111.6 5.1 %collective-permute-done.28 = bf16[96,1024]{1,0:T(8,128)(2,1)S(1)} collective-permute-done((bf16[96,1024]{1,0:T(8,128)(2,1)S(1)}, bf16[96,1024]{1,0:T(8,128)(2,1)S(1)}, u32[]{:S(2)}, u32[]{:S(2)}) %collective-permute-start.28) | collective-permute-done | bytes 196640 | tf_op jit(solution)/shard_map/ppermute | solution.py:283
  116.7 0.5 collective-permute-done.27
  117.2 0.1 add_add_fusion.1
  117.3 6.6 %collective-permute-start.30 = (f32[64,1024]{1,0:T(8,128)S(1)}, f32[64,1024]{1,0:T(8,128)S(1)}, u32[]{:S(2)}, u32[]{:S(2)}) collective-permute-start(f32[64,1024]{1,0:T(8,128)S(1)} %add_add_fusion.3.mine_ref), channel_id=1, source_target_pairs={{0,1},{1,0},{2,3},{3,2},{4,5},{5,4},{6,7},{7,6},{8,9},{9,8},{10,11... | collective-permute-start | bytes 786440 | tf_op jit(solution)/shard_map/ppermute | solution.py:295
  124.0 0.9 collective-permute-start.32
  125.0 2.0 %collective-permute-start.33 = (bf16[96,1024]{1,0:T(8,128)(2,1)S(1)}, bf16[96,1024]{1,0:T(8,128)(2,1)S(1)}, u32[]{:S(2)}, u32[]{:S(2)}) collective-permute-start(bf16[96,1024]{1,0:T(8,128)(2,1)S(1)} %get-tuple-element.30), channel_id=1, source_target_pairs={{0,96},{8,104},{16,112},{24,120},{32,0},{40,8},{48,16},{56,24},{64... | collective-permute-start | bytes 589832 | tf_op jit(solution)/shard_map/ppermute | solution.py:279
  126.9 3.4 %copy-done = f32[2,16,64,1024]{3,2,1,0:T(8,128)S(1)} copy-done((f32[2,16,64,1024]{3,2,1,0:T(8,128)S(1)}, f32[2,16,64,1024]{3,2,1,0:T(8,128)}, u32[]{:S(2)}) %copy-start) | copy-done | bytes 8388632
  130.3 4.3 %shard_map.80 = f32[2,16,64,1024]{3,2,1,0:T(8,128)} custom-call(s32[5]{0:T(128)S(1)} %copy-done.1, f32[64,1024]{1,0:T(8,128)S(1)} %add_add_fusion.3.mine_ref, f32[64,1024]{1,0:T(8,128)S(1)} %collective-permute-done.30.theirs_ref, f32[2,16,64,1024]{3,2,1,0:T(8,128)S(1)} %copy-done), custom_call_target="tpu_custom_call" | custom-call | flops 8388608 | bytes 16777216 | tf_op jit(solution)/shard_map/pallas_call | solution.py:117
  134.6 1.4 collective-permute-done.31
  136.0 0.3 collective-permute-done.33
  136.3 0.1 add_add_fusion
  136.4 1.2 collective-permute-start.34
  137.6 1.2 collective-permute-done.34.theirs_ref
  138.8 1.4 %shard_map.81 = f32[2,256,256]{2,1,0:T(8,128)} custom-call(s32[5]{0:T(128)S(1)} %copy-done.1, f32[64,1024]{1,0:T(8,128)S(1)} %slice_divide_fusion.mine_ref, f32[64,1024]{1,0:T(8,128)S(1)} %collective-permute-done.34.theirs_ref), custom_call_target="tpu_custom_call" | custom-call | flops 1000 | bytes 1048576 | tf_op jit(solution)/shard_map/pallas_call | solution.py:139
  (44 shorter events, 0.4 us)
Async XLA Ops:
  5.8 6.0 %collective-permute-start = (f32[4,16,1024]{2,1,0:T(8,128)}, f32[4,16,1024]{2,1,0:T(8,128)S(1)}, u32[]{:S(2)}, u32[]{:S(2)}) collective-permute-start(f32[4,16,1024]{2,1,0:T(8,128)} %shard_map.78), channel_id=1, source_target_pairs={{0,1},{1,0},{2,3},{3,2},{4,5},{5,4},{6,7},{7,6},{8,9},{9,8},{10,11... | collective-permute-start | bytes 786440 | tf_op jit(solution)/shard_map/ppermute | solution.py:295
  11.7 23.5 %copy-start.5 = (s32[32,2]{0,1:T(2,128)S(1)}, s32[32,2]{0,1:T(2,128)}, u32[]{:S(2)}) copy-start(s32[32,2]{0,1:T(2,128)} %param.9) | copy-start | bytes 772
  11.7 34.5 %copy-start.1 = (s32[5]{0:T(128)S(1)}, s32[5]{0:T(128)}, u32[]{:S(2)}) copy-start(s32[5]{0:T(128)} %stack.25.place) | copy-start | bytes 64
  11.7 34.5 %copy-start.2 = (f32[2,256,256]{2,1,0:T(8,128)S(1)}, f32[2,256,256]{2,1,0:T(8,128)}, u32[]{:S(2)}) copy-start(f32[2,256,256]{2,1,0:T(8,128)} %refs_10_.1) | copy-start | bytes 1572868
  11.7 34.4 %copy-start.3 = (bf16[512,512]{1,0:T(8,128)(2,1)S(1)}, bf16[512,512]{1,0:T(8,128)(2,1)}, u32[]{:S(2)}) copy-start(bf16[512,512]{1,0:T(8,128)(2,1)} %constant.31.clone.refs_11_) | copy-start | bytes 1572868
  12.9 5.4 %collective-permute-start.3 = (f32[16,1024]{1,0:T(8,128)S(1)}, f32[16,1024]{1,0:T(8,128)S(1)}, u32[]{:S(2)}, u32[]{:S(2)}) collective-permute-start(f32[16,1024]{1,0:T(8,128)S(1)} %get-tuple-element.33), channel_id=1, source_target_pairs={{0,6},{1,7},{2,0},{3,1},{4,2},{5,3},{6,4},{7,5},{8,14},{9,15},{10,... | collective-permute-start | bytes 196616 | tf_op jit(solution)/shard_map/ppermute | solution.py:291
  16.8 6.4 %collective-permute-start.1 = (f32[16,1024]{1,0:T(8,128)S(1)}, f32[16,1024]{1,0:T(8,128)S(1)}, u32[]{:S(2)}, u32[]{:S(2)}) collective-permute-start(f32[16,1024]{1,0:T(8,128)S(1)} %get-tuple-element.34), channel_id=1, source_target_pairs={{0,2},{1,3},{2,4},{3,5},{4,6},{5,7},{6,0},{7,1},{8,10},{9,11},{10,... | collective-permute-start | bytes 196616 | tf_op jit(solution)/shard_map/ppermute | solution.py:291
  16.8 6.4 %collective-permute-start.2 = (f32[16,1024]{1,0:T(8,128)S(1)}, f32[16,1024]{1,0:T(8,128)S(1)}, u32[]{:S(2)}, u32[]{:S(2)}) collective-permute-start(f32[16,1024]{1,0:T(8,128)S(1)} %get-tuple-element.32), channel_id=1, source_target_pairs={{0,4},{1,5},{2,6},{3,7},{4,0},{5,1},{6,2},{7,3},{8,12},{9,13},{10,... | collective-permute-start | bytes 196616 | tf_op jit(solution)/shard_map/ppermute | solution.py:291
  23.2 2.8 %collective-permute-start.6 = (bf16[16,1024]{1,0:T(8,128)(2,1)S(1)}, bf16[16,1024]{1,0:T(8,128)(2,1)S(1)}, u32[]{:S(2)}, u32[]{:S(2)}) collective-permute-start(bf16[16,1024]{1,0:T(8,128)(2,1)S(1)} %fusion.5), channel_id=1, source_target_pairs={{0,6},{1,7},{2,0},{3,1},{4,2},{5,3},{6,4},{7,5},{8,14},{9,15},{10,... | collective-permute-start | bytes 98312 | tf_op jit(solution)/shard_map/ppermute | solution.py:291
  24.2 4.4 %collective-permute-start.5 = (bf16[16,1024]{1,0:T(8,128)(2,1)S(1)}, bf16[16,1024]{1,0:T(8,128)(2,1)S(1)}, u32[]{:S(2)}, u32[]{:S(2)}) collective-permute-start(bf16[16,1024]{1,0:T(8,128)(2,1)S(1)} %fusion.5), channel_id=1, source_target_pairs={{0,4},{1,5},{2,6},{3,7},{4,0},{5,1},{6,2},{7,3},{8,12},{9,13},{10,... | collective-permute-start | bytes 98312 | tf_op jit(solution)/shard_map/ppermute | solution.py:291
  24.2 4.6 %collective-permute-start.4 = (bf16[16,1024]{1,0:T(8,128)(2,1)S(1)}, bf16[16,1024]{1,0:T(8,128)(2,1)S(1)}, u32[]{:S(2)}, u32[]{:S(2)}) collective-permute-start(bf16[16,1024]{1,0:T(8,128)(2,1)S(1)} %fusion.5), channel_id=1, source_target_pairs={{0,2},{1,3},{2,4},{3,5},{4,6},{5,7},{6,0},{7,1},{8,10},{9,11},{10,... | collective-permute-start | bytes 98312 | tf_op jit(solution)/shard_map/ppermute | solution.py:291
  28.8 10.7 %collective-permute-start.7 = (bf16[64,1024]{1,0:T(8,128)(2,1)S(1)}, bf16[64,1024]{1,0:T(8,128)(2,1)S(1)}, u32[]{:S(2)}, u32[]{:S(2)}) collective-permute-start(bf16[64,1024]{1,0:T(8,128)(2,1)S(1)} %pad_maximum_fusion.refs_0_), channel_id=1, source_target_pairs={{0,120},{8,0},{16,8},{24,16},{32,24},{40,32},{48,40},{56,48},{64,5... | collective-permute-start | bytes 393224 | tf_op jit(solution)/shard_map/ppermute | solution.py:279
  33.8 8.0 %collective-permute-start.8 = (bf16[64,1024]{1,0:T(8,128)(2,1)S(1)}, bf16[64,1024]{1,0:T(8,128)(2,1)S(1)}, u32[]{:S(2)}, u32[]{:S(2)}) collective-permute-start(bf16[64,1024]{1,0:T(8,128)(2,1)S(1)} %pad_maximum_fusion.refs_0_), channel_id=1, source_target_pairs={{0,112},{8,120},{16,0},{24,8},{32,16},{40,24},{48,32},{56,40},{64,... | collective-permute-start | bytes 393224 | tf_op jit(solution)/shard_map/ppermute | solution.py:279
  34.3 9.2 %collective-permute-start.9 = (bf16[64,1024]{1,0:T(8,128)(2,1)S(1)}, bf16[64,1024]{1,0:T(8,128)(2,1)S(1)}, u32[]{:S(2)}, u32[]{:S(2)}) collective-permute-start(bf16[64,1024]{1,0:T(8,128)(2,1)S(1)} %pad_maximum_fusion.refs_0_), channel_id=1, source_target_pairs={{0,104},{8,112},{16,120},{24,0},{32,8},{40,16},{48,24},{56,32},{64... | collective-permute-start | bytes 393224 | tf_op jit(solution)/shard_map/ppermute | solution.py:279
  35.1 9.8 %collective-permute-start.10 = (bf16[64,1024]{1,0:T(8,128)(2,1)S(1)}, bf16[64,1024]{1,0:T(8,128)(2,1)S(1)}, u32[]{:S(2)}, u32[]{:S(2)}) collective-permute-start(bf16[64,1024]{1,0:T(8,128)(2,1)S(1)} %pad_maximum_fusion.refs_0_), channel_id=1, source_target_pairs={{0,96},{8,104},{16,112},{24,120},{32,0},{40,8},{48,16},{56,24},{64... | collective-permute-start | bytes 393224 | tf_op jit(solution)/shard_map/ppermute | solution.py:279
  35.4 9.4 %collective-permute-start.11 = (bf16[64,1024]{1,0:T(8,128)(2,1)S(1)}, bf16[64,1024]{1,0:T(8,128)(2,1)S(1)}, u32[]{:S(2)}, u32[]{:S(2)}) collective-permute-start(bf16[64,1024]{1,0:T(8,128)(2,1)S(1)} %pad_maximum_fusion.refs_0_), channel_id=1, source_target_pairs={{0,1},{1,0},{2,3},{3,2},{4,5},{5,4},{6,7},{7,6},{8,9},{9,8},{10,11... | collective-permute-start | bytes 393224 | tf_op jit(solution)/shard_map/ppermute | solution.py:295
  39.5 5.4 %collective-permute-start.12 = (bf16[64,1024]{1,0:T(8,128)(2,1)S(1)}, bf16[64,1024]{1,0:T(8,128)(2,1)S(1)}, u32[]{:S(2)}, u32[]{:S(2)}) collective-permute-start(bf16[64,1024]{1,0:T(8,128)(2,1)S(1)} %collective-permute-done.7.refs_1_), channel_id=1, source_target_pairs={{0,1},{1,0},{2,3},{3,2},{4,5},{5,4},{6,7},{7,6},{8,9},{9,8},{10,11... | collective-permute-start | bytes 393224 | tf_op jit(solution)/shard_map/ppermute | solution.py:295
  41.7 3.1 %collective-permute-start.13 = (bf16[64,1024]{1,0:T(8,128)(2,1)S(1)}, bf16[64,1024]{1,0:T(8,128)(2,1)S(1)}, u32[]{:S(2)}, u32[]{:S(2)}) collective-permute-start(bf16[64,1024]{1,0:T(8,128)(2,1)S(1)} %collective-permute-done.8.refs_2_), channel_id=1, source_target_pairs={{0,1},{1,0},{2,3},{3,2},{4,5},{5,4},{6,7},{7,6},{8,9},{9,8},{10,11... | collective-permute-start | bytes 393224 | tf_op jit(solution)/shard_map/ppermute | solution.py:295
  43.5 2.3 %collective-permute-start.14 = (bf16[64,1024]{1,0:T(8,128)(2,1)S(1)}, bf16[64,1024]{1,0:T(8,128)(2,1)S(1)}, u32[]{:S(2)}, u32[]{:S(2)}) collective-permute-start(bf16[64,1024]{1,0:T(8,128)(2,1)S(1)} %collective-permute-done.9.refs_3_), channel_id=1, source_target_pairs={{0,1},{1,0},{2,3},{3,2},{4,5},{5,4},{6,7},{7,6},{8,9},{9,8},{10,11... | collective-permute-start | bytes 393224 | tf_op jit(solution)/shard_map/ppermute | solution.py:295
  44.8 1.3 collective-permute-start.15
  46.2 1.0 copy-start.4
  82.6 2.5 %collective-permute-start.16 = (bf16[416,1024]{1,0:T(8,128)(2,1)S(1)}, bf16[416,1024]{1,0:T(8,128)(2,1)S(1)}, u32[]{:S(2)}, u32[]{:S(2)}) collective-permute-start(bf16[416,1024]{1,0:T(8,128)(2,1)S(1)} %get-tuple-element.14), channel_id=1, source_target_pairs={{0,1},{1,0},{2,3},{3,2},{4,5},{5,4},{6,7},{7,6},{8,9},{9,8},{10,11... | collective-permute-start | bytes 2555912 | tf_op jit(solution)/shard_map/ppermute | solution.py:295
  85.4 9.0 %collective-permute-start.20 = (bf16[64,1024]{1,0:T(8,128)(2,1)S(1)}, bf16[64,1024]{1,0:T(8,128)(2,1)S(1)}, u32[]{:S(2)}, u32[]{:S(2)}) collective-permute-start(bf16[64,1024]{1,0:T(8,128)(2,1)S(1)} %get-tuple-element.27), channel_id=1, source_target_pairs={{0,32},{8,40},{16,48},{24,56},{32,64},{40,72},{48,80},{56,88},{64,... | collective-permute-start | bytes 393224 | tf_op jit(solution)/shard_map/ppermute | solution.py:279
  85.5 9.7 %collective-permute-start.19 = (bf16[64,1024]{1,0:T(8,128)(2,1)S(1)}, bf16[64,1024]{1,0:T(8,128)(2,1)S(1)}, u32[]{:S(2)}, u32[]{:S(2)}) collective-permute-start(bf16[64,1024]{1,0:T(8,128)(2,1)S(1)} %get-tuple-element.28), channel_id=1, source_target_pairs={{0,24},{8,32},{16,40},{24,48},{32,56},{40,64},{48,72},{56,80},{64,... | collective-permute-start | bytes 393224 | tf_op jit(solution)/shard_map/ppermute | solution.py:279
  89.5 7.5 %collective-permute-start.18 = (bf16[64,1024]{1,0:T(8,128)(2,1)S(1)}, bf16[64,1024]{1,0:T(8,128)(2,1)S(1)}, u32[]{:S(2)}, u32[]{:S(2)}) collective-permute-start(bf16[64,1024]{1,0:T(8,128)(2,1)S(1)} %get-tuple-element.29), channel_id=1, source_target_pairs={{0,16},{8,24},{16,32},{24,40},{32,48},{40,56},{48,64},{56,72},{64,... | collective-permute-start | bytes 393224 | tf_op jit(solution)/shard_map/ppermute | solution.py:279
  89.5 11.2 %collective-permute-start.17 = (bf16[64,1024]{1,0:T(8,128)(2,1)S(1)}, bf16[64,1024]{1,0:T(8,128)(2,1)S(1)}, u32[]{:S(2)}, u32[]{:S(2)}) collective-permute-start(bf16[64,1024]{1,0:T(8,128)(2,1)S(1)} %get-tuple-element.26), channel_id=1, source_target_pairs={{0,8},{8,16},{16,24},{24,32},{32,40},{40,48},{48,56},{56,64},{64,7... | collective-permute-start | bytes 393224 | tf_op jit(solution)/shard_map/ppermute | solution.py:279
  90.1 10.7 %collective-permute-start.23 = (bf16[96,1024]{1,0:T(8,128)(2,1)S(1)}, bf16[96,1024]{1,0:T(8,128)(2,1)S(1)}, u32[]{:S(2)}, u32[]{:S(2)}) collective-permute-start(bf16[96,1024]{1,0:T(8,128)(2,1)S(1)} %fusion), channel_id=1, source_target_pairs={{0,6},{1,7},{2,0},{3,1},{4,2},{5,3},{6,4},{7,5},{8,14},{9,15},{10,... | collective-permute-start | bytes 589832 | tf_op jit(solution)/shard_map/ppermute | solution.py:291
  94.4 8.7 %collective-permute-start.22 = (bf16[96,1024]{1,0:T(8,128)(2,1)S(1)}, bf16[96,1024]{1,0:T(8,128)(2,1)S(1)}, u32[]{:S(2)}, u32[]{:S(2)}) collective-permute-start(bf16[96,1024]{1,0:T(8,128)(2,1)S(1)} %fusion), channel_id=1, source_target_pairs={{0,2},{1,3},{2,4},{3,5},{4,6},{5,7},{6,0},{7,1},{8,10},{9,11},{10,... | collective-permute-start | bytes 589832 | tf_op jit(solution)/shard_map/ppermute | solution.py:291
  95.2 7.9 %collective-permute-start.21 = (bf16[96,1024]{1,0:T(8,128)(2,1)S(1)}, bf16[96,1024]{1,0:T(8,128)(2,1)S(1)}, u32[]{:S(2)}, u32[]{:S(2)}) collective-permute-start(bf16[96,1024]{1,0:T(8,128)(2,1)S(1)} %fusion), channel_id=1, source_target_pairs={{0,4},{1,5},{2,6},{3,7},{4,0},{5,1},{6,2},{7,3},{8,12},{9,13},{10,... | collective-permute-start | bytes 589832 | tf_op jit(solution)/shard_map/ppermute | solution.py:291
  103.3 5.6 %collective-permute-start.26 = (bf16[64,1024]{1,0:T(8,128)(2,1)S(1)}, bf16[64,1024]{1,0:T(8,128)(2,1)S(1)}, u32[]{:S(2)}, u32[]{:S(2)}) collective-permute-start(bf16[64,1024]{1,0:T(8,128)(2,1)S(1)} %convert_element_type.84), channel_id=1, source_target_pairs={{0,6},{1,7},{2,0},{3,1},{4,2},{5,3},{6,4},{7,5},{8,14},{9,15},{10,... | collective-permute-start | bytes 393224 | tf_op jit(solution)/shard_map/ppermute | solution.py:291
  103.4 6.8 %collective-permute-start.25 = (bf16[64,1024]{1,0:T(8,128)(2,1)S(1)}, bf16[64,1024]{1,0:T(8,128)(2,1)S(1)}, u32[]{:S(2)}, u32[]{:S(2)}) collective-permute-start(bf16[64,1024]{1,0:T(8,128)(2,1)S(1)} %convert_element_type.84), channel_id=1, source_target_pairs={{0,4},{1,5},{2,6},{3,7},{4,0},{5,1},{6,2},{7,3},{8,12},{9,13},{10,... | collective-permute-start | bytes 393224 | tf_op jit(solution)/shard_map/ppermute | solution.py:291
  105.0 5.9 %collective-permute-start.24 = (bf16[64,1024]{1,0:T(8,128)(2,1)S(1)}, bf16[64,1024]{1,0:T(8,128)(2,1)S(1)}, u32[]{:S(2)}, u32[]{:S(2)}) collective-permute-start(bf16[64,1024]{1,0:T(8,128)(2,1)S(1)} %convert_element_type.84), channel_id=1, source_target_pairs={{0,2},{1,3},{2,4},{3,5},{4,6},{5,7},{6,0},{7,1},{8,10},{9,11},{10,... | collective-permute-start | bytes 393224 | tf_op jit(solution)/shard_map/ppermute | solution.py:291
  105.8 5.8 %collective-permute-start.29 = (bf16[96,1024]{1,0:T(8,128)(2,1)S(1)}, bf16[96,1024]{1,0:T(8,128)(2,1)S(1)}, u32[]{:S(2)}, u32[]{:S(2)}) collective-permute-start(bf16[96,1024]{1,0:T(8,128)(2,1)S(1)} %reduce-precision_convert_fusion), channel_id=1, source_target_pairs={{0,24},{8,0},{16,8},{24,16},{32,56},{40,32},{48,40},{56,48},{64,88... | collective-permute-start | bytes 589832 | tf_op jit(solution)/shard_map/ppermute | solution.py:283
  108.9 7.7 %collective-permute-start.28 = (bf16[96,1024]{1,0:T(8,128)(2,1)S(1)}, bf16[96,1024]{1,0:T(8,128)(2,1)S(1)}, u32[]{:S(2)}, u32[]{:S(2)}) collective-permute-start(bf16[96,1024]{1,0:T(8,128)(2,1)S(1)} %reduce-precision_convert_fusion), channel_id=1, source_target_pairs={{0,8},{8,16},{16,24},{24,0},{32,40},{40,48},{48,56},{56,32},{64,72... | collective-permute-start | bytes 589832 | tf_op jit(solution)/shard_map/ppermute | solution.py:283
  109.0 8.2 %collective-permute-start.27 = (bf16[96,1024]{1,0:T(8,128)(2,1)S(1)}, bf16[96,1024]{1,0:T(8,128)(2,1)S(1)}, u32[]{:S(2)}, u32[]{:S(2)}) collective-permute-start(bf16[96,1024]{1,0:T(8,128)(2,1)S(1)} %reduce-precision_convert_fusion), channel_id=1, source_target_pairs={{0,16},{8,24},{16,0},{24,8},{32,48},{40,56},{48,32},{56,40},{64,80... | collective-permute-start | bytes 589832 | tf_op jit(solution)/shard_map/ppermute | solution.py:283
  117.3 9.7 %collective-permute-start.30 = (f32[64,1024]{1,0:T(8,128)S(1)}, f32[64,1024]{1,0:T(8,128)S(1)}, u32[]{:S(2)}, u32[]{:S(2)}) collective-permute-start(f32[64,1024]{1,0:T(8,128)S(1)} %add_add_fusion.3.mine_ref), channel_id=1, source_target_pairs={{0,1},{1,0},{2,3},{3,2},{4,5},{5,4},{6,7},{7,6},{8,9},{9,8},{10,11... | collective-permute-start | bytes 786440 | tf_op jit(solution)/shard_map/ppermute | solution.py:295
  124.0 12.0 %collective-permute-start.31 = (bf16[96,1024]{1,0:T(8,128)(2,1)S(1)}, bf16[96,1024]{1,0:T(8,128)(2,1)S(1)}, u32[]{:S(2)}, u32[]{:S(2)}) collective-permute-start(bf16[96,1024]{1,0:T(8,128)(2,1)S(1)} %get-tuple-element.30), channel_id=1, source_target_pairs={{0,32},{8,40},{16,48},{24,56},{32,64},{40,72},{48,80},{56,88},{64,... | collective-permute-start | bytes 589832 | tf_op jit(solution)/shard_map/ppermute | solution.py:279
  124.0 11.9 %collective-permute-start.32 = (bf16[96,1024]{1,0:T(8,128)(2,1)S(1)}, bf16[96,1024]{1,0:T(8,128)(2,1)S(1)}, u32[]{:S(2)}, u32[]{:S(2)}) collective-permute-start(bf16[96,1024]{1,0:T(8,128)(2,1)S(1)} %get-tuple-element.30), channel_id=1, source_target_pairs={{0,64},{8,72},{16,80},{24,88},{32,96},{40,104},{48,112},{56,120},{... | collective-permute-start | bytes 589832 | tf_op jit(solution)/shard_map/ppermute | solution.py:279
  125.0 11.3 %collective-permute-start.33 = (bf16[96,1024]{1,0:T(8,128)(2,1)S(1)}, bf16[96,1024]{1,0:T(8,128)(2,1)S(1)}, u32[]{:S(2)}, u32[]{:S(2)}) collective-permute-start(bf16[96,1024]{1,0:T(8,128)(2,1)S(1)} %get-tuple-element.30), channel_id=1, source_target_pairs={{0,96},{8,104},{16,112},{24,120},{32,0},{40,8},{48,16},{56,24},{64... | collective-permute-start | bytes 589832 | tf_op jit(solution)/shard_map/ppermute | solution.py:279
  126.9 3.4 %copy-start = (f32[2,16,64,1024]{3,2,1,0:T(8,128)S(1)}, f32[2,16,64,1024]{3,2,1,0:T(8,128)}, u32[]{:S(2)}) copy-start(f32[2,16,64,1024]{3,2,1,0:T(8,128)} %field_ref.5) | copy-start | bytes 25165828
  136.4 2.4 %collective-permute-start.34 = (f32[64,1024]{1,0:T(8,128)S(1)}, f32[64,1024]{1,0:T(8,128)S(1)}, u32[]{:S(2)}, u32[]{:S(2)}) collective-permute-start(f32[64,1024]{1,0:T(8,128)S(1)} %slice_divide_fusion.mine_ref), channel_id=1, source_target_pairs={{0,1},{1,0},{2,3},{3,2},{4,5},{5,4},{6,7},{7,6},{8,9},{9,8},{10,11... | collective-permute-start | bytes 786440 | tf_op jit(solution)/shard_map/ppermute | solution.py:295
